TPU v7x, 128 devices: a whole 4x4x4 slice. The times are simulated.
128 devices in a mesh: pts: 16 (over z, y_hi, core), grp: 8 (over x, y_lo).
Axes of the slice: x: 4, y: 4 (y_hi: 2, y_lo: 2; y = y_hi * 2 + y_lo), z: 4, core: 2. Of those that a mesh axis runs over, the one named last changes fastest.
Arguments:
- adjoint_in: bfloat16 [1152, 1280, 256], P(None, ('pts', 'grp')), may hold values from -6 to 6
- land_sea: int32 [1280, 256], P(('pts', 'grp')), may hold values 0 or 1
- depth_class: int32 [1280, 256], P(('pts', 'grp')), may hold values from 0 to 7
- damping: float32 [1280, 256], P(('pts', 'grp')), may hold values from 0.05 to 0.5
- transparency: float32 [1280, 256], P(('pts', 'grp')), may hold values from 0.6 to 1
- outlets: int32 [64], replicated, may hold values from 0 to 327679
- flux_weight: float32 [1152], replicated, may hold values from 0.5 to 2
- jacobian: bfloat16 [1152, 1152], replicated, may hold values from -0.1875 to 0.1875
- source_scale: float32 [8], replicated, may hold values from 0.1 to 0.5
- freq_damp: float32 [1152], replicated, may hold values from 0.2 to 1
- courant: float32 [32], replicated, may hold values from 0.3 to 0.45
- wind_growth: float32 [1152], replicated, may hold values from 0.01 to 0.06
Outputs:
- adjoint_out: bfloat16 [1152, 1280, 256], P(None, ('pts', 'grp'))
- wind_sens: float32 [2, 1280, 256], P(None, ('pts', 'grp'))
All inputs are finite; a program needn't handle non-finite values. No bound on the sum of `land_sea` on one device may be relied on, other than what follows from the above.
Results may differ from a plain program's by a relative error of at most 0.0057.
Values may be sent and summed in bfloat16 or wider, within the bound.
No kernel may reach another device: no remote copies, remote signals or barrier semaphores. Data moves between devices by JAX's collectives and lax.ppermute only.
A program may use at most 128 MiB of HBM per device.

v0:
```python
import math

import jax
import jax.numpy as jnp
from jax import lax
from jax.sharding import PartitionSpec as P

DIR = 36
FREQ = 32
NSUB = 4
NCLASS = 8


def direction_cosines():
    angles = 2.0 * math.pi * (jnp.arange(DIR, dtype=jnp.float32) + 0.5) / DIR
    return (jnp.tile(jnp.cos(angles), FREQ), jnp.tile(jnp.sin(angles), FREQ))


def upwind_weights(courant):
    cosine, sine = direction_cosines()
    speed = jnp.repeat(courant, DIR)
    along_x = speed * cosine
    along_y = speed * sine
    zeros = jnp.zeros_like(along_x)
    return (
        jnp.maximum(along_x, zeros),
        jnp.maximum(-along_x, zeros),
        jnp.maximum(along_y, zeros),
        jnp.maximum(-along_y, zeros),
        1.0 - jnp.abs(along_x) - jnp.abs(along_y),
    )


def propagate(spectrum, weights, passage):
    eastward, westward, northward, southward, centre_keep = tuple(
        (piece[:, None, None] for piece in weights)
    )
    for substep in range(NSUB):
        padded = jnp.pad(spectrum, ((0, 0), (1, 1), (1, 1)))
        spectrum = passage * (
            centre_keep * spectrum
            + eastward * padded[:, 1:-1, 2:]
            + westward * padded[:, 1:-1, :-2]
            + northward * padded[:, 2:, 1:-1]
            + southward * padded[:, :-2, 1:-1]
        )
    return spectrum


def source_adjoint(spectrum, jacobian, source_rate, damp_rows, freq_damp):
    coupled = lax.dot_general(
        jacobian, spectrum, (((0,), (0,)), ((), ())), preferred_element_type=jnp.float32
    )
    values = spectrum.astype(jnp.float32)
    return (
        values + source_rate[None, :] * coupled - damp_rows[None, :] * freq_damp[:, None] * values
    ).astype(jnp.bfloat16)


def body(
    adjoint_in,
    land_sea,
    depth_class,
    damping,
    transparency,
    outlets,
    flux_weight,
    jacobian,
    source_scale,
    freq_damp,
    courant,
    wind_growth,
):
    components, row_count, lon_count = adjoint_in.shape
    devices = lax.axis_size(("pts", "grp"))
    per_device = components // devices
    point_count = row_count * lon_count
    position = lax.axis_index(("pts", "grp"))
    ocean_local = land_sea.astype(jnp.float32)
    passage_local = ocean_local * transparency
    coastline = lax.all_gather(passage_local, ("pts", "grp"), axis=0, tiled=True)
    cosine, sine = direction_cosines()
    forcing = jnp.stack([wind_growth * cosine, wind_growth * sine])
    ocean_rows = ocean_local.reshape(point_count)
    classes = depth_class.reshape(point_count)
    class_ids = jnp.arange(NCLASS, dtype=jnp.int32)[:, None]
    source_rate = jnp.sum(
        jnp.where(classes[None, :] == class_ids, source_scale[:, None], 0.0), axis=0
    )
    damp_rows = damping.reshape(point_count)
    flat_index = position * point_count + jnp.arange(point_count, dtype=jnp.int32)
    seed_count = jnp.sum((flat_index[None, :] == outlets[:, None]).astype(jnp.float32), axis=0)
    incoming = adjoint_in.reshape(components, point_count)
    seeded = (
        ocean_rows[None, :]
        * (incoming.astype(jnp.float32) + flux_weight[:, None] * seed_count[None, :])
    ).astype(jnp.bfloat16)
    mixed = source_adjoint(seeded, jacobian, source_rate, damp_rows, freq_damp)
    wind_first = jnp.dot(
        forcing, seeded, precision=lax.Precision.HIGHEST, preferred_element_type=jnp.float32
    )
    arrived = lax.all_to_all(
        mixed.reshape(components, row_count, lon_count),
        ("pts", "grp"),
        split_axis=0,
        concat_axis=1,
        tiled=True,
    )
    offset = position * per_device
    local_weights = tuple(
        (
            lax.dynamic_slice_in_dim(piece, offset, per_device, 0)
            for piece in upwind_weights(courant)
        )
    )
    propagated = propagate(arrived.astype(jnp.float32), local_weights, coastline).astype(
        jnp.bfloat16
    )
    home = lax.all_to_all(
        propagated, ("pts", "grp"), split_axis=1, concat_axis=0, tiled=True
    ).reshape(components, point_count)
    adjoint_out = source_adjoint(home, jacobian, source_rate, damp_rows, freq_damp).reshape(
        components, row_count, lon_count
    )
    wind_second = jnp.dot(
        forcing, home, precision=lax.Precision.HIGHEST, preferred_element_type=jnp.float32
    )
    wind_sens = (wind_first + wind_second).reshape(2, row_count, lon_count)
    return (adjoint_out, wind_sens)


def solution(mesh):
    placed = (
        P(None, ("pts", "grp"), None),
        P(("pts", "grp"), None),
        P(("pts", "grp"), None),
        P(("pts", "grp"), None),
        P(("pts", "grp"), None),
        P(),
        P(),
        P(),
        P(),
        P(),
        P(),
        P(),
    )
    return jax.shard_map(
        body,
        mesh=mesh,
        in_specs=placed,
        out_specs=(P(None, ("pts", "grp"), None), P(None, ("pts", "grp"), None)),
        check_vma=False,
    )
```

profile of v0, /device:TPU:96, one launch (start us, length us, event | category | flops | bytes accessed | tf_op | source)
XLA Modules:
  0.0 815.9 jit_solution(16402472275892524580)
XLA Ops:
  7.2 0.9 mul.129
  8.1 0.7 eq.31
  8.8 0.7 convert_element_type.47
  9.5 9.9 %copy.44 = f32[1152,10,256]{0,2,1:T(8,128)} copy(bf16[1152,10,256]{2,0,1:T(8,128)(2,1)} %param.12) | data formatting | bytes 17694720 | tf_op jit(solution)/shard_map/convert_element_type | solution.py:96
  19.4 0.2 convert_reduce_fusion
  19.7 5.8 fusion.42
  25.6 10.9 %fusion.44 = bf16[1152,2560]{0,1:T(8,128)(2,1)} fusion(bf16[1152,2560]{0,1:T(8,128)(2,1)S(1)} %fusion.42, bf16[1152,1152]{1,0:T(8,128)(2,1)S(1)} %copy-done, f32[1152]{0:T(1024)S(1)} %copy-done.10, f32[2560]{0:T(1024)S(1)} %mul.129, f32[2560]{0:T(1024)S(1)} %select_reduce_fusion), kind=kOutput, calls=%fused_computation.67 | convolution fusion | flops 6815416320 | bytes 14475776 | tf_op jit(solution)/shard_map/dot_general | solution.py:51
  36.4 12.0 %copy.45 = bf16[1152,10,256]{2,1,0:T(8,128)(2,1)} copy(bf16[1152,10,256]{0,2,1:T(8,128)(2,1)} %bitcast.49) | data formatting | bytes 11796480 | tf_op jit(solution)/shard_map/reshape | solution.py:103
  48.5 10.3 %all-to-all-start = ((bf16[1152,10,256]{2,1,0:T(8,128)(2,1)}), bf16[1152,10,256]{2,1,0:T(8,128)(2,1)}, u32[]{:S(2)}, u32[]{:S(2)}) async-start(bf16[1152,10,256]{2,1,0:T(8,128)(2,1)} %copy.45), calls=%async_computation | async-start | bytes 18874368 | tf_op jit(solution)/shard_map/all_to_all | solution.py:102
  58.7 0.4 all-gather.3.cloned.1.call-start
  59.2 0.6 multiply_bitcast_fusion
  60.2 0.1 reshape.55
  60.4 364.2 %all-gather.3.cloned.1.call-done = f32[128,10,256]{2,1,0:T(8,128)} async-done(((f32[1,10,256]{2,1,0:T(8,128)}), f32[128,10,256]{2,1,0:T(8,128)}) %all-gather.3.cloned.1.call-update) | async-done | bytes 1310736 | tf_op jit(solution)/shard_map/all_gather | solution.py:81
  424.6 2.5 reshape.64
  427.1 9.9 %copy_convert_fusion = f32[1152,10,256]{2,0,1:T(8,128)} fusion(bf16[1152,10,256]{2,1,0:T(8,128)(2,1)} %all-to-all-done), kind=kLoop, calls=%fused_computation.68 | loop fusion | flops 2949120 | bytes 17694720 | tf_op jit(solution)/shard_map/convert_element_type | solution.py:116
  437.0 15.4 %reshape.62 = f32[128,9,10,256]{3,1,0,2:T(8,128)} reshape(f32[1152,10,256]{2,0,1:T(8,128)} %copy_convert_fusion) | data formatting | bytes 23592960 | tf_op jit(solution)/shard_map/convert_element_type | solution.py:116
  452.4 19.6 %copy.47 = f32[9,128,10,256]{3,2,1,0:T(8,128)} copy(f32[9,128,10,256]{3,0,1,2:T(8,128)} %bitcast.43) | data formatting | bytes 23592960 | tf_op jit(solution)/shard_map/convert_element_type | solution.py:116
  472.0 16.4 %reshape.61 = f32[9,1280,256]{2,1,0:T(8,128)} reshape(f32[9,128,10,256]{3,2,1,0:T(8,128)} %copy.47) | data formatting | bytes 23592960 | tf_op jit(solution)/shard_map/convert_element_type | solution.py:116
  488.4 25.7 %fusion.9 = f32[9,1280,256]{2,1,0:T(8,128)} fusion(f32[9,1280,256]{2,1,0:T(8,128)} %reshape.61, f32[9]{0:T(128)S(1)} %get-tuple-element.20, f32[9]{0:T(128)S(1)} %get-tuple-element.19, f32[9]{0:T(128)S(1)} %get-tuple-element.17, f32[9]{0:T(128)S(1)} %get-tuple-element.18, f32[9]{0:T(128)S(1)} %get-tuple-element.16, f32[1280,256]{1,0:T(8,128)} %reshape.64), kind=kLoop, calls=%fused_computation.31 | loop fusion | flops 29491200 | bytes 24903860 | tf_op jit(solution)/shard_map/mul | solution.py:40
  514.1 25.3 %fusion.18 = f32[9,1280,256]{2,1,0:T(8,128)} fusion(f32[9,1280,256]{2,1,0:T(8,128)} %fusion.9, f32[9]{0:T(128)S(1)} %get-tuple-element.20, f32[9]{0:T(128)S(1)} %get-tuple-element.19, f32[9]{0:T(128)S(1)} %get-tuple-element.17, f32[9]{0:T(128)S(1)} %get-tuple-element.18, f32[9]{0:T(128)S(1)} %get-tuple-element.16, f32[1280,256]{1,0:T(8,128)S(1)} %copy-done.1), kind=kLoop, calls=%fused_computation.40 | loop fusion | flops 29491200 | bytes 24903860 | tf_op jit(solution)/shard_map/mul | solution.py:40
  539.4 25.3 %fusion.27 = f32[9,1280,256]{2,1,0:T(8,128)} fusion(f32[9,1280,256]{2,1,0:T(8,128)} %fusion.18, f32[9]{0:T(128)S(1)} %get-tuple-element.20, f32[9]{0:T(128)S(1)} %get-tuple-element.19, f32[9]{0:T(128)S(1)} %get-tuple-element.17, f32[9]{0:T(128)S(1)} %get-tuple-element.18, f32[9]{0:T(128)S(1)} %get-tuple-element.16, f32[1280,256]{1,0:T(8,128)S(1)} %copy-done.1), kind=kLoop, calls=%fused_computation.49 | loop fusion | flops 29491200 | bytes 24903860 | tf_op jit(solution)/shard_map/mul | solution.py:40
  564.7 34.8 %fusion.37 = bf16[9,1280,256]{2,1,0:T(8,128)(2,1)} fusion(f32[9,1280,256]{2,1,0:T(8,128)} %fusion.27, f32[9]{0:T(128)S(1)} %get-tuple-element.20, f32[9]{0:T(128)S(1)} %get-tuple-element.19, f32[9]{0:T(128)S(1)} %get-tuple-element.17, f32[9]{0:T(128)S(1)} %get-tuple-element.18, f32[9]{0:T(128)S(1)} %get-tuple-element.16, f32[1280,256]{1,0:T(8,128)S(1)} %copy-done.1), kind=kLoop, calls=%fused_computation.59 | loop fusion | flops 32440320 | bytes 19005620 | tf_op jit(solution)/shard_map/convert_element_type | solution.py:116
  599.6 9.5 %copy.48 = bf16[9,1280,256]{2,0,1:T(8,128)(2,1)} copy(bf16[9,1280,256]{2,1,0:T(8,128)(2,1)} %fusion.37) | data formatting | bytes 11796480 | tf_op jit(solution)/shard_map/convert_element_type | solution.py:116
  609.1 10.4 %all-to-all-start.1 = ((bf16[9,1280,256]{2,0,1:T(8,128)(2,1)}), bf16[9,1280,256]{2,0,1:T(8,128)(2,1)}, u32[]{:S(2)}, u32[]{:S(2)}) async-start(bf16[9,1280,256]{2,0,1:T(8,128)(2,1)} %copy.48), calls=%async_computation.1 | async-start | bytes 20971520 | tf_op jit(solution)/shard_map/all_to_all | solution.py:119
  619.5 7.3 fusion.45
  626.9 121.5 %all-to-all-done.1 = bf16[9,1280,256]{2,0,1:T(8,128)(2,1)} async-done(((bf16[9,1280,256]{2,0,1:T(8,128)(2,1)}), bf16[9,1280,256]{2,0,1:T(8,128)(2,1)}, u32[]{:S(2)}, u32[]{:S(2)}) %all-to-all-start.1) | async-done | bytes 5898272 | tf_op jit(solution)/shard_map/all_to_all | solution.py:119
  748.3 12.1 %copy.50 = bf16[128,9,10,256]{3,2,1,0:T(8,128)(2,1)} copy(bf16[128,9,10,256]{3,1,2,0:T(8,128)(2,1)} %bitcast.7) | data formatting | bytes 11796480 | tf_op jit(solution)/shard_map/all_to_all | solution.py:119
  760.4 10.2 %copy.56 = bf16[144,8,10,256]{3,1,2,0:T(8,128)(2,1)} copy(bf16[144,8,10,256]{3,2,1,0:T(8,128)(2,1)} %bitcast.47) | data formatting | bytes 11796480
  770.6 8.8 %copy.51 = bf16[1152,2560]{0,1:T(8,128)(2,1)} copy(bf16[1152,2560]{1,0:T(8,128)(2,1)} %bitcast.44) | data formatting | bytes 11796480 | tf_op jit(solution)/shard_map/reshape | solution.py:121
  779.5 5.7 convolution_add_fusion
  785.1 14.8 %fusion.43 = bf16[1152,2560]{0,1:T(8,128)(2,1)} fusion(bf16[1152,2560]{0,1:T(8,128)(2,1)} %copy.51, bf16[1152,2560]{1,0:T(8,128)(2,1)} %bitcast.46, bf16[1152,1152]{1,0:T(8,128)(2,1)S(1)} %copy-done, f32[1152]{0:T(1024)S(1)} %copy-done.10, f32[2560]{0:T(1024)S(1)} %mul.129, f32[2560]{0:T(1024)S(1)} %select_reduce_fusion), kind=kOutput, calls=%fused_computation.66 | convolution fusion | flops 6815416320 | bytes 20374016 | tf_op jit(solution)/shard_map/dot_general | solution.py:51
  800.0 8.9 %copy.52 = bf16[1152,10,256]{2,0,1:T(8,128)(2,1)} copy(bf16[1152,10,256]{0,2,1:T(8,128)(2,1)} %bitcast.48) | data formatting | bytes 11796480
  (38 shorter events, 0.7 us)
Async XLA Ops:
  7.2 18.4 %copy-start = (bf16[1152,1152]{1,0:T(8,128)(2,1)S(1)}, bf16[1152,1152]{1,0:T(8,128)(2,1)}, u32[]{:S(2)}) copy-start(bf16[1152,1152]{1,0:T(8,128)(2,1)} %param.19) | copy-start | bytes 7962628
  7.2 12.3 %copy-start.7 = (s32[64]{0:T(128)S(1)}, s32[64]{0:T(128)}, u32[]{:S(2)}) copy-start(s32[64]{0:T(128)} %param.17) | copy-start | bytes 772
  7.2 12.4 %copy-start.8 = (f32[8]{0:T(128)S(1)}, f32[8]{0:T(128)}, u32[]{:S(2)}) copy-start(f32[8]{0:T(128)} %param.20) | copy-start | bytes 100
  7.2 12.5 %copy-start.5 = (f32[1152]{0:T(1024)S(1)}, f32[1152]{0:T(1024)}, u32[]{:S(2)}) copy-start(f32[1152]{0:T(1024)} %param.18) | copy-start | bytes 13828
  19.4 6.1 copy-start.10
  25.6 10.9 %copy-start.2 = (bf16[1152,2560]{0,1:T(8,128)(2,1)}, bf16[1152,2560]{0,1:T(8,128)(2,1)S(1)}, u32[]{:S(2)}) copy-start(bf16[1152,2560]{0,1:T(8,128)(2,1)S(1)} %fusion.42) | copy-start | bytes 17694724
  48.5 10.7 %copy-start.3 = (s32[10,256]{1,0:T(8,128)S(1)}, s32[10,256]{1,0:T(8,128)}, u32[]{:S(2)}) copy-start(s32[10,256]{1,0:T(8,128)} %param.13) | copy-start | bytes 30724
  48.5 10.7 %copy-start.4 = (f32[10,256]{1,0:T(8,128)S(1)}, f32[10,256]{1,0:T(8,128)}, u32[]{:S(2)}) copy-start(f32[10,256]{1,0:T(8,128)} %param.16) | copy-start | bytes 30724
  48.5 11.7 %copy-start.9 = (f32[32]{0:T(128)S(1)}, f32[32]{0:T(128)}, u32[]{:S(2)}) copy-start(f32[32]{0:T(128)} %param.22) | copy-start | bytes 388
  48.5 11.9 %copy-start.6 = (f32[1152]{0:T(1024)S(1)}, f32[1152]{0:T(1024)}, u32[]{:S(2)}) copy-start(f32[1152]{0:T(1024)} %param.23) | copy-start | bytes 13828
  48.5 378.6 %all-to-all-start = ((bf16[1152,10,256]{2,1,0:T(8,128)(2,1)}), bf16[1152,10,256]{2,1,0:T(8,128)(2,1)}, u32[]{:S(2)}, u32[]{:S(2)}) async-start(bf16[1152,10,256]{2,1,0:T(8,128)(2,1)} %copy.45), calls=%async_computation | async-start | bytes 18874368 | tf_op jit(solution)/shard_map/all_to_all | solution.py:102
  58.7 365.9 %all-gather.3.cloned.1.call-start = ((), (), s32[]{:S(2)}) async-start(), calls=%async_computation.2 | async-start | bytes 2113536 | tf_op jit(solution)/shard_map/all_gather | solution.py:81
  488.4 25.7 %copy-start.1 = (f32[1280,256]{1,0:T(8,128)S(1)}, f32[1280,256]{1,0:T(8,128)}, u32[]{:S(2)}) copy-start(f32[1280,256]{1,0:T(8,128)} %reshape.64) | copy-start | bytes 3932164
  609.1 139.2 %all-to-all-start.1 = ((bf16[9,1280,256]{2,0,1:T(8,128)(2,1)}), bf16[9,1280,256]{2,0,1:T(8,128)(2,1)}, u32[]{:S(2)}, u32[]{:S(2)}) async-start(bf16[9,1280,256]{2,0,1:T(8,128)(2,1)} %copy.48), calls=%async_computation.1 | async-start | bytes 20971520 | tf_op jit(solution)/shard_map/all_to_all | solution.py:119
Sparse Core Ops, SparseCore 0:
  61.8 362.7 all-gather.2
where the time goes:
time: 828 us; the launch traced here: 816 us
  waiting for transfers between devices  486 us (59%)
  other arithmetic  129 us (16%)
  local copies, waits for them, and re-layouts  127 us (15%)
  matrix products  38.7 us (5%)
  starting transfers between devices  21.1 us (3%)
  between operations  14.5 us (2%)
    all_gather x1, waiting for transfers between devices, body(): lax.all_gather(passage_local, ('pts', 'grp'), axis=0, tiled=True)  364 us
    all_to_all x1, waiting for transfers between devices, body(): lax.all_to_all(propagated, ('pts', 'grp'), split_axis=1, concat_axis=0, t...  121 us
    mul x3, other arithmetic, propagate(): passage * (centre_keep * spectrum + eastward * padded[:, 1:-1, 2:] + west...  76.3 us
    convert_element_type x3, local copies, waits for them, and re-layouts, body(): arrived.astype(jnp.float32)  51.4 us
    convert_element_type x1, other arithmetic, body(): propagate(arrived.astype(jnp.float32), local_weights, coastline)  34.8 us
    dot_general x2, matrix products, source_adjoint(): lax.dot_general(jacobian, spectrum, (((0,), (0,)), ((), ())), preferred_e...  25.7 us
    unnamed x25, local copies, waits for them, and re-layouts  21.6 us
  transfers between devices with their start and end apart: 3, of which 2 were waited for; matrix products, arithmetic and copies ran while one was open for 1% of the time, Pallas kernels for 0%

commit v1 on v0

v1 whole, which is shorter than its diff:
```python
import math

import jax
import jax.numpy as jnp
import numpy as np
from jax import lax
from jax.experimental import pallas as pl
from jax.experimental.pallas import tpu as pltpu
from jax.sharding import PartitionSpec as P

DIR = 36
FREQ = 32
NSUB = 4
NCLASS = 8
LON = 256
K = DIR * FREQ
HALF = K // 2
QUAD = K // 4
ROWS = 10
HALO = NSUB
TAIL = 16
AXES = ("pts", "grp")
VMEM = 56 * 1024 * 1024

ANGLES = 2.0 * math.pi * (np.arange(DIR) + 0.5) / DIR


def params():
    return pltpu.CompilerParams(vmem_limit_bytes=VMEM)


def whole(shape):
    return pl.BlockSpec(shape, lambda *_: (0,) * len(shape))


def three_pieces(x):
    hi = x.astype(jnp.bfloat16)
    rest = x - hi.astype(jnp.float32)
    mid = rest.astype(jnp.bfloat16)
    return hi, mid, (rest - mid.astype(jnp.float32)).astype(jnp.bfloat16)


def one_hot_order(chunk, size):
    row = lax.broadcasted_iota(jnp.int32, (size, K), 0) + chunk * size
    source = (row & (FREQ - 1)) * DIR + (row >> 5)
    column = lax.broadcasted_iota(jnp.int32, (size, K), 1)
    return jnp.where(column == source, 1.0, 0.0).astype(jnp.bfloat16)


def turn_kernel(jac_ref, out_ref):
    pick = one_hot_order(pl.program_id(0), 128)
    out_ref[...] = lax.dot_general(
        pick, jac_ref[...], (((1,), (1,)), ((), ())), preferred_element_type=jnp.float32
    ).astype(jnp.bfloat16)


def turn(jacobian):
    return pl.pallas_call(
        turn_kernel,
        grid=(K // 128,),
        in_specs=[whole((K, K))],
        out_specs=pl.BlockSpec((128, K), lambda m: (m, 0)),
        out_shape=jax.ShapeDtypeStruct((K, K), jnp.bfloat16),
        compiler_params=params(),
        cost_estimate=pl.CostEstimate(flops=2 * K**3, bytes_accessed=4 * K * K, transcendentals=0),
    )(jacobian)


def sort_columns_kernel(mat_ref, out_ref):
    pick = one_hot_order(pl.program_id(0), 128)
    out_ref[...] = lax.dot_general(
        mat_ref[...], pick, (((1,), (1,)), ((), ())), preferred_element_type=jnp.float32
    ).astype(jnp.bfloat16)


def sort_columns(mat):
    return pl.pallas_call(
        sort_columns_kernel,
        grid=(K // 128,),
        in_specs=[whole((K, K))],
        out_specs=pl.BlockSpec((K, 128), lambda m: (0, m)),
        out_shape=jax.ShapeDtypeStruct((K, K), jnp.bfloat16),
        compiler_params=params(),
        cost_estimate=pl.CostEstimate(flops=2 * K**3, bytes_accessed=4 * K * K, transcendentals=0),
    )(mat)


def wind_rows(forcing, values):
    parts = jnp.concatenate([*three_pieces(forcing), jnp.zeros((8, K), jnp.bfloat16)], axis=0)
    sums = jnp.dot(parts, values, preferred_element_type=jnp.float32)
    return sums[0:8] + sums[8:16] + sums[16:24]


def first_kernel(half, first_row, halo, x_ref, sea_ref, count_ref, rate_ref, damp_ref, pass_ref,
                 fw_ref, fd_ref, jac_ref, forcing_ref, *rest):
    if halo:
        out_a, out_b, held = rest
    else:
        out_a, wind_ref, held = rest
    r = pl.program_id(0) + first_row
    sea = sea_ref[pl.ds(r, 1), :]
    count = count_ref[pl.ds(r, 1), :]
    rate = rate_ref[pl.ds(r, 1), :]
    damp = damp_ref[pl.ds(r, 1), :]
    fw = jnp.concatenate([fw_ref[...], fw_ref[...]], axis=1)
    seeded = (sea * (x_ref[0].astype(jnp.float32) + fw * count)).astype(jnp.bfloat16)
    values = seeded.astype(jnp.float32)
    held[0] = values[:, :128]
    held[1] = values[:, 128:]
    for m in range(HALF // 64):
        rows = slice(m * 64, (m + 1) * 64)
        mixed = jnp.dot(jac_ref[rows, :], seeded, preferred_element_type=jnp.float32)
        fd = fd_ref[rows, :]
        for side in range(2):
            lanes = slice(side * 128, (side + 1) * 128)
            d = half * 18 + 2 * m
            v = jnp.concatenate(
                [held[side, pl.ds(d + e, FREQ, stride=DIR), :] for e in range(2)], axis=0
            )
            moved = v + rate[:, lanes] * mixed[:, lanes] - (damp[:, lanes] * fd) * v
            moved = moved.astype(jnp.bfloat16)
            if not halo:
                out_a[0, rows, lanes] = moved
            elif m * 64 + 64 <= QUAD:
                out_a[0, rows, lanes] = moved
            elif m * 64 >= QUAD:
                out_b[0, m * 64 - QUAD : m * 64 - QUAD + 64, lanes] = moved
            else:
                out_a[0, m * 64 : m * 64 + 32, lanes] = moved[:32]
                out_b[0, 0:32, lanes] = moved[32:]
    if halo:
        pieces = [jnp.broadcast_to(p, (8, LON)).astype(jnp.float32)
                  for p in three_pieces(pass_ref[pl.ds(r, 1), :])]
        which = lax.broadcasted_iota(jnp.int32, (8, LON), 0)
        tail = jnp.where(which == 0, pieces[0], jnp.where(which == 1, pieces[1], jnp.where(which == 2, pieces[2], 0.0)))
        out_a[0, QUAD : QUAD + TAIL, :] = jnp.concatenate([tail, jnp.zeros((8, LON), jnp.float32)], axis=0).astype(jnp.bfloat16)
    else:
        wind_ref[0] = wind_rows(forcing_ref[...], seeded)


def first_source(half, first_row, count_rows, halo, x, sea, count, rate, damp, passage, fw, fd, jac, forcing):
    point = whole((ROWS, LON))
    if halo:
        shapes = [(count_rows, QUAD + TAIL, LON), (count_rows, QUAD, LON)]
        out_shape = [jax.ShapeDtypeStruct(s, jnp.bfloat16) for s in shapes]
    else:
        shapes = [(count_rows, HALF, LON), (count_rows, 8, LON)]
        out_shape = [jax.ShapeDtypeStruct(shapes[0], jnp.bfloat16), jax.ShapeDtypeStruct(shapes[1], jnp.float32)]

    def body(*refs):
        first_kernel(half, first_row, halo, *refs)

    return pl.pallas_call(
        body,
        grid=(count_rows,),
        in_specs=[
            pl.BlockSpec((1, K, LON), lambda i: (i + first_row, 0, 0)),
            point, point, point, point, point,
            whole((K, 128)),
            pl.BlockSpec((HALF, 128), lambda i: (half, 0)),
            pl.BlockSpec((HALF, K), lambda i: (half, 0)),
            whole((8, K)),
        ],
        out_specs=[pl.BlockSpec((1, *s[1:]), lambda i: (i, 0, 0)) for s in shapes],
        out_shape=out_shape,
        scratch_shapes=[pltpu.VMEM((2, K, 128), jnp.float32)],
        compiler_params=params(),
        cost_estimate=pl.CostEstimate(
            flops=2 * K * HALF * LON * count_rows, bytes_accessed=4 * K * LON * count_rows, transcendentals=0
        ),
    )(x, sea, count, rate, damp, passage, fw, fd, jac, forcing)


def sweep_kernel(quad, table_ref, own_pass_ref, halo_pass_ref, courant_ref, edge_ref, inner_ref, halo_ref,
                 out_ref, pass_rows):
    north = quad < 2
    east = quad in (0, 3)
    d = pl.program_id(0)

    @pl.when(d == 0)
    def _():
        for t in range(ROWS + HALO - 1):
            if t < ROWS:
                own = t if north else ROWS - 1 - t
                row = own_pass_ref[own : own + 1, :]
            else:
                far = t - ROWS if north else HALO - 1 - (t - ROWS)
                pieces = halo_pass_ref[far].astype(jnp.float32)
                row = pieces[0:1] + pieces[1:2] + pieces[2:3]
            pass_rows[t] = jnp.broadcast_to(row, (8, LON))

    along_x = table_ref[0, d]
    along_y = table_ref[1, d]
    lane = lax.broadcasted_iota(jnp.int32, (8, LON), 1)
    inside = lane < LON - 1 if east else lane > 0
    for group in range(2):
        rows = slice(group * 16, (group + 1) * 16)
        blocks = []
        for t in range(ROWS + HALO):
            if north:
                ref, at = (edge_ref, t) if t < 4 else (inner_ref, t - 4) if t < 10 else (halo_ref, t - 10)
            else:
                ref, at = (edge_ref, 3 - t) if t < 4 else (inner_ref, 9 - t) if t < 10 else (halo_ref, 13 - t)
            blocks.append(ref[at, rows, :].astype(jnp.float32))
        done = []
        for part in range(2):
            speed = courant_ref[group * 16 + part * 8 : group * 16 + part * 8 + 8, :]
            speed = jnp.concatenate([speed, speed], axis=1)
            across = speed * along_x
            upward = speed * along_y
            centre = 1.0 - across - upward
            across = jnp.where(inside, across, 0.0)
            v = [b[part * 8 : part * 8 + 8] for b in blocks]
            for step in range(NSUB):
                v = [
                    pass_rows[t]
                    * (centre * v[t] + across * pltpu.roll(v[t], LON - 1 if east else 1, 1) + upward * v[t + 1])
                    for t in range(len(v) - 1)
                ]
            done.append(v)
        for t in range(ROWS):
            out_ref[t if north else ROWS - 1 - t, rows, :] = jnp.concatenate(
                [done[0][t], done[1][t]], axis=0
            ).astype(jnp.bfloat16)


def sweep(quad, table, passage, carrier, courant, edge, inner, halo):
    def body(*refs):
        sweep_kernel(quad, *refs)

    inner_at = (quad % 2) * (QUAD // FREQ)
    return pl.pallas_call(
        body,
        grid=(QUAD // FREQ,),
        in_specs=[
            pl.BlockSpec(memory_space=pltpu.SMEM),
            whole((ROWS, LON)),
            pl.BlockSpec((HALO, TAIL, LON), lambda d: (0, QUAD // TAIL, 0)),
            whole((FREQ, 128)),
            pl.BlockSpec((HALO, FREQ, LON), lambda d: (0, d, 0)),
            pl.BlockSpec((ROWS - HALO, FREQ, LON), lambda d: (0, d + inner_at, 0)),
            pl.BlockSpec((HALO, FREQ, LON), lambda d: (0, d, 0)),
        ],
        out_specs=pl.BlockSpec((ROWS, FREQ, LON), lambda d: (0, d, 0)),
        out_shape=jax.ShapeDtypeStruct((ROWS, QUAD, LON), jnp.bfloat16),
        scratch_shapes=[pltpu.VMEM((ROWS + HALO - 1, 8, LON), jnp.float32)],
        compiler_params=params(),
        cost_estimate=pl.CostEstimate(
            flops=46 * 7 * QUAD * LON, bytes_accessed=48 * QUAD * LON, transcendentals=0
        ),
    )(table, passage, carrier, courant, edge, inner, halo)


def second_kernel(v0, v1, v2, v3, rate_ref, damp_ref, fd_ref, jac_ref, forcing_ref, wind_in, out_ref, wind_ref,
                  joined, held):
    r = pl.program_id(0)
    rate = rate_ref[pl.ds(r, 1), :]
    damp = damp_ref[pl.ds(r, 1), :]
    for q, v_ref in enumerate((v0, v1, v2, v3)):
        joined[q * QUAD : (q + 1) * QUAD, :] = v_ref[0]
    spectrum = joined[...]
    for m in range(K // 64):
        rows = slice(m * 64, (m + 1) * 64)
        mixed = jnp.dot(jac_ref[rows, :], spectrum, preferred_element_type=jnp.float32)
        fd = fd_ref[rows, :]
        for side in range(2):
            lanes = slice(side * 128, (side + 1) * 128)
            v = joined[rows, lanes].astype(jnp.float32)
            moved = v + rate[:, lanes] * mixed[:, lanes] - (damp[:, lanes] * fd) * v
            for e in range(2):
                held[side, pl.ds(2 * m + e, FREQ, stride=DIR), :] = moved[e * FREQ : (e + 1) * FREQ]
    for side in range(2):
        out_ref[0, :, side * 128 : (side + 1) * 128] = held[side].astype(jnp.bfloat16)
    wind_ref[0] = wind_in[0] + wind_rows(forcing_ref[...], spectrum)


def second_source(swept, rate, damp, fd, jac, forcing, wind):
    point = whole((ROWS, LON))
    return pl.pallas_call(
        second_kernel,
        grid=(ROWS,),
        in_specs=[pl.BlockSpec((1, QUAD, LON), lambda r: (r, 0, 0))] * 4
        + [
            point, point,
            whole((K, 128)),
            whole((K, K)),
            whole((8, K)),
            pl.BlockSpec((1, 8, LON), lambda r: (r, 0, 0)),
        ],
        out_specs=[
            pl.BlockSpec((1, K, LON), lambda r: (r, 0, 0)),
            pl.BlockSpec((1, 8, LON), lambda r: (r, 0, 0)),
        ],
        out_shape=[
            jax.ShapeDtypeStruct((ROWS, K, LON), jnp.bfloat16),
            jax.ShapeDtypeStruct((ROWS, 8, LON), jnp.float32),
        ],
        scratch_shapes=[pltpu.VMEM((K, LON), jnp.bfloat16), pltpu.VMEM((2, K, 128), jnp.float32)],
        compiler_params=params(),
        cost_estimate=pl.CostEstimate(
            flops=2 * K * K * LON * ROWS, bytes_accessed=4 * K * LON * ROWS, transcendentals=0
        ),
    )(*swept, rate, damp, fd, jac, forcing, wind)


def by_direction(per_component):
    return per_component.reshape(FREQ, DIR).T.reshape(K)


def body(
    adjoint_in,
    land_sea,
    depth_class,
    damping,
    transparency,
    outlets,
    flux_weight,
    jacobian,
    source_scale,
    freq_damp,
    courant,
    wind_growth,
):
    devices = lax.axis_size(AXES)
    position = lax.axis_index(AXES)
    x = adjoint_in.transpose(1, 0, 2)
    sea = land_sea.astype(jnp.float32)
    passage = sea * transparency
    rate = jnp.zeros((ROWS, LON), jnp.float32)
    for c in range(NCLASS):
        rate = jnp.where(depth_class == c, source_scale[c], rate)
    flat = (
        position * (ROWS * LON)
        + lax.broadcasted_iota(jnp.int32, (ROWS, LON), 0) * LON
        + lax.broadcasted_iota(jnp.int32, (ROWS, LON), 1)
    )
    count = jnp.sum((flat[None] == outlets[:, None, None]).astype(jnp.float32), axis=0)
    cosine = jnp.asarray(np.tile(np.cos(ANGLES), FREQ), jnp.float32)
    sine = jnp.asarray(np.tile(np.sin(ANGLES), FREQ), jnp.float32)
    forcing = jnp.pad(jnp.stack([wind_growth * cosine, wind_growth * sine]), ((0, 6), (0, 0)))
    forcing_sorted = forcing.reshape(8, FREQ, DIR).transpose(0, 2, 1).reshape(8, K)
    fw = jnp.broadcast_to(flux_weight[:, None], (K, 128))
    fd = jnp.broadcast_to(by_direction(freq_damp)[:, None], (K, 128))
    speed = jnp.broadcast_to(courant[:, None], (FREQ, 128))

    turned = turn(jacobian)
    common = (x, sea, count, rate, damping, passage, fw, fd, turned, forcing)
    down = [(i + 1, i) for i in range(devices - 1)]
    up = [(i, i + 1) for i in range(devices - 1)]
    south_edge = first_source(0, 0, HALO, True, *common)
    north_edge = first_source(1, ROWS - HALO, HALO, True, *common)
    edges = [south_edge[0], south_edge[1], north_edge[0], north_edge[1]]
    halos = [None] * 4
    for q in (0, 2, 1, 3):
        halos[q] = lax.ppermute(edges[q], AXES, down if q < 2 else up)
    north_inner, wind_high = first_source(0, HALO, ROWS - HALO, False, *common)
    south_inner, wind_low = first_source(1, 0, ROWS - HALO, False, *common)
    sorted_jac = sort_columns(turned)
    wind = jnp.concatenate([wind_low[:HALO], wind_high], axis=0)
    swept = [None] * 4
    per = QUAD // FREQ
    for q in (0, 2, 1, 3):
        angles = ANGLES[q * per : (q + 1) * per]
        table = jnp.asarray(np.abs(np.stack([np.cos(angles), np.sin(angles)])), jnp.float32)
        carrier = halos[0] if q < 2 else halos[2]
        inner = north_inner if q < 2 else south_inner
        swept[q] = sweep(q, table, passage, carrier, speed, edges[q], inner, halos[q])
    out, wind_out = second_source(swept, rate, damping, fd, sorted_jac, forcing_sorted, wind)
    return out.transpose(1, 0, 2), wind_out[:, :2, :].transpose(1, 0, 2)


def solution(mesh):
    rows = P(AXES, None)
    placed = (P(None, AXES, None), rows, rows, rows, rows, P(), P(), P(), P(), P(), P(), P())
    return jax.shard_map(
        body,
        mesh=mesh,
        in_specs=placed,
        out_specs=(P(None, AXES, None), P(None, AXES, None)),
        check_vma=False,
    )
```

time: 828 us -> 152 us (0.18); the launches traced: 816 us -> 149 us
  waiting for transfers between devices: 486 us -> 0.35 us
  other arithmetic: 129 us -> 10.8 us
  local copies, waits for them, and re-layouts: 127 us -> 11.3 us
  Pallas kernels: 0 us -> 111 us
  matrix products: 38.7 us -> 0 us
  between operations: 14.5 us -> 0.77 us
    all_gather x1 -> x0, waiting for transfers between devices: 364 us -> none  [body(): lax.all_gather(passage_local, ('pts', 'grp'), axis=0, tiled=True)]
    all_to_all x2 -> x0, waiting for transfers between devices: 121 us -> none  [the longest x1 121 us: body(): lax.all_to_all(propagated, ('pts', 'grp'), split_axis=1, concat_axis=0, t...]
    pallas_call x0 -> x11, Pallas kernels: none -> 111 us  [the longest x4 35.4 us: sweep(): pl.pallas_call(body, grid=(QUAD // FREQ,), in_specs=[pl.BlockSpec(memory_...]
    mul x4 -> x1, other arithmetic: 76.3 us -> 0.75 us  [body(): wind_growth * cosine]
    convert_element_type x5 -> x0, local copies, waits for them, and re-layouts: 70.8 us -> none  [the longest x3 51.4 us: body(): arrived.astype(jnp.float32)]
    convert_element_type x4 -> x1, other arithmetic: 51.2 us -> 1.32 us  [body(): sea = land_sea.astype(jnp.float32)]
    dot_general x4 -> x0, matrix products: 38.7 us -> none  [the longest x2 25.7 us: source_adjoint(): lax.dot_general(jacobian, spectrum, (((0,), (0,)), ((), ())), preferred_e...]
    all_to_all x2 -> x0, starting transfers between devices: 20.7 us -> none  [the longest x1 10.4 us: body(): lax.all_to_all(propagated, ('pts', 'grp'), split_axis=1, concat_axis=0, t...]
  transfers between devices with their start and end apart: 3 -> 4, of which waited for: 2 -> 1; matrix products, arithmetic and copies ran while one was open for 1% -> 3% of each run, Pallas kernels for 0% -> 43%
where the time goes in v1:
time: 152 us; the launch traced here: 149 us
  Pallas kernels  111 us (73%)
  starting transfers between devices  15.2 us (10%)
  local copies, waits for them, and re-layouts  11.3 us (7%)
  other arithmetic  10.8 us (7%)
    pallas_call x4, Pallas kernels, sweep(): pl.pallas_call(body, grid=(QUAD // FREQ,), in_specs=[pl.BlockSpec(memory_...  35.4 us
    pallas_call x4, Pallas kernels, first_source(): pl.pallas_call(body, grid=(count_rows,), in_specs=[pl.BlockSpec((1, K, LO...  33.1 us
    pallas_call x1, Pallas kernels, second_source(): pl.pallas_call(second_kernel, grid=(ROWS,), in_specs=[pl.BlockSpec((1, QU...  20.9 us
    ppermute x4, starting transfers between devices, body(): halos[q] = lax.ppermute(edges[q], AXES, down if q < 2 else up)  15.2 us
    pallas_call x1, Pallas kernels, turn(): pl.pallas_call(turn_kernel, grid=(K // 128,), in_specs=[whole((K, K))], o...  10.9 us
    pallas_call x1, Pallas kernels, sort_columns(): pl.pallas_call(sort_columns_kernel, grid=(K // 128,), in_specs=[whole((K,...  10.4 us
    select_n x1, other arithmetic, body(): rate = jnp.where(depth_class == c, source_scale[c], rate)  5.84 us
  transfers between devices with their start and end apart: 4, of which 1 were waited for; matrix products, arithmetic and copies ran while one was open for 3% of the time, Pallas kernels for 43%

profile of v1, /device:TPU:96, one launch (start us, length us, event | category | flops | bytes accessed | tf_op | source)
XLA Modules:
  0.0 149.1 jit_solution(9500687330018918115)
XLA Ops:
  0.6 1.6 %fusion.1 = (f32[1]{0:T(128)}, f32[1]{0:T(128)}, f32[1]{0:T(128)}, f32[1]{0:T(128)}, f32[1]{0:T(128)}, /*index=5*/f32[1]{0:T(128)}, f32[1]{0:T(128)}, f32[1]{0:T(128)}) fusion(f32[8]{0:T(128)} %param.26), kind=kLoop, calls=%fused_computation.10 | loop fusion | bytes 64 | tf_op jit(solution)/shard_map/slice | solution.py:331
  2.4 1.3 convert_element_type.8.refs_1_
  3.7 0.8 reshape.30
  4.6 0.7 fusion
  5.4 10.9 %shard_map.185.refs_8_.mat_ref = bf16[1152,1152]{1,0:T(8,128)(2,1)} custom-call(bf16[1152,1152]{1,0:T(8,128)(2,1)} %jac_ref.1), custom_call_target="tpu_custom_call" | custom-call | flops 3057647616 | bytes 5308416 | tf_op jit(solution)/shard_map/pallas_call | solution.py:58
  16.3 0.8 convert_reduce_fusion.refs_2_
  17.1 0.6 select_maximum_fusion.refs_9_
  17.7 5.8 %select_select_fusion = (f32[10,256]{1,0:T(8,128)}, f32[10,256]{1,0:T(8,128)}) fusion(s32[10,256]{1,0:T(8,128)S(1)} %copy-done.6, f32[]{:T(128)} %bitcast.8, f32[]{:T(128)} %bitcast.7, f32[]{:T(128)} %bitcast.6, f32[]{:T(128)} %bitcast.5, f32[]{:T(128)} %bitcast.4, f32[]{:T(128)} %bitcast.3, f32[]{:T(128)} %bitcast.2, f32[]{:T(128)} %bitcast.1, ...), kind=kLoop, calls=%fused_computation.5 | loop fusion | flops 46080 | bytes 51232 | tf_op jit(solution)/shard_map/jit(_where)/select_n | solution.py:331
  23.6 1.0 broadcast_in_dim.60.refs_7_.fd_ref
  24.6 1.1 broadcast_in_dim.58.refs_6_
  25.7 6.5 %shard_map.190 = (bf16[4,304,256]{2,1,0:T(8,128)(2,1)}, bf16[4,288,256]{2,1,0:T(8,128)(2,1)}) custom-call(bf16[10,1152,256]{2,1,0:T(8,128)(2,1)} %bitcast.14, f32[10,256]{1,0:T(8,128)} %convert_element_type.8.refs_1_, f32[10,256]{1,0:T(8,128)} %convert_reduce_fusion.refs_2_, f32[10,256]{1,0:T(8,128)} %get-tuple-element.32.refs_3_.rate_ref, ...), custom_call_target="tpu_custom_call" | custom-call | flops 1358954496 | bytes 4718592 | tf_op jit(solution)/shard_map/pallas_call | solution.py:153
  32.2 3.5 %collective-permute-start.3 = (bf16[4,288,256]{2,1,0:T(8,128)(2,1)}, bf16[4,288,256]{2,1,0:T(8,128)(2,1)S(1)}, u32[]{:S(2)}, u32[]{:S(2)}) collective-permute-start(bf16[4,288,256]{2,1,0:T(8,128)(2,1)} %get-tuple-element.17.refs_4_), channel_id=1, source_target_pairs={{0,1},{1,2},{2,3},{3,4},{4,5},{5,6},{6,7},{7,8},{8,9},{9,10},{10,1... | collective-permute-start | bytes 1769480 | tf_op jit(solution)/shard_map/ppermute | solution.py:355
  35.7 3.3 %collective-permute-start.2 = (bf16[4,304,256]{2,1,0:T(8,128)(2,1)}, bf16[4,304,256]{2,1,0:T(8,128)(2,1)S(1)}, u32[]{:S(2)}, u32[]{:S(2)}) collective-permute-start(bf16[4,304,256]{2,1,0:T(8,128)(2,1)} %get-tuple-element.15.refs_4_), channel_id=1, source_target_pairs={{0,1},{1,2},{2,3},{3,4},{4,5},{5,6},{6,7},{7,8},{8,9},{9,10},{10,1... | collective-permute-start | bytes 1867784 | tf_op jit(solution)/shard_map/ppermute | solution.py:355
  39.0 6.6 %shard_map.186 = (bf16[4,304,256]{2,1,0:T(8,128)(2,1)}, bf16[4,288,256]{2,1,0:T(8,128)(2,1)}) custom-call(bf16[10,1152,256]{2,1,0:T(8,128)(2,1)} %bitcast.15, f32[10,256]{1,0:T(8,128)} %convert_element_type.8.refs_1_, f32[10,256]{1,0:T(8,128)} %convert_reduce_fusion.refs_2_, f32[10,256]{1,0:T(8,128)} %get-tuple-element.32.refs_3_.rate_ref, ...), custom_call_target="tpu_custom_call" | custom-call | flops 1358954496 | bytes 4718592 | tf_op jit(solution)/shard_map/pallas_call | solution.py:153
  45.6 6.5 %collective-permute-start.1 = (bf16[4,288,256]{2,1,0:T(8,128)(2,1)}, bf16[4,288,256]{2,1,0:T(8,128)(2,1)S(1)}, u32[]{:S(2)}, u32[]{:S(2)}) collective-permute-start(bf16[4,288,256]{2,1,0:T(8,128)(2,1)} %get-tuple-element.14.refs_4_), channel_id=1, source_target_pairs={{1,0},{2,1},{3,2},{4,3},{5,4},{6,5},{7,6},{8,7},{9,8},{10,9},{11,1... | collective-permute-start | bytes 1769480 | tf_op jit(solution)/shard_map/ppermute | solution.py:355
  52.1 1.9 %collective-permute-start = (bf16[4,304,256]{2,1,0:T(8,128)(2,1)}, bf16[4,304,256]{2,1,0:T(8,128)(2,1)S(1)}, u32[]{:S(2)}, u32[]{:S(2)}) collective-permute-start(bf16[4,304,256]{2,1,0:T(8,128)(2,1)} %get-tuple-element.12.refs_4_), channel_id=1, source_target_pairs={{1,0},{2,1},{3,2},{4,3},{5,4},{6,5},{7,6},{8,7},{9,8},{10,9},{11,1... | collective-permute-start | bytes 1867784 | tf_op jit(solution)/shard_map/ppermute | solution.py:355
  54.0 9.9 %shard_map.191 = (bf16[6,576,256]{2,1,0:T(8,128)(2,1)}, f32[6,8,256]{2,1,0:T(8,128)}) custom-call(bf16[10,1152,256]{2,1,0:T(8,128)(2,1)} %bitcast.16, f32[10,256]{1,0:T(8,128)} %convert_element_type.8.refs_1_, f32[10,256]{1,0:T(8,128)} %convert_reduce_fusion.refs_2_, f32[10,256]{1,0:T(8,128)} %get-tuple-element.32.refs_3_.rate_ref, f32[10,256]{1,0:T(8,128)} %damp_ref.1, ...), custom_call_target="tpu_custom_call" | custom-call | flops 2038431744 | bytes 7077888 | tf_op jit(solution)/shard_map/pallas_call | solution.py:153
  64.3 0.7 reshape.32.forcing_ref
  65.0 0.8 slice.38
  65.8 10.0 %shard_map.187 = (bf16[6,576,256]{2,1,0:T(8,128)(2,1)}, f32[6,8,256]{2,1,0:T(8,128)}) custom-call(bf16[10,1152,256]{2,1,0:T(8,128)(2,1)} %bitcast.17, f32[10,256]{1,0:T(8,128)} %convert_element_type.8.refs_1_, f32[10,256]{1,0:T(8,128)} %convert_reduce_fusion.refs_2_, f32[10,256]{1,0:T(8,128)} %get-tuple-element.32.refs_3_.rate_ref, f32[10,256]{1,0:T(8,128)} %damp_ref.1, ...), custom_call_target="tpu_custom_call" | custom-call | flops 2038431744 | bytes 7077888 | tf_op jit(solution)/shard_map/pallas_call | solution.py:153
  75.8 1.4 pad_maximum_fusion.wind_in
  77.2 10.4 %shard_map.194.jac_ref = bf16[1152,1152]{1,0:T(8,128)(2,1)} custom-call(bf16[1152,1152]{1,0:T(8,128)(2,1)} %shard_map.185.refs_8_.mat_ref), custom_call_target="tpu_custom_call" | custom-call | flops 3057647616 | bytes 5308416 | tf_op jit(solution)/shard_map/pallas_call | solution.py:77
  87.9 0.7 broadcast_in_dim.61.refs_3_
  88.8 8.9 %shard_map.192.v2 = bf16[10,288,256]{2,1,0:T(8,128)(2,1)} custom-call(f32[2,9]{1,0:T(2,128)} %constant.46.clone.refs_0_, f32[10,256]{1,0:T(8,128)} %get-tuple-element.33.refs_5_.refs_1_, bf16[4,304,256]{2,1,0:T(8,128)(2,1)} %copy-done.1, f32[32,128]{1,0:T(8,128)} %broadcast_in_dim.61.refs_3_, bf16[4,304,256]{2,1,0:T(8,128)(2,1)} %get-tuple-element.15.refs_4_, ...), custom_call_target="tpu_custom_call" | custom-call | flops 23740416 | bytes 3538944 | tf_op jit(solution)/shard_map/pallas_call | solution.py:232
  97.6 0.8 copy-done.4
  98.4 8.8 %shard_map.193.v3 = bf16[10,288,256]{2,1,0:T(8,128)(2,1)} custom-call(f32[2,9]{1,0:T(2,128)} %constant.47.clone.refs_0_, f32[10,256]{1,0:T(8,128)} %get-tuple-element.33.refs_5_.refs_1_, bf16[4,304,256]{2,1,0:T(8,128)(2,1)} %copy-done.1, f32[32,128]{1,0:T(8,128)} %broadcast_in_dim.61.refs_3_, bf16[4,288,256]{2,1,0:T(8,128)(2,1)} %get-tuple-element.17.refs_4_, ...), custom_call_target="tpu_custom_call" | custom-call | flops 23740416 | bytes 3538944 | tf_op jit(solution)/shard_map/pallas_call | solution.py:232
  107.3 0.8 copy-done
  108.1 8.9 %shard_map.188.v0 = bf16[10,288,256]{2,1,0:T(8,128)(2,1)} custom-call(f32[2,9]{1,0:T(2,128)} %constant.46.clone.refs_0_, f32[10,256]{1,0:T(8,128)} %get-tuple-element.33.refs_5_.refs_1_, bf16[4,304,256]{2,1,0:T(8,128)(2,1)} %copy-done, f32[32,128]{1,0:T(8,128)} %broadcast_in_dim.61.refs_3_, bf16[4,304,256]{2,1,0:T(8,128)(2,1)} %get-tuple-element.12.refs_4_, ...), custom_call_target="tpu_custom_call" | custom-call | flops 23740416 | bytes 3538944 | tf_op jit(solution)/shard_map/pallas_call | solution.py:232
  117.0 0.8 copy-done.3
  117.8 8.8 %shard_map.189.v1 = bf16[10,288,256]{2,1,0:T(8,128)(2,1)} custom-call(f32[2,9]{1,0:T(2,128)} %constant.47.clone.refs_0_, f32[10,256]{1,0:T(8,128)} %get-tuple-element.33.refs_5_.refs_1_, bf16[4,304,256]{2,1,0:T(8,128)(2,1)} %copy-done, f32[32,128]{1,0:T(8,128)} %broadcast_in_dim.61.refs_3_, bf16[4,288,256]{2,1,0:T(8,128)(2,1)} %get-tuple-element.14.refs_4_, ...), custom_call_target="tpu_custom_call" | custom-call | flops 23740416 | bytes 3538944 | tf_op jit(solution)/shard_map/pallas_call | solution.py:232
  126.6 20.9 %shard_map.195 = (bf16[10,1152,256]{2,1,0:T(8,128)(2,1)}, f32[10,8,256]{2,1,0:T(8,128)}) custom-call(bf16[10,288,256]{2,1,0:T(8,128)(2,1)} %shard_map.188.v0, bf16[10,288,256]{2,1,0:T(8,128)(2,1)} %shard_map.189.v1, bf16[10,288,256]{2,1,0:T(8,128)(2,1)} %shard_map.192.v2, bf16[10,288,256]{2,1,0:T(8,128)(2,1)} %shard_map.193.v3, ...), custom_call_target="tpu_custom_call" | custom-call | flops 6794772480 | bytes 11796480 | tf_op jit(solution)/shard_map/pallas_call | solution.py:279
  147.6 1.5 %slice_bitcast_fusion = f32[2,10,256]{2,0,1:T(2,128)} fusion(f32[10,8,256]{2,1,0:T(8,128)} %get-tuple-element.21), kind=kLoop, calls=%fused_computation.4 | loop fusion | bytes 40960 | tf_op jit(solution)/shard_map/transpose | solution.py:369
  (31 shorter events, 1.0 us)
Async XLA Ops:
  5.4 11.0 %copy-start.9 = (s32[64]{0:T(128)S(1)}, s32[64]{0:T(128)}, u32[]{:S(2)}) copy-start(s32[64]{0:T(128)} %param.23) | copy-start | bytes 772
  5.4 12.3 %copy-start.5 = (s32[10,256]{1,0:T(8,128)S(1)}, s32[10,256]{1,0:T(8,128)}, u32[]{:S(2)}) copy-start(s32[10,256]{1,0:T(8,128)} %param.19) | copy-start | bytes 30724
  5.4 12.3 %copy-start.6 = (s32[10,256]{1,0:T(8,128)S(1)}, s32[10,256]{1,0:T(8,128)}, u32[]{:S(2)}) copy-start(s32[10,256]{1,0:T(8,128)} %param.20) | copy-start | bytes 30724
  5.4 12.3 %copy-start.7 = (f32[10,256]{1,0:T(8,128)S(1)}, f32[10,256]{1,0:T(8,128)}, u32[]{:S(2)}) copy-start(f32[10,256]{1,0:T(8,128)} %param.22) | copy-start | bytes 30724
  5.4 19.2 %copy-start.8 = (f32[1152]{0:T(1024)S(1)}, f32[1152]{0:T(1024)}, u32[]{:S(2)}) copy-start(f32[1152]{0:T(1024)} %param.24) | copy-start | bytes 13828
  32.2 65.4 %collective-permute-start.3 = (bf16[4,288,256]{2,1,0:T(8,128)(2,1)}, bf16[4,288,256]{2,1,0:T(8,128)(2,1)S(1)}, u32[]{:S(2)}, u32[]{:S(2)}) collective-permute-start(bf16[4,288,256]{2,1,0:T(8,128)(2,1)} %get-tuple-element.17.refs_4_), channel_id=1, source_target_pairs={{0,1},{1,2},{2,3},{3,4},{4,5},{5,6},{6,7},{7,8},{8,9},{9,10},{10,1... | collective-permute-start | bytes 1769480 | tf_op jit(solution)/shard_map/ppermute | solution.py:355
  35.7 52.2 %collective-permute-start.2 = (bf16[4,304,256]{2,1,0:T(8,128)(2,1)}, bf16[4,304,256]{2,1,0:T(8,128)(2,1)S(1)}, u32[]{:S(2)}, u32[]{:S(2)}) collective-permute-start(bf16[4,304,256]{2,1,0:T(8,128)(2,1)} %get-tuple-element.15.refs_4_), channel_id=1, source_target_pairs={{0,1},{1,2},{2,3},{3,4},{4,5},{5,6},{6,7},{7,8},{8,9},{9,10},{10,1... | collective-permute-start | bytes 1867784 | tf_op jit(solution)/shard_map/ppermute | solution.py:355
  45.6 71.4 %collective-permute-start.1 = (bf16[4,288,256]{2,1,0:T(8,128)(2,1)}, bf16[4,288,256]{2,1,0:T(8,128)(2,1)S(1)}, u32[]{:S(2)}, u32[]{:S(2)}) collective-permute-start(bf16[4,288,256]{2,1,0:T(8,128)(2,1)} %get-tuple-element.14.refs_4_), channel_id=1, source_target_pairs={{1,0},{2,1},{3,2},{4,3},{5,4},{6,5},{7,6},{8,7},{9,8},{10,9},{11,1... | collective-permute-start | bytes 1769480 | tf_op jit(solution)/shard_map/ppermute | solution.py:355
  52.1 11.9 %copy-start.2 = (f32[8,1152]{1,0:T(8,128)S(1)}, f32[8,1152]{1,0:T(8,128)}, u32[]{:S(2)}) copy-start(f32[8,1152]{1,0:T(8,128)} %select_maximum_fusion.refs_9_) | copy-start | bytes 110596
  52.1 55.2 %collective-permute-start = (bf16[4,304,256]{2,1,0:T(8,128)(2,1)}, bf16[4,304,256]{2,1,0:T(8,128)(2,1)S(1)}, u32[]{:S(2)}, u32[]{:S(2)}) collective-permute-start(bf16[4,304,256]{2,1,0:T(8,128)(2,1)} %get-tuple-element.12.refs_4_), channel_id=1, source_target_pairs={{1,0},{2,1},{3,2},{4,3},{5,4},{6,5},{7,6},{8,7},{9,8},{10,9},{11,1... | collective-permute-start | bytes 1867784 | tf_op jit(solution)/shard_map/ppermute | solution.py:355
  77.2 10.7 %copy-start.10 = (f32[32]{0:T(128)S(1)}, f32[32]{0:T(128)}, u32[]{:S(2)}) copy-start(f32[32]{0:T(128)} %param.28) | copy-start | bytes 388
  87.9 0.8 copy-start.1
  97.6 0.8 copy-start.4
  107.3 0.8 copy-start
  117.0 0.8 copy-start.3

commit v2 on v0

v2 whole, which is shorter than its diff:
```python
import math

import jax
import jax.numpy as jnp
import numpy as np
from jax import lax
from jax.experimental import pallas as pl
from jax.experimental.pallas import tpu as pltpu
from jax.sharding import PartitionSpec as P

DIR = 36
FREQ = 32
NSUB = 4
NCLASS = 8
LON = 256
K = DIR * FREQ
HALF = K // 2
QUAD = K // 4
ROWS = 10
HALO = NSUB
TAIL = 16
AXES = ("pts", "grp")
VMEM = 56 * 1024 * 1024

ANGLES = 2.0 * math.pi * (np.arange(DIR) + 0.5) / DIR


def params():
    return pltpu.CompilerParams(vmem_limit_bytes=VMEM)


def whole(shape):
    return pl.BlockSpec(shape, lambda *_: (0,) * len(shape))


def block(*shape):
    return pl.BlockSpec(shape, lambda i: (i,) + (0,) * (len(shape) - 1))


def smem():
    return pl.BlockSpec(memory_space=pltpu.SMEM)


def cost(flops, read):
    return pl.CostEstimate(flops=int(flops), bytes_accessed=int(read), transcendentals=0)


def three_pieces(x):
    hi = x.astype(jnp.bfloat16).astype(jnp.float32)
    mid = (x - hi).astype(jnp.bfloat16).astype(jnp.float32)
    return hi, mid, x - hi - mid


def stack_pieces(pieces):
    which = lax.broadcasted_iota(jnp.int32, (8, LON), 0)
    rows = jnp.zeros((8, LON), jnp.float32)
    for at, piece in enumerate(pieces):
        rows = jnp.where(which == at, jnp.broadcast_to(piece, (8, LON)), rows)
    return jnp.concatenate([rows, jnp.zeros((8, LON), jnp.float32)], axis=0).astype(jnp.bfloat16)


def contract(matrix, spectrum):
    return lax.dot_general(matrix, spectrum, (((0,), (0,)), ((), ())), preferred_element_type=jnp.float32)


def column(vector):
    return jnp.broadcast_to(vector, (128, K)).T


def point_fields(land_ref, depth_ref, outlets_ref, scale_ref, sea, count, rate):
    sea[...] = land_ref[...].astype(jnp.float32)
    depth = depth_ref[...]
    total = jnp.zeros((ROWS, LON), jnp.float32)
    for c in range(NCLASS):
        total = jnp.where(depth == c, scale_ref[c], total)
    rate[...] = total
    shape = (ROWS, LON)
    flat = lax.broadcasted_iota(jnp.int32, shape, 0) * LON + lax.broadcasted_iota(jnp.int32, shape, 1)
    flat = flat + lax.axis_index(AXES) * (ROWS * LON)
    hits = jnp.zeros(shape, jnp.float32)
    for n in range(outlets_ref.shape[0]):
        hits = hits + jnp.where(flat == outlets_ref[n], 1.0, 0.0)
    count[...] = hits


def first_kernel(part, x_ref, land_ref, depth_ref, damp_ref, clear_ref, outlets_ref, scale_ref,
                 comp_a, comp_b, comp_c, jac_ref, *rest):
    sea, count, rate, held = rest[-4:]
    step = pl.program_id(0)
    if part == "south":
        fw_ref, fd_ref, wave_ref, message, other, wind_ref = rest[:-4]
        first_row = 2 * step
    else:
        fw_ref, fd_ref, wave_ref = comp_a, comp_b, comp_c
        message, other, middle, wind_ref = rest[:-4]
        first_row = jnp.where(step == 2, 4, 2 * step + 6)

    @pl.when(step == 0)
    def _():
        point_fields(land_ref, depth_ref, outlets_ref, scale_ref, sea, count, rate)
        if part == "south":
            fw_ref[...] = column(comp_a[0:1, :])
            fd_ref[...] = column(comp_a[1:2, :])
            forcing = column(comp_a[2:3, :]) * comp_b[...]
            hi, mid, low = three_pieces(forcing)
            lane = lax.broadcasted_iota(jnp.int32, (K, 128), 1)
            mixed = jnp.where(lane < 8, hi, jnp.where(lane < 16, mid, low))
            wave_ref[...] = mixed.astype(jnp.bfloat16)

    fw = fw_ref[...]
    fw = jnp.concatenate([fw, fw], axis=1)
    seeds = []
    fields = []
    for e in range(2):
        r = first_row + e
        lone = sea[pl.ds(r, 1), :] * (x_ref[e].astype(jnp.float32) + fw * count[pl.ds(r, 1), :])
        seeds.append(lone.astype(jnp.bfloat16))
        fields.append((rate[pl.ds(r, 1), :], damp_ref[pl.ds(r, 1), :]))
    spectrum = jnp.concatenate(seeds, axis=1)
    for m in range(3):
        rows = slice(m * 384, (m + 1) * 384)
        mixed = contract(jac_ref[:, rows], spectrum)
        fd = fd_ref[rows, :]
        for piece in range(4):
            e, side = divmod(piece, 2)
            lanes = slice(side * 128, (side + 1) * 128)
            at = slice(piece * 128, (piece + 1) * 128)
            v = seeds[e][rows, lanes].astype(jnp.float32)
            held[piece, rows, :] = (
                v + fields[e][0][:, lanes] * mixed[:, at] - (fields[e][1][:, lanes] * fd) * v
            )
    wind = contract(wave_ref[...], spectrum)
    wind = wind[0:8] + wind[8:16] + wind[16:24]
    wind_ref[0] = wind[:, :LON]
    wind_ref[1] = wind[:, LON:]

    def half_out(half, ref):
        for d in range(18):
            for piece in range(4):
                e, side = divmod(piece, 2)
                ref[e, d * FREQ : (d + 1) * FREQ, side * 128 : (side + 1) * 128] = held[
                    piece, pl.ds(half * 18 + d, FREQ, stride=DIR), :
                ].astype(jnp.bfloat16)

    def message_out(half):
        half_out(half, message)
        for e in range(2):
            r = first_row + e
            passage = sea[pl.ds(r, 1), :] * clear_ref[pl.ds(r, 1), :]
            message[e, HALF : HALF + TAIL, :] = stack_pieces(three_pieces(passage))

    if part == "south":
        message_out(0)
        half_out(1, other)
    else:
        half_out(0, other)

        @pl.when(step < 2)
        def _():
            message_out(1)

        @pl.when(step == 2)
        def _():
            half_out(1, middle)


def first_source(part, x, land, depth, damping, clear, outlets, scale, comps, jacobian):
    point = whole((ROWS, LON))
    comp_specs = [whole(c.shape) for c in comps]
    out_specs, out_shape = [], []

    def add(spec, shape, dtype=jnp.bfloat16):
        out_specs.append(spec)
        out_shape.append(jax.ShapeDtypeStruct(shape, dtype))

    def rows_at(index, size):
        return pl.BlockSpec((2, size, LON), lambda i: (index(i), 0, 0))

    if part == "south":
        count_rows = 4
        source = rows_at(lambda i: i, K)
        for dtype in (jnp.float32, jnp.float32, jnp.bfloat16):
            add(whole((K, 128)), (K, 128), dtype)
        add(rows_at(lambda i: i, HALF + TAIL), (4, HALF + TAIL, LON))
        add(rows_at(lambda i: i, HALF), (4, HALF, LON))
        add(rows_at(lambda i: i, 8), (4, 8, LON), jnp.float32)
    else:
        count_rows = 6
        source = rows_at(lambda i: jnp.where(i == 2, 2, i + 3), K)
        add(rows_at(lambda i: jnp.minimum(i, 1), HALF + TAIL), (4, HALF + TAIL, LON))
        add(rows_at(lambda i: jnp.where(i == 2, 0, i + 1), HALF), (6, HALF, LON))
        add(rows_at(lambda i: 0, HALF), (2, HALF, LON))
        add(rows_at(lambda i: jnp.where(i == 2, 0, i + 1), 8), (6, 8, LON), jnp.float32)

    def body(*refs):
        first_kernel(part, *refs)

    return pl.pallas_call(
        body,
        grid=(count_rows // 2,),
        in_specs=[source] + [point] * 4 + [smem(), smem()] + comp_specs + [whole((K, K))],
        out_specs=out_specs,
        out_shape=out_shape,
        scratch_shapes=[pltpu.VMEM((ROWS, LON), jnp.float32)] * 3 + [pltpu.VMEM((4, K, 128), jnp.float32)],
        compiler_params=params(),
        cost_estimate=cost(0, 0),
        name="first_source_" + part,
    )(x, land, depth, damping, clear, outlets, scale, *comps, jacobian)


SPLIT = 1
PART = QUAD // SPLIT
STEPS = 4 * SPLIT


def sweep_rows(quad, table_ref, courant_ref, pass_rows, step, load, emit):
    east = quad in (0, 3)
    lane = lax.broadcasted_iota(jnp.int32, (16, 128), 1)
    last = lane == 127 if east else lane == 0
    shift = 127 if east else 1
    halves = (slice(0, 128), slice(128, 256))
    order = halves if east else halves[::-1]

    def chunk(i, carry):
        d = step * (PART // FREQ) + i // 2
        rows = pl.ds(pl.multiple_of(i * 16, 16), 16)
        speed = courant_ref[pl.ds(pl.multiple_of((i % 2) * 16, 16), 16), :]
        across = speed * table_ref[0, d]
        upward = speed * table_ref[1, d]
        centre = 1.0 - across - upward
        walled = jnp.where(last, 0.0, across)

        def advance(v, first):
            turned = [[pltpu.roll(value, shift, 1) for value in half[:-1]] for half in v]
            fresh = [[], []]
            for t in range(len(v[0]) - 1):
                beside = (jnp.where(last, turned[1][t], turned[0][t]), turned[1][t])
                for half, weight in ((0, across), (1, walled)):
                    fresh[half].append(
                        pass_rows[first + t, :, order[half]]
                        * (centre * v[half][t] + weight * beside[half] + upward * v[half][t + 1])
                    )
            return fresh

        emit(rows, order, advance)
        return carry

    lax.fori_loop(0, PART // 16, chunk, 0, unroll=3)


def own_passage(land_ref, clear_ref, pass_rows, north):
    passage = land_ref[...].astype(jnp.float32) * clear_ref[...]
    for t in range(ROWS):
        own = t if north else ROWS - 1 - t
        pass_rows[t] = jnp.broadcast_to(passage[own : own + 1, :], (16, LON))


def inner_kernel(table_ref, land_ref, clear_ref, courant_ref, low_n, high_n, low_s, mid_s, high_s,
                 done_n, state_n, done_s, state_s, pass_rows):
    step = pl.program_id(0)

    def quadrant(quad):
        north = quad < 2

        @pl.when(step == quad * SPLIT)
        def _():
            own_passage(land_ref, clear_ref, pass_rows, north)

        def load(t, rows, lanes):
            r = t if north else ROWS - 1 - t
            if north:
                value = low_n[r, rows, lanes] if r < 4 else high_n[r - 4, rows, lanes]
            else:
                value = low_s[r, rows, lanes] if r < 4 else mid_s[r - 4, rows, lanes] if r < 6 else high_s[r - 6, rows, lanes]
            return value.astype(jnp.float32)

        done, state = (done_n, state_n) if north else (done_s, state_s)

        def emit(rows, order, advance):
            v = [[load(t, rows, lanes) for t in range(ROWS)] for lanes in order]
            for s in range(NSUB):
                v = advance(v, 0)
                if s < NSUB - 1:
                    for half in range(2):
                        state[s, rows, order[half]] = v[half][-1]
            for half in range(2):
                for t in range(ROWS - NSUB):
                    done[t if north else ROWS - NSUB - 1 - t, rows, order[half]] = v[half][t].astype(jnp.bfloat16)

        @pl.when((step >= quad * SPLIT) & (step < (quad + 1) * SPLIT))
        def _():
            sweep_rows(quad, table_ref, courant_ref, pass_rows, step, load, emit)

    for quad in range(4):
        quadrant(quad)


def north_rows(count_rows, at=0):
    return pl.BlockSpec((count_rows, PART, LON), lambda i: (at, jnp.minimum(i, STEPS // 2 - 1), 0))


def south_rows(count_rows, at=0):
    return pl.BlockSpec((count_rows, PART, LON), lambda i: (at, jnp.maximum(i - STEPS // 2, 0), 0))


def inner_sweep(table, land, clear, courant, low_n, high_n, low_s, mid_s, high_s):
    return pl.pallas_call(
        inner_kernel,
        grid=(STEPS,),
        in_specs=[
            smem(), whole((ROWS, LON)), whole((ROWS, LON)), whole((FREQ, 128)),
            north_rows(4), north_rows(6), south_rows(4), south_rows(2), south_rows(4),
        ],
        out_specs=[north_rows(6), north_rows(3), south_rows(6), south_rows(3)],
        out_shape=[
            jax.ShapeDtypeStruct((6, HALF, LON), jnp.bfloat16),
            jax.ShapeDtypeStruct((3, HALF, LON), jnp.float32),
        ] * 2,
        scratch_shapes=[pltpu.VMEM((ROWS, 16, LON), jnp.float32)],
        compiler_params=params(),
        cost_estimate=cost(0, 0),
        name="inner_sweep",
    )(table, land, clear, courant, low_n, high_n, low_s, mid_s, high_s)


def outer_kernel(north, table_ref, land_ref, clear_ref, courant_ref, halo_pass, first, state, halo, done, pass_rows):
    step = pl.program_id(0)

    @pl.when(step == 0)
    def _():
        own_passage(land_ref, clear_ref, pass_rows, north)
        for t in range(HALO - 1):
            pieces = halo_pass[t if north else HALO - 1 - t].astype(jnp.float32)
            pass_rows[ROWS + t] = jnp.broadcast_to(pieces[0:1] + pieces[1:2] + pieces[2:3], (16, LON))

    def emit(rows, order, advance):
        v = [
            [first[0, rows, lanes].astype(jnp.float32)]
            + [halo[t if north else HALO - 1 - t, rows, lanes].astype(jnp.float32) for t in range(HALO)]
            for lanes in order
        ]
        for s in range(NSUB):
            v = advance(v, ROWS - 1 - s)
            if s < NSUB - 1:
                v = [[state[s, rows, lanes]] + half for lanes, half in zip(order, v)]
        for half in range(2):
            for t in range(HALO):
                done[t if north else HALO - 1 - t, rows, order[half]] = v[half][t].astype(jnp.bfloat16)

    for quad in (0, 1) if north else (2, 3):
        at = quad % 2

        @pl.when((step >= at * SPLIT) & (step < (at + 1) * SPLIT))
        def _():
            sweep_rows(quad, table_ref, courant_ref, pass_rows, step + (quad - at) * SPLIT, None, emit)


def outer_sweep(north, table, land, clear, courant, first, state, halo):
    def rows_of(count_rows, at=0):
        return pl.BlockSpec((count_rows, PART, LON), lambda i: (at, i, 0))

    def body(*refs):
        outer_kernel(north, *refs)

    return pl.pallas_call(
        body,
        grid=(STEPS // 2,),
        in_specs=[
            smem(), whole((ROWS, LON)), whole((ROWS, LON)), whole((FREQ, 128)),
            pl.BlockSpec((HALO, TAIL, LON), lambda i: (0, HALF // TAIL, 0)),
            rows_of(1, 5 if north else 0), rows_of(3), rows_of(4),
        ],
        out_specs=rows_of(4),
        out_shape=jax.ShapeDtypeStruct((4, HALF, LON), jnp.bfloat16),
        scratch_shapes=[pltpu.VMEM((ROWS + HALO - 1, 16, LON), jnp.float32)],
        compiler_params=params(),
        cost_estimate=cost(16 * 7 * K * LON * 40, 50 * K * LON),
        name="outer_sweep_north" if north else "outer_sweep_south",
    )(table, land, clear, courant, halo, first, state, halo)


def second_kernel(in_n, out_n, in_s, out_s, land_ref, depth_ref, damp_ref, scale_ref, fd_ref, jac_ref, wave_ref,
                  wind_a, wind_b, out_ref, wind_ref, rate, held):
    step = pl.program_id(0)

    @pl.when(step == 0)
    def _():
        depth = depth_ref[...]
        total = jnp.zeros((ROWS, LON), jnp.float32)
        for c in range(NCLASS):
            total = jnp.where(depth == c, scale_ref[c], total)
        rate[...] = total

    def take(half, ref):
        for d in range(18):
            for piece in range(4):
                e, side = divmod(piece, 2)
                held[piece, pl.ds(half * 18 + d, FREQ, stride=DIR), :] = ref[
                    e, d * FREQ : (d + 1) * FREQ, side * 128 : (side + 1) * 128
                ].astype(jnp.float32)

    pl.when(step < 3)(lambda: take(0, in_n))
    pl.when(step >= 3)(lambda: take(0, out_n))
    pl.when(step < 2)(lambda: take(1, out_s))
    pl.when(step >= 2)(lambda: take(1, in_s))
    spectrum = jnp.concatenate([held[piece].astype(jnp.bfloat16) for piece in range(4)], axis=1)
    fields = []
    for e in range(2):
        r = 2 * step + e
        fields.append((rate[pl.ds(r, 1), :], damp_ref[pl.ds(r, 1), :]))
    for m in range(3):
        rows = slice(m * 384, (m + 1) * 384)
        mixed = contract(jac_ref[:, rows], spectrum)
        fd = fd_ref[rows, :]
        for piece in range(4):
            e, side = divmod(piece, 2)
            lanes = slice(side * 128, (side + 1) * 128)
            at = slice(piece * 128, (piece + 1) * 128)
            v = held[piece, rows, :]
            out_ref[e, rows, lanes] = (
                v + fields[e][0][:, lanes] * mixed[:, at] - (fields[e][1][:, lanes] * fd) * v
            ).astype(jnp.bfloat16)
    wind = contract(wave_ref[...], spectrum)
    wind = wind[0:8] + wind[8:16] + wind[16:24]
    for e in range(2):
        before = jnp.where(step < 2, wind_a[e], wind_b[e])
        wind_ref[e] = (before + wind[:, e * LON : (e + 1) * LON])[:2]


def second_source(in_n, out_n, in_s, out_s, land, depth, damping, scale, fd, jac, wave, wind_low, wind_high):
    point = whole((ROWS, LON))

    def at(index, size):
        return pl.BlockSpec((2, size, LON), lambda i: (index(i), 0, 0))

    return pl.pallas_call(
        second_kernel,
        grid=(ROWS // 2,),
        in_specs=[
            at(lambda i: jnp.minimum(i, 2), HALF),
            at(lambda i: jnp.maximum(i - 3, 0), HALF),
            at(lambda i: jnp.maximum(i - 2, 0), HALF),
            at(lambda i: jnp.minimum(i, 1), HALF),
            point, point, point, smem(),
            whole((K, 128)), whole((K, K)), whole((K, 128)),
            at(lambda i: jnp.minimum(i, 1), 8),
            at(lambda i: jnp.maximum(i - 2, 0), 8),
        ],
        out_specs=[block(2, K, LON), block(2, 2, LON)],
        out_shape=[
            jax.ShapeDtypeStruct((ROWS, K, LON), jnp.bfloat16),
            jax.ShapeDtypeStruct((ROWS, 2, LON), jnp.float32),
        ],
        scratch_shapes=[pltpu.VMEM((ROWS, LON), jnp.float32), pltpu.VMEM((4, K, 128), jnp.float32)],
        compiler_params=params(),
        cost_estimate=cost(2 * K * K * LON * ROWS * 2, 4 * K * LON * ROWS),
        name="second_source",
    )(in_n, out_n, in_s, out_s, land, depth, damping, scale, fd, jac, wave, wind_low, wind_high)


def body(
    adjoint_in,
    land_sea,
    depth_class,
    damping,
    transparency,
    outlets,
    flux_weight,
    jacobian,
    source_scale,
    freq_damp,
    courant,
    wind_growth,
):
    devices = lax.axis_size(AXES)
    x = adjoint_in.transpose(1, 0, 2)
    compass = np.zeros((K, 128), np.float32)
    for at in range(3):
        compass[:, 8 * at] = np.tile(np.cos(ANGLES), FREQ)
        compass[:, 8 * at + 1] = np.tile(np.sin(ANGLES), FREQ)
    comps = (jnp.stack([flux_weight, freq_damp, wind_growth]), jnp.asarray(compass))
    common = (x, land_sea, depth_class, damping, transparency, outlets, source_scale)
    fw, fd, wave, low_n, low_s, wind_low = first_source("south", *common, comps + (comps[0],), jacobian)
    halo_n = lax.ppermute(low_n, AXES, [(i + 1, i) for i in range(devices - 1)])
    high_s, high_n, mid_s, wind_high = first_source("north", *common, (fw, fd, wave), jacobian)
    halo_s = lax.ppermute(high_s, AXES, [(i, i + 1) for i in range(devices - 1)])
    speed = jnp.broadcast_to(courant[:, None], (FREQ, 128))
    table = jnp.asarray(np.abs(np.stack([np.cos(ANGLES), np.sin(ANGLES)])), jnp.float32)
    local = (table, land_sea, transparency, speed)
    in_n, state_n, in_s, state_s = inner_sweep(*local, low_n, high_n, low_s, mid_s, high_s)
    out_n = outer_sweep(True, *local, high_n, state_n, halo_n)
    state_s, out_n = lax.optimization_barrier((state_s, out_n))
    out_s = outer_sweep(False, *local, low_s, state_s, halo_s)
    out, wind_out = second_source(
        in_n, out_n, in_s, out_s, land_sea, depth_class, damping, source_scale, fd, jacobian, wave,
        wind_low, wind_high,
    )
    return out.transpose(1, 0, 2), wind_out.transpose(1, 0, 2)


def solution(mesh):
    rows = P(AXES, None)
    placed = (P(None, AXES, None), rows, rows, rows, rows, P(), P(), P(), P(), P(), P(), P())
    return jax.shard_map(
        body,
        mesh=mesh,
        in_specs=placed,
        out_specs=(P(None, AXES, None), P(None, AXES, None)),
        check_vma=False,
    )
```

time: 828 us -> 101 us (0.12)
  the two profiles are of different devices: /device:TPU:96 before, /device:TPU:6 now
where the time goes in v2:
time: 101 us
  Pallas kernels  69.5 us (69%)
  waiting for transfers between devices  19.1 us (19%)
  starting transfers between devices  5.84 us (6%)
  local copies, waits for them, and re-layouts  4.84 us (5%)
    pallas_call x2, Pallas kernels, first_source(): pl.pallas_call(body, grid=(count_rows // 2,), in_specs=[source] + [point]...  20.2 us
    pallas_call x1, Pallas kernels, inner_sweep(): pl.pallas_call(inner_kernel, grid=(STEPS,), in_specs=[smem(), whole((ROWS...  19.6 us
    ppermute x1, waiting for transfers between devices, body(): halo_n = lax.ppermute(low_n, AXES, [(i + 1, i) for i in range(devices - 1)])  19.1 us
    pallas_call x1, Pallas kernels, second_source(): pl.pallas_call(second_kernel, grid=(ROWS // 2,), in_specs=[at(lambda i: j...  15.3 us
    pallas_call x2, Pallas kernels, outer_sweep(): pl.pallas_call(body, grid=(STEPS // 2,), in_specs=[smem(), whole((ROWS, L...  14.3 us
    ppermute x1, starting transfers between devices, body(): halo_n = lax.ppermute(low_n, AXES, [(i + 1, i) for i in range(devices - 1)])  3.75 us
    another operation x3, local copies, waits for them, and re-layouts, body(): jnp.stack([flux_weight, freq_damp, wind_growth])  2.1 us
    ppermute x1, starting transfers between devices, body(): lax.ppermute(high_s, AXES, [(i, i + 1) for i in range(devices - 1)])  2.09 us
  transfers between devices with their start and end apart: 2, of which 1 were waited for; matrix products, arithmetic and copies ran while one was open for 1% of the time, Pallas kernels for 38%

profile of v2, /device:TPU:6, one launch (start us, length us, event | category | flops | bytes accessed | tf_op | source)
XLA Modules:
  0.0 100.6 jit_solution(312801428468282546)
XLA Ops:
  0.6 0.7 stack.12
  1.3 0.7 stack.13
  2.0 0.7 stack.14
  2.7 0.6 pad_maximum_fusion.refs_7_.refs_9_
  3.4 9.0 %first_source_south.1 = (f32[1152,128]{1,0:T(8,128)}, f32[1152,128]{1,0:T(8,128)}, bf16[1152,128]{1,0:T(8,128)(2,1)}, bf16[4,592,256]{2,1,0:T(8,128)(2,1)}, bf16...) custom-call(bf16[10,1152,256]{2,1,0:T(8,128)(2,1)} %bitcast.3, s32[10,256]{1,0:T(8,128)} %land_ref.3, s32[10,256]{1,0:T(8,128)} %depth_ref.1, ...), custom_call_target="tpu_custom_call" | custom-call | tf_op jit(solution)/shard_map/first_source_south/pallas_call | solution.py:198
  12.4 3.8 %collective-permute-start = (bf16[4,592,256]{2,1,0:T(8,128)(2,1)}, bf16[4,592,256]{2,1,0:T(8,128)(2,1)S(1)}, u32[]{:S(2)}, u32[]{:S(2)}) collective-permute-start(bf16[4,592,256]{2,1,0:T(8,128)(2,1)} %get-tuple-element.20.low_n), channel_id=1, source_target_pairs={{1,0},{2,1},{3,2},{4,3},{5,4},{6,5},{7,6},{8,7},{9,8},{10,9},{11,1... | collective-permute-start | bytes 3637256 | tf_op jit(solution)/shard_map/ppermute | solution.py:484
  16.2 0.0 copy-start.2
  16.2 11.2 %first_source_north.1 = (bf16[4,592,256]{2,1,0:T(8,128)(2,1)}, bf16[6,576,256]{2,1,0:T(8,128)(2,1)}, bf16[2,576,256]{2,1,0:T(8,128)(2,1)}, f32[6,8,256]{2,1,0:T(8,128)}) custom-call(bf16[10,1152,256]{2,1,0:T(8,128)(2,1)} %bitcast.4, s32[10,256]{1,0:T(8,128)} %land_ref.3, s32[10,256]{1,0:T(8,128)} %depth_ref.1, f32[10,256]{1,0:T(8,128)} %damp_ref.1, ...), custom_call_target="tpu_custom_call" | custom-call | tf_op jit(solution)/shard_map/first_source_north/pallas_call | solution.py:198
  27.3 2.1 %collective-permute-start.1 = (bf16[4,592,256]{2,1,0:T(8,128)(2,1)}, bf16[4,592,256]{2,1,0:T(8,128)(2,1)S(1)}, u32[]{:S(2)}, u32[]{:S(2)}) collective-permute-start(bf16[4,592,256]{2,1,0:T(8,128)(2,1)} %get-tuple-element.27.high_s), channel_id=1, source_target_pairs={{0,1},{1,2},{2,3},{3,4},{4,5},{5,6},{6,7},{7,8},{8,9},{9,10},{10,1... | collective-permute-start | bytes 3637256 | tf_op jit(solution)/shard_map/ppermute | solution.py:486
  29.4 0.0 copy-done.2
  29.5 0.7 broadcast_in_dim.2.courant_ref.refs_3_
  30.1 19.6 %inner_sweep.1 = (bf16[6,576,256]{2,1,0:T(8,128)(2,1)}, f32[3,576,256]{2,1,0:T(8,128)}, bf16[6,576,256]{2,1,0:T(8,128)(2,1)}, f32[3,576,256]{2,1,0:T(8,128)}) custom-call(f32[2,36]{1,0:T(2,128)} %constant.5.clone.table_ref.refs_0_, s32[10,256]{1,0:T(8,128)} %land_ref.3, f32[10,256]{1,0:T(8,128)} %refs_2_.7, f32[32,128]{1,0:T(8,128)} %broadcast_in_dim.2.courant_ref.refs_3_, ...), custom_call_target="tpu_custom_call" | custom-call | tf_op jit(solution)/shard_map/inner_sweep/pallas_call | solution.py:307
  49.8 19.1 %collective-permute-done.refs_4_.refs_7_ = bf16[4,592,256]{2,1,0:T(8,128)(2,1)S(1)} collective-permute-done((bf16[4,592,256]{2,1,0:T(8,128)(2,1)}, bf16[4,592,256]{2,1,0:T(8,128)(2,1)S(1)}, u32[]{:S(2)}, u32[]{:S(2)}) %collective-permute-start) | collective-permute-done | bytes 1212448 | tf_op jit(solution)/shard_map/ppermute | solution.py:484
  68.9 0.0 copy-start.1
  68.9 1.0 %copy-done.1 = bf16[4,592,256]{2,1,0:T(8,128)(2,1)} copy-done((bf16[4,592,256]{2,1,0:T(8,128)(2,1)}, bf16[4,592,256]{2,1,0:T(8,128)(2,1)S(1)}, u32[]{:S(2)}) %copy-start.1) | copy-done | bytes 1212440
  69.9 7.1 %outer_sweep_north.1.out_n = bf16[4,576,256]{2,1,0:T(8,128)(2,1)} custom-call(f32[2,36]{1,0:T(2,128)} %constant.5.clone.table_ref.refs_0_, s32[10,256]{1,0:T(8,128)} %land_ref.3, f32[10,256]{1,0:T(8,128)} %refs_2_.7, f32[32,128]{1,0:T(8,128)} %broadcast_in_dim.2.courant_ref.refs_3_, bf16[4,592,256]{2,1,0:T(8,128)(2,1)} %copy-done.1, ...), custom_call_target="tpu_custom_call" | custom-call | flops 1321205760 | bytes 14745600 | tf_op jit(solution)/shard_map/outer_sweep_north/pallas_call | solution.py:365
  77.1 0.0 collective-permute-done.1.refs_4_.refs_7_
  77.1 0.0 copy-start
  77.1 1.0 %copy-done = bf16[4,592,256]{2,1,0:T(8,128)(2,1)} copy-done((bf16[4,592,256]{2,1,0:T(8,128)(2,1)}, bf16[4,592,256]{2,1,0:T(8,128)(2,1)S(1)}, u32[]{:S(2)}) %copy-start) | copy-done | bytes 1212440
  78.1 7.2 %outer_sweep_south.1.out_s = bf16[4,576,256]{2,1,0:T(8,128)(2,1)} custom-call(f32[2,36]{1,0:T(2,128)} %constant.5.clone.table_ref.refs_0_, s32[10,256]{1,0:T(8,128)} %land_ref.3, f32[10,256]{1,0:T(8,128)} %refs_2_.7, f32[32,128]{1,0:T(8,128)} %broadcast_in_dim.2.courant_ref.refs_3_, bf16[4,592,256]{2,1,0:T(8,128)(2,1)} %copy-done, ...), custom_call_target="tpu_custom_call" | custom-call | flops 1321205760 | bytes 14745600 | tf_op jit(solution)/shard_map/outer_sweep_south/pallas_call | solution.py:365
  85.3 15.3 %second_source.1 = (bf16[10,1152,256]{2,1,0:T(8,128)(2,1)}, f32[10,2,256]{2,1,0:T(2,128)}) custom-call(bf16[6,576,256]{2,1,0:T(8,128)(2,1)} %get-tuple-element.28.in_n, bf16[4,576,256]{2,1,0:T(8,128)(2,1)} %outer_sweep_north.1.out_n, bf16[6,576,256]{2,1,0:T(8,128)(2,1)} %get-tuple-element.32.in_s, bf16[4,576,256]{2,1,0:T(8,128)(2,1)} %outer_sweep_south.1.out_s, ...), custom_call_target="tpu_custom_call" | custom-call | flops 13589544960 | bytes 11796480 | tf_op jit(solution)/shard_map/second_source/pallas_call | solution.py:436
Async XLA Ops:
  12.4 56.5 %collective-permute-start = (bf16[4,592,256]{2,1,0:T(8,128)(2,1)}, bf16[4,592,256]{2,1,0:T(8,128)(2,1)S(1)}, u32[]{:S(2)}, u32[]{:S(2)}) collective-permute-start(bf16[4,592,256]{2,1,0:T(8,128)(2,1)} %get-tuple-element.20.low_n), channel_id=1, source_target_pairs={{1,0},{2,1},{3,2},{4,3},{5,4},{6,5},{7,6},{8,7},{9,8},{10,9},{11,1... | collective-permute-start | bytes 3637256 | tf_op jit(solution)/shard_map/ppermute | solution.py:484
  16.2 13.3 %copy-start.2 = (f32[32]{0:T(128)S(1)}, f32[32]{0:T(128)}, u32[]{:S(2)}) copy-start(f32[32]{0:T(128)} %param.24) | copy-start | bytes 388
  27.3 49.7 %collective-permute-start.1 = (bf16[4,592,256]{2,1,0:T(8,128)(2,1)}, bf16[4,592,256]{2,1,0:T(8,128)(2,1)S(1)}, u32[]{:S(2)}, u32[]{:S(2)}) collective-permute-start(bf16[4,592,256]{2,1,0:T(8,128)(2,1)} %get-tuple-element.27.high_s), channel_id=1, source_target_pairs={{0,1},{1,2},{2,3},{3,4},{4,5},{5,6},{6,7},{7,8},{8,9},{9,10},{10,1... | collective-permute-start | bytes 3637256 | tf_op jit(solution)/shard_map/ppermute | solution.py:486
  68.9 1.0 %copy-start.1 = (bf16[4,592,256]{2,1,0:T(8,128)(2,1)}, bf16[4,592,256]{2,1,0:T(8,128)(2,1)S(1)}, u32[]{:S(2)}) copy-start(bf16[4,592,256]{2,1,0:T(8,128)(2,1)S(1)} %collective-permute-done.refs_4_.refs_7_) | copy-start | bytes 3637252
  77.1 1.0 %copy-start = (bf16[4,592,256]{2,1,0:T(8,128)(2,1)}, bf16[4,592,256]{2,1,0:T(8,128)(2,1)S(1)}, u32[]{:S(2)}) copy-start(bf16[4,592,256]{2,1,0:T(8,128)(2,1)S(1)} %collective-permute-done.1.refs_4_.refs_7_) | copy-start | bytes 3637252

commit v3 on v0

v3 whole, which is shorter than its diff:
```python
import math

import jax
import jax.numpy as jnp
import numpy as np
from jax import lax
from jax.experimental import pallas as pl
from jax.experimental.pallas import tpu as pltpu
from jax.sharding import PartitionSpec as P

DIR = 36
FREQ = 32
NSUB = 4
NCLASS = 8
LON = 256
K = DIR * FREQ
HALF = K // 2
QUAD = K // 4
ROWS = 10
HALO = NSUB
TAIL = 16
AXES = ("pts", "grp")
VMEM = 28 * 1024 * 1024
OPENING_VMEM = 57 * 1024 * 1024
NEXT_VMEM = 54 * 1024 * 1024

ANGLES = 2.0 * math.pi * (np.arange(DIR) + 0.5) / DIR


def params(limit=VMEM):
    return pltpu.CompilerParams(vmem_limit_bytes=limit)


def held_whole():
    return pl.BlockSpec(memory_space=pltpu.VMEM)


def smem():
    return pl.BlockSpec(memory_space=pltpu.SMEM)


def cost(flops, read):
    return pl.CostEstimate(flops=int(flops), bytes_accessed=int(read), transcendentals=0)


def three_pieces(x):
    hi = x.astype(jnp.bfloat16).astype(jnp.float32)
    mid = (x - hi).astype(jnp.bfloat16).astype(jnp.float32)
    return hi, mid, x - hi - mid


def stack_pieces(pieces):
    which = lax.broadcasted_iota(jnp.int32, (8, LON), 0)
    rows = jnp.zeros((8, LON), jnp.float32)
    for at, piece in enumerate(pieces):
        rows = jnp.where(which == at, jnp.broadcast_to(piece, (8, LON)), rows)
    return jnp.concatenate([rows, jnp.zeros((8, LON), jnp.float32)], axis=0).astype(jnp.bfloat16)


def contract(matrix, spectrum):
    return lax.dot_general(matrix, spectrum, (((0,), (0,)), ((), ())), preferred_element_type=jnp.float32)


def column(vector):
    return jnp.broadcast_to(vector[None, :], (128, K)).T


def point_fields(land_ref, depth_ref, outlets_ref, scale_ref, sea, count, rate):
    sea[...] = land_ref[...].astype(jnp.float32)
    depth = depth_ref[...]
    total = jnp.zeros((ROWS, LON), jnp.float32)
    for c in range(NCLASS):
        total = jnp.where(depth == c, scale_ref[c], total)
    rate[...] = total
    shape = (ROWS, LON)
    flat = lax.broadcasted_iota(jnp.int32, shape, 0) * LON + lax.broadcasted_iota(jnp.int32, shape, 1)
    flat = flat + lax.axis_index(AXES) * (ROWS * LON)
    hits = jnp.zeros(shape, jnp.float32)
    for n in range(outlets_ref.shape[0]):
        hits = hits + jnp.where(flat == outlets_ref[n], 1.0, 0.0)
    count[...] = hits


def first_kernel(pair, opening, x_ref, land_ref, depth_ref, damp_ref, clear_ref, outlets_ref, scale_ref, *rest):
    tables = 4 if opening else 3
    if pair < 2:
        far = [x_ref.at[2 * pair : 2 * pair + 2], rest[tables], land_ref, depth_ref, damp_ref, clear_ref, outlets_ref,
               scale_ref, *rest[:tables]]
        near, sems = rest[-len(far) - 1 : -1], rest[-1]
        rest = rest[: -len(far) - 1]
        copies = [pltpu.make_async_copy(a, b, sems.at[i]) for i, (a, b) in enumerate(zip(far, near))]
        x_ref, jac_ref, land_ref, depth_ref, damp_ref, clear_ref, outlets_ref, scale_ref = near[:8]
        rest = near[8:] + (jac_ref,) + rest[tables + 1 :]
    else:
        near, sems = rest[-2], rest[-1]
        rest = rest[:-2]
        copies = [pltpu.make_async_copy(x_ref.at[2 * pair : 2 * pair + 2], near, sems.at[0])]
        x_ref = near
    for copy in copies:
        copy.start()
    for copy in copies[2:]:
        copy.wait()
    sea, count, rate, held = rest[-4:]
    rest = rest[:-4]
    if opening:
        weight_ref, freq_ref, growth_ref, compass_ref, _, fw_ref, fd_ref, wave_ref = rest[:8]
        fw_ref[...] = column(weight_ref[...])
        fd_ref[...] = column(freq_ref[...])
        hi, mid, low = three_pieces(column(growth_ref[...]) * compass_ref[...])
        lane = lax.broadcasted_iota(jnp.int32, (K, 128), 1)
        wave_ref[...] = jnp.where(lane < 8, hi, jnp.where(lane < 16, mid, low)).astype(jnp.bfloat16)
        outs = rest[8:]
    else:
        fw_ref, fd_ref, wave_ref, jac_ref = rest[:4]
        outs = rest[4:]
    halves, wind_ref = outs[:2], outs[2]
    point_fields(land_ref, depth_ref, outlets_ref, scale_ref, sea, count, rate)
    for copy in copies[:2]:
        copy.wait()

    fw = fw_ref[...]
    fw = jnp.concatenate([fw, fw], axis=1)
    seeds = []
    fields = []
    for e in range(2):
        r = slice(2 * pair + e, 2 * pair + e + 1)
        lone = sea[r, :] * (x_ref[e].astype(jnp.float32) + fw * count[r, :])
        seeds.append(lone.astype(jnp.bfloat16))
        fields.append((rate[r, :], damp_ref[r, :]))
    spectrum = jnp.concatenate(seeds, axis=1)
    for m in range(3):
        rows = slice(m * 384, (m + 1) * 384)
        mixed = contract(jac_ref[:, rows], spectrum)
        fd = fd_ref[rows, :]
        for piece in range(4):
            e, side = divmod(piece, 2)
            lanes = slice(side * 128, (side + 1) * 128)
            at = slice(piece * 128, (piece + 1) * 128)
            v = seeds[e][rows, lanes].astype(jnp.float32)
            held[piece, rows, :] = (
                v + fields[e][0][:, lanes] * mixed[:, at] - (fields[e][1][:, lanes] * fd) * v
            )
    wind = contract(wave_ref[...], spectrum)
    wind = wind[0:8] + wind[8:16] + wind[16:24]
    for e in range(2):
        wind_ref[e] = wind[:, e * LON : (e + 1) * LON]
    for half in range(2):
        for d in range(18):
            for piece in range(4):
                e, side = divmod(piece, 2)
                halves[half][e, d * FREQ : (d + 1) * FREQ, side * 128 : (side + 1) * 128] = held[
                    piece, pl.ds(half * 18 + d, FREQ, stride=DIR), :
                ].astype(jnp.bfloat16)
    if pair != 2:
        for e in range(2):
            r = slice(2 * pair + e, 2 * pair + e + 1)
            pieces = three_pieces(sea[r, :] * clear_ref[r, :])
            halves[0 if pair < 2 else 1][e, HALF : HALF + TAIL, :] = stack_pieces(pieces)


def first_source(pair, opening, x, land, depth, damping, clear, outlets, scale, comps, jacobian):
    sizes = (HALF + TAIL if pair < 2 else HALF, HALF + TAIL if pair > 2 else HALF)
    out_shape = [jax.ShapeDtypeStruct((2, size, LON), jnp.bfloat16) for size in sizes]
    out_shape.append(jax.ShapeDtypeStruct((2, 8, LON), jnp.float32))
    if opening:
        tables = [jax.ShapeDtypeStruct((K, 128), dtype) for dtype in (jnp.float32, jnp.float32, jnp.bfloat16)]
        out_shape = tables + out_shape
    scratch = [pltpu.VMEM((ROWS, LON), jnp.float32)] * 3 + [pltpu.VMEM((4, K, 128), jnp.float32)]
    scratch.append(pltpu.VMEM((2, K, LON), jnp.bfloat16))
    if pair < 2:
        scratch.append(pltpu.VMEM((K, K), jnp.bfloat16))
        scratch += [pltpu.VMEM(a.shape, a.dtype) for a in (land, depth, damping, clear)]
        scratch += [pltpu.SMEM(a.shape, a.dtype) for a in (outlets, scale)]
        scratch += [pltpu.VMEM(a.shape, a.dtype) for a in comps]
    scratch.append(pltpu.SemaphoreType.DMA((12,)))
    anywhere = pl.BlockSpec(memory_space=pl.ANY)
    place = anywhere if pair < 2 else held_whole()

    def body(*refs):
        first_kernel(pair, opening, *refs)

    return pl.pallas_call(
        body,
        grid=(1,),
        in_specs=[anywhere] + [place] * 4 + [place if pair < 2 else smem()] * 2 + [place] * (len(comps) + 1),
        out_specs=[held_whole()] * len(out_shape),
        out_shape=out_shape,
        scratch_shapes=scratch,
        compiler_params=params((OPENING_VMEM, NEXT_VMEM, VMEM, VMEM, VMEM)[pair]),
        cost_estimate=cost(2 * K * K * LON * 2, 4 * K * LON * 2),
        name=f"first_source_{pair}",
    )(x, land, depth, damping, clear, outlets, scale, *comps, jacobian)


def sweep_rows(north, table_ref, courant_ref, pass_rows, emit):
    halves = (slice(0, 128), slice(128, 256))
    lane = lax.broadcasted_iota(jnp.int32, (16, 128), 1)
    for quad in (0, 1) if north else (2, 3):
        east = quad in (0, 3)
        last = lane == 127 if east else lane == 0
        shift = 127 if east else 1
        order = halves if east else halves[::-1]

        def chunk(i, carry, quad=quad, last=last, shift=shift, order=order):
            d = quad * (QUAD // FREQ) + i // 2
            rows = pl.ds(pl.multiple_of((quad % 2) * QUAD + i * 16, 16), 16)
            speed = courant_ref[pl.ds(pl.multiple_of((i % 2) * 16, 16), 16), :]
            across = speed * table_ref[0, d]
            upward = speed * table_ref[1, d]
            centre = 1.0 - across - upward
            upward = upward / centre
            across = across / centre
            walled = jnp.where(last, 0.0, across)
            square = centre * centre

            def advance(v, first):
                turned = [
                    [pltpu.roll(value.astype(jnp.bfloat16), shift, 1).astype(jnp.float32) for value in half[:-1]]
                    for half in v
                ]
                fresh = [[], []]
                for t in range(len(v[0]) - 1):
                    beside = (jnp.where(last, turned[1][t], turned[0][t]), turned[1][t])
                    for half, weight in ((0, across), (1, walled)):
                        fresh[half].append(
                            pass_rows[first + t, :, order[half]]
                            * (v[half][t] + weight * beside[half] + upward * v[half][t + 1])
                        )
                return fresh

            emit(rows, order, advance, square * square)
            return carry

        lax.fori_loop(0, QUAD // 16, chunk, 0, unroll=3)


def own_passage(land_ref, clear_ref, pass_rows, north):
    passage = land_ref[...].astype(jnp.float32) * clear_ref[...]
    for t in range(ROWS):
        own = t if north else ROWS - 1 - t
        pass_rows[t] = jnp.broadcast_to(passage[own : own + 1, :], (16, LON))


def row_of(sources, r, *rest):
    for source in sources:
        if r < source.shape[0]:
            return source[(r, *rest)].astype(jnp.float32)
        r -= source.shape[0]


def inner_kernel(north, table_ref, land_ref, clear_ref, courant_ref, *rest):
    sources, (done, state, pass_rows) = rest[:-3], rest[-3:]
    own_passage(land_ref, clear_ref, pass_rows, north)

    def emit(rows, order, advance, scale):
        v = [[row_of(sources, t if north else ROWS - 1 - t, rows, lanes) for t in range(ROWS)] for lanes in order]
        for s in range(NSUB):
            v = advance(v, 0)
            if s < NSUB - 1:
                for half in range(2):
                    state[s, rows, order[half]] = v[half][-1]
        for half in range(2):
            for t in range(ROWS - NSUB):
                done[t if north else ROWS - NSUB - 1 - t, rows, order[half]] = (scale * v[half][t]).astype(jnp.bfloat16)

    sweep_rows(north, table_ref, courant_ref, pass_rows, emit)


def inner_sweep(north, table, land, clear, courant, sources):
    def body(*refs):
        inner_kernel(north, *refs)

    return pl.pallas_call(
        body,
        in_specs=[smem()] + [held_whole()] * (3 + len(sources)),
        out_specs=[held_whole()] * 2,
        out_shape=[
            jax.ShapeDtypeStruct((6, HALF, LON), jnp.bfloat16),
            jax.ShapeDtypeStruct((3, HALF, LON), jnp.float32),
        ],
        scratch_shapes=[pltpu.VMEM((ROWS, 16, LON), jnp.float32)],
        compiler_params=params(),
        cost_estimate=cost(30 * 7 * K * LON * 40, 60 * K * LON),
        name="inner_sweep_north" if north else "inner_sweep_south",
    )(table, land, clear, courant, *sources)


def outer_kernel(north, begin, count, messages, table_ref, land_ref, clear_ref, courant_ref, first, state, *rest):
    halo, done, pass_rows = rest[:messages], rest[messages], rest[-1]
    state_out = rest[messages + 1] if begin + count < HALO else None

    def halo_row(t, rows, lanes=slice(None)):
        return halo[t // 2][t % 2 if north else 1 - t % 2, rows, lanes].astype(jnp.float32)

    own_passage(land_ref, clear_ref, pass_rows, north)
    for t in range(begin + count):
        pieces = halo_row(t, slice(HALF, HALF + TAIL))
        pass_rows[ROWS + t] = jnp.broadcast_to(pieces[0:1] + pieces[1:2] + pieces[2:3], (16, LON))

    def emit(rows, order, advance, scale):
        v = []
        for lanes in order:
            if begin == 0:
                before = first[1 if north else 0, rows, lanes].astype(jnp.float32)
            else:
                before = halo_row(begin - 1, rows, lanes)
            v.append([before] + [halo_row(begin + t, rows, lanes) for t in range(count)])
        for s in range(NSUB):
            v = advance(v, ROWS - 1 + begin - s)
            if s < NSUB - 1:
                if state_out is not None:
                    for half in range(2):
                        state_out[s, rows, order[half]] = v[half][-1]
                v = [[state[s, rows, lanes]] + half for lanes, half in zip(order, v)]
        for half in range(2):
            for t in range(count):
                done[t if north else count - 1 - t, rows, order[half]] = (scale * v[half][t]).astype(jnp.bfloat16)

    sweep_rows(north, table_ref, courant_ref, pass_rows, emit)


def outer_sweep(north, begin, count, table, land, clear, courant, first, state, halos):
    def body(*refs):
        outer_kernel(north, begin, count, len(halos), *refs)

    out_shape = [jax.ShapeDtypeStruct((count, HALF, LON), jnp.bfloat16)]
    if begin + count < HALO:
        out_shape.append(jax.ShapeDtypeStruct((3, HALF, LON), jnp.float32))
    return pl.pallas_call(
        body,
        in_specs=[smem()] + [held_whole()] * (5 + len(halos)),
        out_specs=[held_whole()] * len(out_shape),
        out_shape=out_shape,
        scratch_shapes=[pltpu.VMEM((ROWS + HALO, 16, LON), jnp.float32)],
        compiler_params=params(),
        cost_estimate=cost(count * 4 * 7 * K * LON * 40, 50 * K * LON),
        name=f"outer_sweep_{'north' if north else 'south'}_{begin}",
    )(table, land, clear, courant, first, state, *halos)


def second_kernel(pair, at_n, at_s, n_ref, s_ref, *refs):
    depth_ref, damp_ref, scale_ref, fd_ref, jac_ref, wave_ref, wind_in = refs[:7]
    out_ref, wind_ref, held = refs[-3:]
    here = slice(2 * pair, 2 * pair + 2)
    depth = depth_ref[here, :]
    rate = jnp.zeros((2, LON), jnp.float32)
    for c in range(NCLASS):
        rate = jnp.where(depth == c, scale_ref[c], rate)
    damp = damp_ref[here, :]
    for half, ref, at in ((0, n_ref, at_n), (1, s_ref, at_s)):
        for d in range(18):
            for piece in range(4):
                e, side = divmod(piece, 2)
                held[piece, pl.ds(half * 18 + d, FREQ, stride=DIR), :] = ref[
                    at + e, d * FREQ : (d + 1) * FREQ, side * 128 : (side + 1) * 128
                ].astype(jnp.float32)
    spectrum = jnp.concatenate([held[piece].astype(jnp.bfloat16) for piece in range(4)], axis=1)
    for m in range(3):
        rows = slice(m * 384, (m + 1) * 384)
        mixed = contract(jac_ref[:, rows], spectrum)
        fd = fd_ref[rows, :]
        for piece in range(4):
            e, side = divmod(piece, 2)
            lanes = slice(side * 128, (side + 1) * 128)
            at = slice(piece * 128, (piece + 1) * 128)
            v = held[piece, rows, :]
            out_ref[e, rows, lanes] = (
                v + rate[e : e + 1, lanes] * mixed[:, at] - (damp[e : e + 1, lanes] * fd) * v
            ).astype(jnp.bfloat16)
    wind = contract(wave_ref[...], spectrum)
    wind = wind[0:8] + wind[8:16] + wind[16:24]
    for e in range(2):
        wind_ref[e] = (wind_in[e] + wind[:, e * LON : (e + 1) * LON])[:2]


def second_source(pair, north, at_n, south, at_s, before, depth, damping, scale, fd, jac, wave, wind):
    def body(*refs):
        second_kernel(pair, at_n, at_s, *refs)

    return pl.pallas_call(
        body,
        grid=(1,),
        in_specs=[held_whole()] * 4
        + [smem()]
        + [held_whole()] * 4
        + [pl.BlockSpec(memory_space=pl.ANY)] * len(before),
        out_specs=[pl.BlockSpec((2, K, LON), lambda i: (pair, 0, 0)), pl.BlockSpec((2, 2, LON), lambda i: (pair, 0, 0))],
        out_shape=[
            jax.ShapeDtypeStruct((ROWS, K, LON), jnp.bfloat16),
            jax.ShapeDtypeStruct((ROWS, 2, LON), jnp.float32),
        ],
        input_output_aliases={9: 0, 10: 1} if before else {},
        scratch_shapes=[pltpu.VMEM((4, K, 128), jnp.float32)],
        compiler_params=params(),
        cost_estimate=cost(2 * K * K * LON * 2, 4 * K * LON * 2),
        name=f"second_source_{pair}",
    )(north, south, depth, damping, scale, fd, jac, wave, wind, *before)


def body(
    adjoint_in,
    land_sea,
    depth_class,
    damping,
    transparency,
    outlets,
    flux_weight,
    jacobian,
    source_scale,
    freq_damp,
    courant,
    wind_growth,
):
    devices = lax.axis_size(AXES)
    x = adjoint_in.transpose(1, 0, 2)
    compass = np.zeros((K, 128), np.float32)
    for at in range(3):
        compass[:, 8 * at] = np.tile(np.cos(ANGLES), FREQ)
        compass[:, 8 * at + 1] = np.tile(np.sin(ANGLES), FREQ)
    comps = (flux_weight, freq_damp, wind_growth, jnp.asarray(compass))
    common = (x, land_sea, depth_class, damping, transparency, outlets, source_scale)
    down = [(i + 1, i) for i in range(devices - 1)]
    up = [(i, i + 1) for i in range(devices - 1)]
    speed = jnp.broadcast_to(courant[:, None], (FREQ, 128))
    table = jnp.asarray(np.abs(np.stack([np.cos(ANGLES), np.sin(ANGLES)])), jnp.float32)
    local = (table, land_sea, transparency, speed)
    n, s, winds, halo_n, halo_s = {}, {}, {}, {}, {}

    fw, fd, wave, n[0], s[0], winds[0] = first_source(0, True, *common, comps, jacobian)
    halo_n[0] = lax.ppermute(n[0], AXES, down)
    comps = (fw, fd, wave)
    for pair in (1, 4, 3, 2):
        n[pair], s[pair], winds[pair] = first_source(pair, False, *common, comps, jacobian)
    halo_n[1] = lax.ppermute(n[1], AXES, down)
    in_n, state_n = inner_sweep(True, *local, [n[pair] for pair in range(5)])
    in_s, state_s = inner_sweep(False, *local, [s[pair] for pair in range(5)])
    s[4], state_s = lax.optimization_barrier((s[4], state_s))
    halo_s[0] = lax.ppermute(s[4], AXES, up)
    last = (depth_class, damping, source_scale, fd, jacobian, wave)
    part = second_source(2, in_n, 4, in_s, 0, (), *last, winds[2])
    (edge,) = outer_sweep(True, 0, HALO, *local, n[4], state_n, (halo_n[0], halo_n[1]))
    s[3], edge = lax.optimization_barrier((s[3], edge))
    halo_s[1] = lax.ppermute(s[3], AXES, up)
    part = second_source(3, edge, 0, in_s, 2, part, *last, winds[3])
    part = second_source(4, edge, 2, in_s, 4, part, *last, winds[4])
    state_s, *part = lax.optimization_barrier((state_s, *part))
    edge, state_s = outer_sweep(False, 0, 2, *local, s[0], state_s, (halo_s[0],))
    part = second_source(1, in_n, 2, edge, 0, part, *last, winds[1])
    state_s, *part = lax.optimization_barrier((state_s, *part))
    (edge,) = outer_sweep(False, 2, 2, *local, s[0], state_s, (halo_s[0], halo_s[1]))
    out, wind_out = second_source(0, in_n, 0, edge, 0, part, *last, winds[0])
    return out.transpose(1, 0, 2), wind_out.transpose(1, 0, 2)


def solution(mesh):
    rows = P(AXES, None)
    placed = (P(None, AXES, None), rows, rows, rows, rows, P(), P(), P(), P(), P(), P(), P())
    return jax.shard_map(
        body,
        mesh=mesh,
        in_specs=placed,
        out_specs=(P(None, AXES, None), P(None, AXES, None)),
        check_vma=False,
    )
```

time: 828 us -> 81.7 us (0.10); the launches traced: 816 us -> 81.4 us
  waiting for transfers between devices: 486 us -> 1.47 us
  other arithmetic: 129 us -> 0 us
  local copies, waits for them, and re-layouts: 127 us -> 0.17 us
  Pallas kernels: 0 us -> 64.2 us
  matrix products: 38.7 us -> 0 us
  between operations: 14.5 us -> 1.03 us
    all_gather x1 -> x0, waiting for transfers between devices: 364 us -> none  [body(): lax.all_gather(passage_local, ('pts', 'grp'), axis=0, tiled=True)]
    all_to_all x2 -> x0, waiting for transfers between devices: 121 us -> none  [the longest x1 121 us: body(): lax.all_to_all(propagated, ('pts', 'grp'), split_axis=1, concat_axis=0, t...]
    mul x4 -> x0, other arithmetic: 76.3 us -> none  [the longest x3 76.3 us: propagate(): passage * (centre_keep * spectrum + eastward * padded[:, 1:-1, 2:] + west...]
    convert_element_type x5 -> x0, local copies, waits for them, and re-layouts: 70.8 us -> none  [the longest x3 51.4 us: body(): arrived.astype(jnp.float32)]
    pallas_call x0 -> x15, Pallas kernels: none -> 64.2 us  [the longest x5 22.4 us: first_source(): pl.pallas_call(body, grid=(1,), in_specs=[anywhere] + [place] * 4 + [plac...]
    convert_element_type x4 -> x0, other arithmetic: 51.2 us -> none  [the longest x1 34.8 us: body(): propagate(arrived.astype(jnp.float32), local_weights, coastline)]
    dot_general x4 -> x0, matrix products: 38.7 us -> none  [the longest x2 25.7 us: source_adjoint(): lax.dot_general(jacobian, spectrum, (((0,), (0,)), ((), ())), preferred_e...]
    unnamed x25 -> x38, local copies, waits for them, and re-layouts: 21.6 us -> 0.1 us
  transfers between devices with their start and end apart: 3 -> 4, of which waited for: 2 -> 1; matrix products, arithmetic and copies ran while one was open for 1% -> 0% of each run, Pallas kernels for 0% -> 63%
where the time goes in v3:
time: 81.7 us; the launch traced here: 81.4 us
  Pallas kernels  64.2 us (79%)
  starting transfers between devices  14.5 us (18%)
  waiting for transfers between devices  1.47 us (2%)
  between operations  1.03 us (1%)
    pallas_call x5, Pallas kernels, first_source(): pl.pallas_call(body, grid=(1,), in_specs=[anywhere] + [place] * 4 + [plac...  22.4 us
    pallas_call x5, Pallas kernels, second_source(): pl.pallas_call(body, grid=(1,), in_specs=[held_whole()] * 4 + [smem()] +...  17.1 us
    pallas_call x2, Pallas kernels, inner_sweep(): pl.pallas_call(body, in_specs=[smem()] + [held_whole()] * (3 + len(source...  13.5 us
    pallas_call x3, Pallas kernels, outer_sweep(): pl.pallas_call(body, in_specs=[smem()] + [held_whole()] * (5 + len(halos)...  11.1 us
    ppermute x1, starting transfers between devices, body(): halo_n[0] = lax.ppermute(n[0], AXES, down)  6.4 us
    ppermute x1, starting transfers between devices, body(): halo_s[0] = lax.ppermute(s[4], AXES, up)  3.46 us
    ppermute x1, starting transfers between devices, body(): halo_n[1] = lax.ppermute(n[1], AXES, down)  2.55 us
    ppermute x1, starting transfers between devices, body(): halo_s[1] = lax.ppermute(s[3], AXES, up)  2.14 us
  transfers between devices with their start and end apart: 4, of which 1 were waited for; matrix products, arithmetic and copies ran while one was open for 0% of the time, Pallas kernels for 63%

profile of v3, /device:TPU:96, one launch (start us, length us, event | category | flops | bytes accessed | tf_op | source)
XLA Modules:
  0.0 81.4 jit_solution(6471297802209111860)
XLA Ops:
  0.6 6.3 %first_source_0.1 = (f32[1152,128]{1,0:T(8,128)}, f32[1152,128]{1,0:T(8,128)}, bf16[1152,128]{1,0:T(8,128)(2,1)}, bf16[2,592,256]{2,1,0:T(8,128)(2,1)}, bf16[2,5...) custom-call(bf16[10,1152,256]{2,1,0:T(8,128)(2,1)} %bitcast.3, s32[10,256]{1,0:T(8,128)} %refs_1_.19, s32[10,256]{1,0:T(8,128)} %refs_2_.29, ...), custom_call_target="tpu_custom_call" | custom-call | flops 1358954496 | bytes 2359296 | tf_op jit(solution)/shard_map/first_source_0/pallas_call | solution.py:182
  7.0 6.4 %collective-permute-start = (bf16[2,592,256]{2,1,0:T(8,128)(2,1)}, bf16[2,592,256]{2,1,0:T(8,128)(2,1)}, u32[]{:S(2)}, u32[]{:S(2)}) collective-permute-start(bf16[2,592,256]{2,1,0:T(8,128)(2,1)} %get-tuple-element.46.refs_4_), channel_id=1, source_target_pairs={{1,0},{2,1},{3,2},{4,3},{5,4},{6,5},{7,6},{8,7},{9,8},{10,9},{11,1... | collective-permute-start | bytes 1818632 | tf_op jit(solution)/shard_map/ppermute | solution.py:430
  13.4 0.0 copy-start
  13.4 0.0 copy-start.1
  13.4 0.0 copy-start.6
  13.4 0.0 copy-start.7
  13.5 0.0 copy-start.8
  13.5 0.0 copy-start.9
  13.5 0.0 copy-start.10
  13.5 0.0 copy-start.13
  13.5 6.1 %first_source_1.1 = (bf16[2,592,256]{2,1,0:T(8,128)(2,1)}, bf16[2,576,256]{2,1,0:T(8,128)(2,1)}, f32[2,8,256]{2,1,0:T(8,128)}) custom-call(bf16[10,1152,256]{2,1,0:T(8,128)(2,1)} %bitcast.4, s32[10,256]{1,0:T(8,128)} %refs_1_.19, s32[10,256]{1,0:T(8,128)} %refs_2_.29, f32[10,256]{1,0:T(8,128)} %refs_3_.19, f32[10,256]{1,0:T(8,128)} %refs_2_.28, s32[64]{0:T(128)} %refs_5_.9, ...), custom_call_target="tpu_custom_call" | custom-call | flops 1358954496 | bytes 2359296 | tf_op jit(solution)/shard_map/first_source_1/pallas_call | solution.py:182
  19.6 2.6 %collective-permute-start.1 = (bf16[2,592,256]{2,1,0:T(8,128)(2,1)}, bf16[2,592,256]{2,1,0:T(8,128)(2,1)S(1)}, u32[]{:S(2)}, u32[]{:S(2)}) collective-permute-start(bf16[2,592,256]{2,1,0:T(8,128)(2,1)} %get-tuple-element.50.refs_5_), channel_id=1, source_target_pairs={{1,0},{2,1},{3,2},{4,3},{5,4},{6,5},{7,6},{8,7},{9,8},{10,9},{11,1... | collective-permute-start | bytes 1818632 | tf_op jit(solution)/shard_map/ppermute | solution.py:434
  22.3 3.3 %first_source_2.1 = (bf16[2,576,256]{2,1,0:T(8,128)(2,1)S(1)}, bf16[2,576,256]{2,1,0:T(8,128)(2,1)S(1)}, f32[2,8,256]{2,1,0:T(8,128)S(1)}) custom-call(bf16[10,1152,256]{2,1,0:T(8,128)(2,1)S(1)} %bitcast.5, s32[10,256]{1,0:T(8,128)S(1)} %copy-done.8, s32[10,256]{1,0:T(8,128)S(1)} %copy-done.6, f32[10,256]{1,0:T(8,128)S(1)} %copy-done.7, ...), custom_call_target="tpu_custom_call" | custom-call | flops 1358954496 | bytes 2359296 | tf_op jit(solution)/shard_map/first_source_2/pallas_call | solution.py:182
  25.7 3.3 %first_source_4.1 = (bf16[2,576,256]{2,1,0:T(8,128)(2,1)S(1)}, bf16[2,592,256]{2,1,0:T(8,128)(2,1)S(1)}, f32[2,8,256]{2,1,0:T(8,128)S(1)}) custom-call(bf16[10,1152,256]{2,1,0:T(8,128)(2,1)S(1)} %bitcast.6, s32[10,256]{1,0:T(8,128)S(1)} %copy-done.8, s32[10,256]{1,0:T(8,128)S(1)} %copy-done.6, f32[10,256]{1,0:T(8,128)S(1)} %copy-done.7, ...), custom_call_target="tpu_custom_call" | custom-call | flops 1358954496 | bytes 2359296 | tf_op jit(solution)/shard_map/first_source_4/pallas_call | solution.py:182
  29.0 0.0 copy-start.18
  29.0 0.0 copy-start.14
  29.0 3.3 %first_source_3.1 = (bf16[2,576,256]{2,1,0:T(8,128)(2,1)S(1)}, bf16[2,592,256]{2,1,0:T(8,128)(2,1)S(1)}, f32[2,8,256]{2,1,0:T(8,128)S(1)}) custom-call(bf16[10,1152,256]{2,1,0:T(8,128)(2,1)S(1)} %bitcast.7, s32[10,256]{1,0:T(8,128)S(1)} %copy-done.8, s32[10,256]{1,0:T(8,128)S(1)} %copy-done.6, f32[10,256]{1,0:T(8,128)S(1)} %copy-done.7, ...), custom_call_target="tpu_custom_call" | custom-call | flops 1358954496 | bytes 2359296 | tf_op jit(solution)/shard_map/first_source_3/pallas_call | solution.py:182
  32.4 0.1 broadcast_in_dim.2.refs_3_
  32.5 0.0 copy-start.15
  32.5 6.7 %inner_sweep_south.1 = (bf16[6,576,256]{2,1,0:T(8,128)(2,1)S(1)}, f32[3,576,256]{2,1,0:T(8,128)S(1)}) custom-call(f32[2,36]{1,0:T(2,128)S(1)} %copy-done.14, s32[10,256]{1,0:T(8,128)S(1)} %copy-done.8, f32[10,256]{1,0:T(8,128)S(1)} %copy-done.9, f32[32,128]{1,0:T(8,128)S(1)} %broadcast_in_dim.2.refs_3_, bf16[2,576,256]{2,1,0:T(8,128)(2,1)S(1)} %copy-done.5, ...), custom_call_target="tpu_custom_call" | custom-call | flops 2477260800 | bytes 17694720 | tf_op jit(solution)/shard_map/inner_sweep_south/pallas_call | solution.py:273
  39.2 3.5 %collective-permute-start.2 = (bf16[2,592,256]{2,1,0:T(8,128)(2,1)S(1)}, bf16[2,592,256]{2,1,0:T(8,128)(2,1)S(1)}, u32[]{:S(2)}, u32[]{:S(2)}) collective-permute-start(bf16[2,592,256]{2,1,0:T(8,128)(2,1)S(1)} %get-tuple-element.75.refs_8_), channel_id=1, source_target_pairs={{0,1},{1,2},{2,3},{3,4},{4,5},{5,6},{6,7},{7,8},{8,9},{9,10},{10,1... | collective-permute-start | bytes 1818632 | tf_op jit(solution)/shard_map/ppermute | solution.py:438
  42.7 6.7 %inner_sweep_north.1 = (bf16[6,576,256]{2,1,0:T(8,128)(2,1)S(1)}, f32[3,576,256]{2,1,0:T(8,128)S(1)}) custom-call(f32[2,36]{1,0:T(2,128)S(1)} %copy-done.14, s32[10,256]{1,0:T(8,128)S(1)} %copy-done.8, f32[10,256]{1,0:T(8,128)S(1)} %copy-done.9, f32[32,128]{1,0:T(8,128)S(1)} %broadcast_in_dim.2.refs_3_, bf16[2,592,256]{2,1,0:T(8,128)(2,1)S(1)} %copy-done.15, ...), custom_call_target="tpu_custom_call" | custom-call | flops 2477260800 | bytes 17694720 | tf_op jit(solution)/shard_map/inner_sweep_north/pallas_call | solution.py:273
  49.5 5.3 %outer_sweep_north_0.1.refs_0_ = bf16[4,576,256]{2,1,0:T(8,128)(2,1)S(1)} custom-call(f32[2,36]{1,0:T(2,128)S(1)} %copy-done.14, s32[10,256]{1,0:T(8,128)S(1)} %copy-done.8, f32[10,256]{1,0:T(8,128)S(1)} %copy-done.9, f32[32,128]{1,0:T(8,128)S(1)} %broadcast_in_dim.2.refs_3_, bf16[2,576,256]{2,1,0:T(8,128)(2,1)S(1)} %get-tuple-element.53.refs_8_.refs_4_, ...), custom_call_target="tpu_custom_call" | custom-call | flops 1321205760 | bytes 14745600 | tf_op jit(solution)/shard_map/outer_sweep_north_0/pallas_call | solution.py:329
  54.8 2.1 %collective-permute-start.3 = (bf16[2,592,256]{2,1,0:T(8,128)(2,1)S(1)}, bf16[2,592,256]{2,1,0:T(8,128)(2,1)S(1)}, u32[]{:S(2)}, u32[]{:S(2)}) collective-permute-start(bf16[2,592,256]{2,1,0:T(8,128)(2,1)S(1)} %get-tuple-element.84.refs_7_), channel_id=1, source_target_pairs={{0,1},{1,2},{2,3},{3,4},{4,5},{5,6},{6,7},{7,8},{8,9},{9,10},{10,1... | collective-permute-start | bytes 1818632 | tf_op jit(solution)/shard_map/ppermute | solution.py:443
  56.9 3.4 %second_source_2.1 = (bf16[10,1152,256]{2,1,0:T(8,128)(2,1)}, f32[10,2,256]{2,1,0:T(2,128)}) custom-call(bf16[6,576,256]{2,1,0:T(8,128)(2,1)S(1)} %get-tuple-element.54.refs_0_, bf16[6,576,256]{2,1,0:T(8,128)(2,1)S(1)} %get-tuple-element.64.refs_1_, s32[10,256]{1,0:T(8,128)S(1)} %copy-done.6, f32[10,256]{1,0:T(8,128)S(1)} %copy-done.7, f32[8]{0:T(128)S(1)} %copy-done.10, ...), custom_call_target="tpu_custom_call" | custom-call | flops 1358954496 | bytes 2359296 | tf_op jit(solution)/shard_map/second_source_2/pallas_call | solution.py:380
  60.3 3.4 %second_source_3.1 = (bf16[10,1152,256]{2,1,0:T(8,128)(2,1)}, f32[10,2,256]{2,1,0:T(2,128)}) custom-call(bf16[4,576,256]{2,1,0:T(8,128)(2,1)S(1)} %outer_sweep_north_0.1.refs_0_, bf16[6,576,256]{2,1,0:T(8,128)(2,1)S(1)} %get-tuple-element.64.refs_1_, s32[10,256]{1,0:T(8,128)S(1)} %copy-done.6, ...), custom_call_target="tpu_custom_call", output_to_operand_aliasing={{0}: (9, {}), {1}: (10, {})} | custom-call | flops 1358954496 | bytes 2359296 | tf_op jit(solution)/shard_map/second_source_3/pallas_call | solution.py:380
  63.8 3.4 %second_source_4.1 = (bf16[10,1152,256]{2,1,0:T(8,128)(2,1)}, f32[10,2,256]{2,1,0:T(2,128)}) custom-call(bf16[4,576,256]{2,1,0:T(8,128)(2,1)S(1)} %outer_sweep_north_0.1.refs_0_, bf16[6,576,256]{2,1,0:T(8,128)(2,1)S(1)} %get-tuple-element.64.refs_1_, s32[10,256]{1,0:T(8,128)S(1)} %copy-done.6, ...), custom_call_target="tpu_custom_call", output_to_operand_aliasing={{0}: (9, {}), {1}: (10, {})} | custom-call | flops 1358954496 | bytes 2359296 | tf_op jit(solution)/shard_map/second_source_4/pallas_call | solution.py:380
  67.2 2.9 %outer_sweep_south_0.1 = (bf16[2,576,256]{2,1,0:T(8,128)(2,1)S(1)}, f32[3,576,256]{2,1,0:T(8,128)S(1)}) custom-call(f32[2,36]{1,0:T(2,128)S(1)} %copy-done.14, s32[10,256]{1,0:T(8,128)S(1)} %copy-done.8, f32[10,256]{1,0:T(8,128)S(1)} %copy-done.9, f32[32,128]{1,0:T(8,128)S(1)} %broadcast_in_dim.2.refs_3_, bf16[2,576,256]{2,1,0:T(8,128)(2,1)S(1)} %copy-done.5, ...), custom_call_target="tpu_custom_call" | custom-call | flops 660602880 | bytes 14745600 | tf_op jit(solution)/shard_map/outer_sweep_south_0/pallas_call | solution.py:329
  70.2 3.4 %second_source_1.1 = (bf16[10,1152,256]{2,1,0:T(8,128)(2,1)}, f32[10,2,256]{2,1,0:T(2,128)}) custom-call(bf16[6,576,256]{2,1,0:T(8,128)(2,1)S(1)} %get-tuple-element.54.refs_0_, bf16[2,576,256]{2,1,0:T(8,128)(2,1)S(1)} %get-tuple-element.77.refs_1_, s32[10,256]{1,0:T(8,128)S(1)} %copy-done.6, ...), custom_call_target="tpu_custom_call", output_to_operand_aliasing={{0}: (9, {}), {1}: (10, {})} | custom-call | flops 1358954496 | bytes 2359296 | tf_op jit(solution)/shard_map/second_source_1/pallas_call | solution.py:380
  73.6 1.5 %collective-permute-done.3.refs_7_ = bf16[2,592,256]{2,1,0:T(8,128)(2,1)S(1)} collective-permute-done((bf16[2,592,256]{2,1,0:T(8,128)(2,1)S(1)}, bf16[2,592,256]{2,1,0:T(8,128)(2,1)S(1)}, u32[]{:S(2)}, u32[]{:S(2)}) %collective-permute-start.3) | collective-permute-done | bytes 606240 | tf_op jit(solution)/shard_map/ppermute | solution.py:443
  75.1 2.9 %outer_sweep_south_2.1.refs_1_ = bf16[2,576,256]{2,1,0:T(8,128)(2,1)S(1)} custom-call(f32[2,36]{1,0:T(2,128)S(1)} %copy-done.14, s32[10,256]{1,0:T(8,128)S(1)} %copy-done.8, f32[10,256]{1,0:T(8,128)S(1)} %copy-done.9, f32[32,128]{1,0:T(8,128)S(1)} %broadcast_in_dim.2.refs_3_, bf16[2,576,256]{2,1,0:T(8,128)(2,1)S(1)} %copy-done.5, ...), custom_call_target="tpu_custom_call" | custom-call | flops 660602880 | bytes 14745600 | tf_op jit(solution)/shard_map/outer_sweep_south_2/pallas_call | solution.py:329
  78.0 3.4 %second_source_0.1 = (bf16[10,1152,256]{2,1,0:T(8,128)(2,1)}, f32[10,2,256]{2,1,0:T(2,128)}) custom-call(bf16[6,576,256]{2,1,0:T(8,128)(2,1)S(1)} %get-tuple-element.54.refs_0_, bf16[2,576,256]{2,1,0:T(8,128)(2,1)S(1)} %outer_sweep_south_2.1.refs_1_, s32[10,256]{1,0:T(8,128)S(1)} %copy-done.6, ...), custom_call_target="tpu_custom_call", output_to_operand_aliasing={{0}: (9, {}), {1}: (10, {})} | custom-call | flops 1358954496 | bytes 2359296 | tf_op jit(solution)/shard_map/second_source_0/pallas_call | solution.py:380
  (30 shorter events, 0.1 us)
Async XLA Ops:
  7.0 42.5 %collective-permute-start = (bf16[2,592,256]{2,1,0:T(8,128)(2,1)}, bf16[2,592,256]{2,1,0:T(8,128)(2,1)}, u32[]{:S(2)}, u32[]{:S(2)}) collective-permute-start(bf16[2,592,256]{2,1,0:T(8,128)(2,1)} %get-tuple-element.46.refs_4_), channel_id=1, source_target_pairs={{1,0},{2,1},{3,2},{4,3},{5,4},{6,5},{7,6},{8,7},{9,8},{10,9},{11,1... | collective-permute-start | bytes 1818632 | tf_op jit(solution)/shard_map/ppermute | solution.py:430
  13.4 8.8 %copy-start = (bf16[1152,1152]{1,0:T(8,128)(2,1)S(1)}, bf16[1152,1152]{1,0:T(8,128)(2,1)}, u32[]{:S(2)}) copy-start(bf16[1152,1152]{1,0:T(8,128)(2,1)} %refs_6_.19) | copy-start | bytes 7962628
  13.4 8.8 %copy-start.1 = (bf16[1152,10,256]{2,0,1:T(8,128)(2,1)S(1)}, bf16[1152,10,256]{2,0,1:T(8,128)(2,1)}, u32[]{:S(2)}) copy-start(bf16[1152,10,256]{2,0,1:T(8,128)(2,1)} %param.14) | copy-start | bytes 17694724
  13.4 8.8 %copy-start.2 = (f32[1152,128]{1,0:T(8,128)S(1)}, f32[1152,128]{1,0:T(8,128)}, u32[]{:S(2)}) copy-start(f32[1152,128]{1,0:T(8,128)} %get-tuple-element.48.refs_8_.refs_5_) | copy-start | bytes 1769476
  13.4 8.8 %copy-start.3 = (bf16[1152,128]{1,0:T(8,128)(2,1)S(1)}, bf16[1152,128]{1,0:T(8,128)(2,1)}, u32[]{:S(2)}) copy-start(bf16[1152,128]{1,0:T(8,128)(2,1)} %get-tuple-element.49.refs_9_.refs_7_) | copy-start | bytes 884740
  13.4 8.8 %copy-start.4 = (f32[1152,128]{1,0:T(8,128)S(1)}, f32[1152,128]{1,0:T(8,128)}, u32[]{:S(2)}) copy-start(f32[1152,128]{1,0:T(8,128)} %get-tuple-element.47.refs_7_) | copy-start | bytes 1769476
  13.4 8.8 %copy-start.6 = (s32[10,256]{1,0:T(8,128)S(1)}, s32[10,256]{1,0:T(8,128)}, u32[]{:S(2)}) copy-start(s32[10,256]{1,0:T(8,128)} %refs_2_.29) | copy-start | bytes 30724
  13.4 8.8 %copy-start.7 = (f32[10,256]{1,0:T(8,128)S(1)}, f32[10,256]{1,0:T(8,128)}, u32[]{:S(2)}) copy-start(f32[10,256]{1,0:T(8,128)} %refs_3_.19) | copy-start | bytes 30724
  13.5 8.8 %copy-start.8 = (s32[10,256]{1,0:T(8,128)S(1)}, s32[10,256]{1,0:T(8,128)}, u32[]{:S(2)}) copy-start(s32[10,256]{1,0:T(8,128)} %refs_1_.19) | copy-start | bytes 30724
  13.5 8.8 %copy-start.9 = (f32[10,256]{1,0:T(8,128)S(1)}, f32[10,256]{1,0:T(8,128)}, u32[]{:S(2)}) copy-start(f32[10,256]{1,0:T(8,128)} %refs_2_.28) | copy-start | bytes 30724
  13.5 8.8 %copy-start.10 = (f32[8]{0:T(128)S(1)}, f32[8]{0:T(128)}, u32[]{:S(2)}) copy-start(f32[8]{0:T(128)} %refs_4_.19) | copy-start | bytes 100
  13.5 8.8 %copy-start.13 = (s32[64]{0:T(128)S(1)}, s32[64]{0:T(128)}, u32[]{:S(2)}) copy-start(s32[64]{0:T(128)} %refs_5_.9) | copy-start | bytes 772
  19.6 29.8 %collective-permute-start.1 = (bf16[2,592,256]{2,1,0:T(8,128)(2,1)}, bf16[2,592,256]{2,1,0:T(8,128)(2,1)S(1)}, u32[]{:S(2)}, u32[]{:S(2)}) collective-permute-start(bf16[2,592,256]{2,1,0:T(8,128)(2,1)} %get-tuple-element.50.refs_5_), channel_id=1, source_target_pairs={{1,0},{2,1},{3,2},{4,3},{5,4},{6,5},{7,6},{8,7},{9,8},{10,9},{11,1... | collective-permute-start | bytes 1818632 | tf_op jit(solution)/shard_map/ppermute | solution.py:434
  29.0 3.4 %copy-start.18 = (f32[32]{0:T(128)S(1)}, f32[32]{0:T(128)}, u32[]{:S(2)}) copy-start(f32[32]{0:T(128)} %param.24) | copy-start | bytes 388
  29.0 3.4 %copy-start.5 = (bf16[2,576,256]{2,1,0:T(8,128)(2,1)S(1)}, bf16[2,576,256]{2,1,0:T(8,128)(2,1)}, u32[]{:S(2)}) copy-start(bf16[2,576,256]{2,1,0:T(8,128)(2,1)} %get-tuple-element.55.refs_4_) | copy-start | bytes 1769476
  29.0 3.4 %copy-start.14 = (f32[2,36]{1,0:T(2,128)S(1)}, f32[2,36]{1,0:T(2,128)}, u32[]{:S(2)}) copy-start(f32[2,36]{1,0:T(2,128)} %constant.5.clone.refs_0_) | copy-start | bytes 868
  29.0 3.4 %copy-start.17 = (bf16[2,576,256]{2,1,0:T(8,128)(2,1)S(1)}, bf16[2,576,256]{2,1,0:T(8,128)(2,1)}, u32[]{:S(2)}) copy-start(bf16[2,576,256]{2,1,0:T(8,128)(2,1)} %get-tuple-element.57.refs_5_) | copy-start | bytes 1769476
  32.5 10.2 %copy-start.15 = (bf16[2,592,256]{2,1,0:T(8,128)(2,1)S(1)}, bf16[2,592,256]{2,1,0:T(8,128)(2,1)}, u32[]{:S(2)}) copy-start(bf16[2,592,256]{2,1,0:T(8,128)(2,1)} %get-tuple-element.46.refs_4_) | copy-start | bytes 1818628
  32.5 10.2 %copy-start.16 = (bf16[2,592,256]{2,1,0:T(8,128)(2,1)S(1)}, bf16[2,592,256]{2,1,0:T(8,128)(2,1)}, u32[]{:S(2)}) copy-start(bf16[2,592,256]{2,1,0:T(8,128)(2,1)} %get-tuple-element.50.refs_5_) | copy-start | bytes 1818628
  39.2 28.0 %collective-permute-start.2 = (bf16[2,592,256]{2,1,0:T(8,128)(2,1)S(1)}, bf16[2,592,256]{2,1,0:T(8,128)(2,1)S(1)}, u32[]{:S(2)}, u32[]{:S(2)}) collective-permute-start(bf16[2,592,256]{2,1,0:T(8,128)(2,1)S(1)} %get-tuple-element.75.refs_8_), channel_id=1, source_target_pairs={{0,1},{1,2},{2,3},{3,4},{4,5},{5,6},{6,7},{7,8},{8,9},{9,10},{10,1... | collective-permute-start | bytes 1818632 | tf_op jit(solution)/shard_map/ppermute | solution.py:438
  54.8 20.3 %collective-permute-start.3 = (bf16[2,592,256]{2,1,0:T(8,128)(2,1)S(1)}, bf16[2,592,256]{2,1,0:T(8,128)(2,1)S(1)}, u32[]{:S(2)}, u32[]{:S(2)}) collective-permute-start(bf16[2,592,256]{2,1,0:T(8,128)(2,1)S(1)} %get-tuple-element.84.refs_7_), channel_id=1, source_target_pairs={{0,1},{1,2},{2,3},{3,4},{4,5},{5,6},{6,7},{7,8},{8,9},{9,10},{10,1... | collective-permute-start | bytes 1818632 | tf_op jit(solution)/shard_map/ppermute | solution.py:443
  67.2 3.0 %copy-start.12 = (f32[2,8,256]{2,1,0:T(8,128)S(1)}, f32[2,8,256]{2,1,0:T(8,128)}, u32[]{:S(2)}) copy-start(f32[2,8,256]{2,1,0:T(8,128)} %get-tuple-element.78.refs_8_) | copy-start | bytes 49156
  73.6 4.4 %copy-start.11 = (f32[2,8,256]{2,1,0:T(8,128)S(1)}, f32[2,8,256]{2,1,0:T(8,128)}, u32[]{:S(2)}) copy-start(f32[2,8,256]{2,1,0:T(8,128)} %get-tuple-element.85.refs_8_) | copy-start | bytes 49156

commit v4 on v3

--- a/solution.py
+++ b/solution.py
@@ -21,8 +21,7 @@
 TAIL = 16
 AXES = ("pts", "grp")
 VMEM = 28 * 1024 * 1024
-OPENING_VMEM = 57 * 1024 * 1024
-NEXT_VMEM = 54 * 1024 * 1024
+FIRST_VMEM = {0: 57 * 1024 * 1024, 1: 54 * 1024 * 1024, 4: 28 * 1024 * 1024}
 
 ANGLES = 2.0 * math.pi * (np.arange(DIR) + 0.5) / DIR
 
@@ -81,115 +80,113 @@
     count[...] = hits
 
 
-def first_kernel(pair, opening, x_ref, land_ref, depth_ref, damp_ref, clear_ref, outlets_ref, scale_ref, *rest):
+def first_kernel(pairs, x_ref, jac_hbm, *refs):
+    opening = pairs[0] == 0
     tables = 4 if opening else 3
-    if pair < 2:
-        far = [x_ref.at[2 * pair : 2 * pair + 2], rest[tables], land_ref, depth_ref, damp_ref, clear_ref, outlets_ref,
-               scale_ref, *rest[:tables]]
-        near, sems = rest[-len(far) - 1 : -1], rest[-1]
-        rest = rest[: -len(far) - 1]
-        copies = [pltpu.make_async_copy(a, b, sems.at[i]) for i, (a, b) in enumerate(zip(far, near))]
-        x_ref, jac_ref, land_ref, depth_ref, damp_ref, clear_ref, outlets_ref, scale_ref = near[:8]
-        rest = near[8:] + (jac_ref,) + rest[tables + 1 :]
-    else:
-        near, sems = rest[-2], rest[-1]
-        rest = rest[:-2]
-        copies = [pltpu.make_async_copy(x_ref.at[2 * pair : 2 * pair + 2], near, sems.at[0])]
-        x_ref = near
+    far = refs[: 6 + tables]
+    outs = refs[6 + tables : -7 - len(far)]
+    sea, count, rate, held, x_near, jac_ref = refs[-7 - len(far) : -1 - len(far)]
+    near, sems = refs[-1 - len(far) : -1], refs[-1]
+    copies = [pltpu.make_async_copy(a, b, sems.at[i]) for i, (a, b) in enumerate(zip(far, near))]
+    waits = [pltpu.make_async_copy(jac_hbm, jac_ref, sems.at[len(far)])]
+    for i, pair in enumerate(pairs):
+        waits.append(
+            pltpu.make_async_copy(
+                x_ref.at[2 * pair : 2 * pair + 2], x_near.at[2 * i : 2 * i + 2], sems.at[len(far) + 1 + i]
+            )
+        )
+    for copy in copies + waits:
+        copy.start()
     for copy in copies:
-        copy.start()
-    for copy in copies[2:]:
         copy.wait()
-    sea, count, rate, held = rest[-4:]
-    rest = rest[:-4]
+    land_ref, depth_ref, damp_ref, clear_ref, outlets_ref, scale_ref = near[:6]
     if opening:
-        weight_ref, freq_ref, growth_ref, compass_ref, _, fw_ref, fd_ref, wave_ref = rest[:8]
+        weight_ref, freq_ref, growth_ref, compass_ref = near[6:]
+        fw_ref, fd_ref, wave_ref = outs[:3]
+        outs = outs[3:]
         fw_ref[...] = column(weight_ref[...])
         fd_ref[...] = column(freq_ref[...])
         hi, mid, low = three_pieces(column(growth_ref[...]) * compass_ref[...])
         lane = lax.broadcasted_iota(jnp.int32, (K, 128), 1)
         wave_ref[...] = jnp.where(lane < 8, hi, jnp.where(lane < 16, mid, low)).astype(jnp.bfloat16)
-        outs = rest[8:]
     else:
-        fw_ref, fd_ref, wave_ref, jac_ref = rest[:4]
-        outs = rest[4:]
-    halves, wind_ref = outs[:2], outs[2]
+        fw_ref, fd_ref, wave_ref = near[6:]
     point_fields(land_ref, depth_ref, outlets_ref, scale_ref, sea, count, rate)
-    for copy in copies[:2]:
-        copy.wait()
-
-    fw = fw_ref[...]
-    fw = jnp.concatenate([fw, fw], axis=1)
-    seeds = []
-    fields = []
-    for e in range(2):
-        r = slice(2 * pair + e, 2 * pair + e + 1)
-        lone = sea[r, :] * (x_ref[e].astype(jnp.float32) + fw * count[r, :])
-        seeds.append(lone.astype(jnp.bfloat16))
-        fields.append((rate[r, :], damp_ref[r, :]))
-    spectrum = jnp.concatenate(seeds, axis=1)
-    for m in range(3):
-        rows = slice(m * 384, (m + 1) * 384)
-        mixed = contract(jac_ref[:, rows], spectrum)
-        fd = fd_ref[rows, :]
-        for piece in range(4):
-            e, side = divmod(piece, 2)
-            lanes = slice(side * 128, (side + 1) * 128)
-            at = slice(piece * 128, (piece + 1) * 128)
-            v = seeds[e][rows, lanes].astype(jnp.float32)
-            held[piece, rows, :] = (
-                v + fields[e][0][:, lanes] * mixed[:, at] - (fields[e][1][:, lanes] * fd) * v
-            )
-    wind = contract(wave_ref[...], spectrum)
-    wind = wind[0:8] + wind[8:16] + wind[16:24]
-    for e in range(2):
-        wind_ref[e] = wind[:, e * LON : (e + 1) * LON]
-    for half in range(2):
-        for d in range(18):
+    waits[0].wait()
+
+    for i, pair in enumerate(pairs):
+        waits[1 + i].wait()
+        to = 2 * i if opening else 0
+        halves, wind_ref = (outs[:2], outs[2]) if opening else (outs[3 * i : 3 * i + 2], outs[3 * i + 2])
+        fw = fw_ref[...]
+        fw = jnp.concatenate([fw, fw], axis=1)
+        seeds = []
+        fields = []
+        for e in range(2):
+            r = slice(2 * pair + e, 2 * pair + e + 1)
+            lone = sea[r, :] * (x_near[2 * i + e].astype(jnp.float32) + fw * count[r, :])
+            seeds.append(lone.astype(jnp.bfloat16))
+            fields.append((rate[r, :], damp_ref[r, :]))
+        spectrum = jnp.concatenate(seeds, axis=1)
+        for m in range(3):
+            rows = slice(m * 384, (m + 1) * 384)
+            mixed = contract(jac_ref[:, rows], spectrum)
+            fd = fd_ref[rows, :]
             for piece in range(4):
                 e, side = divmod(piece, 2)
-                halves[half][e, d * FREQ : (d + 1) * FREQ, side * 128 : (side + 1) * 128] = held[
-                    piece, pl.ds(half * 18 + d, FREQ, stride=DIR), :
-                ].astype(jnp.bfloat16)
-    if pair != 2:
+                lanes = slice(side * 128, (side + 1) * 128)
+                at = slice(piece * 128, (piece + 1) * 128)
+                v = seeds[e][rows, lanes].astype(jnp.float32)
+                held[piece, rows, :] = (
+                    v + fields[e][0][:, lanes] * mixed[:, at] - (fields[e][1][:, lanes] * fd) * v
+                )
+        wind = contract(wave_ref[...], spectrum)
+        wind = wind[0:8] + wind[8:16] + wind[16:24]
         for e in range(2):
-            r = slice(2 * pair + e, 2 * pair + e + 1)
-            pieces = three_pieces(sea[r, :] * clear_ref[r, :])
-            halves[0 if pair < 2 else 1][e, HALF : HALF + TAIL, :] = stack_pieces(pieces)
-
-
-def first_source(pair, opening, x, land, depth, damping, clear, outlets, scale, comps, jacobian):
-    sizes = (HALF + TAIL if pair < 2 else HALF, HALF + TAIL if pair > 2 else HALF)
-    out_shape = [jax.ShapeDtypeStruct((2, size, LON), jnp.bfloat16) for size in sizes]
-    out_shape.append(jax.ShapeDtypeStruct((2, 8, LON), jnp.float32))
-    if opening:
-        tables = [jax.ShapeDtypeStruct((K, 128), dtype) for dtype in (jnp.float32, jnp.float32, jnp.bfloat16)]
-        out_shape = tables + out_shape
+            wind_ref[to + e] = wind[:, e * LON : (e + 1) * LON]
+        for half in range(2):
+            for d in range(18):
+                for piece in range(4):
+                    e, side = divmod(piece, 2)
+                    halves[half][to + e, d * FREQ : (d + 1) * FREQ, side * 128 : (side + 1) * 128] = held[
+                        piece, pl.ds(half * 18 + d, FREQ, stride=DIR), :
+                    ].astype(jnp.bfloat16)
+        if pair != 2:
+            for e in range(2):
+                r = slice(2 * pair + e, 2 * pair + e + 1)
+                pieces = three_pieces(sea[r, :] * clear_ref[r, :])
+                halves[0 if pair < 2 else 1][to + e, HALF : HALF + TAIL, :] = stack_pieces(pieces)
+
+
+def first_source(pairs, x, jacobian, land, depth, damping, clear, outlets, scale, comps):
+    out_shape = []
+    if pairs[0] == 0:
+        out_shape += [jax.ShapeDtypeStruct((K, 128), dtype) for dtype in (jnp.float32, jnp.float32, jnp.bfloat16)]
+    for pair in pairs[:1] if pairs[0] == 0 else pairs:
+        count_rows = 2 * len(pairs) if pairs[0] == 0 else 2
+        for size in (HALF + TAIL if pair < 2 else HALF, HALF + TAIL if pair > 2 else HALF):
+            out_shape.append(jax.ShapeDtypeStruct((count_rows, size, LON), jnp.bfloat16))
+        out_shape.append(jax.ShapeDtypeStruct((count_rows, 8, LON), jnp.float32))
+    small = (land, depth, damping, clear, outlets, scale, *comps)
     scratch = [pltpu.VMEM((ROWS, LON), jnp.float32)] * 3 + [pltpu.VMEM((4, K, 128), jnp.float32)]
-    scratch.append(pltpu.VMEM((2, K, LON), jnp.bfloat16))
-    if pair < 2:
-        scratch.append(pltpu.VMEM((K, K), jnp.bfloat16))
-        scratch += [pltpu.VMEM(a.shape, a.dtype) for a in (land, depth, damping, clear)]
-        scratch += [pltpu.SMEM(a.shape, a.dtype) for a in (outlets, scale)]
-        scratch += [pltpu.VMEM(a.shape, a.dtype) for a in comps]
-    scratch.append(pltpu.SemaphoreType.DMA((12,)))
-    anywhere = pl.BlockSpec(memory_space=pl.ANY)
-    place = anywhere if pair < 2 else held_whole()
+    scratch += [pltpu.VMEM((2 * len(pairs), K, LON), jnp.bfloat16), pltpu.VMEM((K, K), jnp.bfloat16)]
+    for at, a in enumerate(small):
+        scratch.append((pltpu.SMEM if at in (4, 5) else pltpu.VMEM)(a.shape, a.dtype))
+    scratch.append(pltpu.SemaphoreType.DMA((len(small) + 1 + len(pairs),)))
 
     def body(*refs):
-        first_kernel(pair, opening, *refs)
+        first_kernel(pairs, *refs)
 
     return pl.pallas_call(
         body,
-        grid=(1,),
-        in_specs=[anywhere] + [place] * 4 + [place if pair < 2 else smem()] * 2 + [place] * (len(comps) + 1),
+        in_specs=[pl.BlockSpec(memory_space=pl.ANY)] * (2 + len(small)),
         out_specs=[held_whole()] * len(out_shape),
         out_shape=out_shape,
         scratch_shapes=scratch,
-        compiler_params=params((OPENING_VMEM, NEXT_VMEM, VMEM, VMEM, VMEM)[pair]),
-        cost_estimate=cost(2 * K * K * LON * 2, 4 * K * LON * 2),
-        name=f"first_source_{pair}",
-    )(x, land, depth, damping, clear, outlets, scale, *comps, jacobian)
+        compiler_params=params(FIRST_VMEM[pairs[0]]),
+        cost_estimate=cost(2 * K * K * LON * 2 * len(pairs), 4 * K * LON * 2 * len(pairs)),
+        name=f"first_source_{pairs[0]}",
+    )(x, jacobian, *small)
 
 
 def sweep_rows(north, table_ref, courant_ref, pass_rows, emit):
@@ -290,7 +287,8 @@
     state_out = rest[messages + 1] if begin + count < HALO else None
 
     def halo_row(t, rows, lanes=slice(None)):
-        return halo[t // 2][t % 2 if north else 1 - t % 2, rows, lanes].astype(jnp.float32)
+        place = (t // 2, t % 2 if north else 1 - t % 2)
+        return halo[place[0]][place[1], rows, lanes].astype(jnp.float32)
 
     own_passage(land_ref, clear_ref, pass_rows, north)
     for t in range(begin + count):
@@ -338,63 +336,76 @@
     )(table, land, clear, courant, first, state, *halos)
 
 
-def second_kernel(pair, at_n, at_s, n_ref, s_ref, *refs):
-    depth_ref, damp_ref, scale_ref, fd_ref, jac_ref, wave_ref, wind_in = refs[:7]
+def second_kernel(jobs, count, *refs):
+    sources, refs = refs[:count], refs[count:]
+    depth_ref, damp_ref, scale_ref, fd_ref, jac_ref, wave_ref = refs[:6]
     out_ref, wind_ref, held = refs[-3:]
-    here = slice(2 * pair, 2 * pair + 2)
-    depth = depth_ref[here, :]
-    rate = jnp.zeros((2, LON), jnp.float32)
-    for c in range(NCLASS):
-        rate = jnp.where(depth == c, scale_ref[c], rate)
-    damp = damp_ref[here, :]
-    for half, ref, at in ((0, n_ref, at_n), (1, s_ref, at_s)):
-        for d in range(18):
+
+    def run(pair, south_at, wind_at):
+        north_at = (0, 2 * pair) if pair < 3 else (1, 2 * pair - 6)
+        here = slice(2 * pair, 2 * pair + 2)
+        depth = depth_ref[here, :]
+        rate = jnp.zeros((2, LON), jnp.float32)
+        for c in range(NCLASS):
+            rate = jnp.where(depth == c, scale_ref[c], rate)
+        damp = damp_ref[here, :]
+        for half, (source, at) in enumerate((north_at, south_at)):
+            for d in range(18):
+                for piece in range(4):
+                    e, side = divmod(piece, 2)
+                    held[piece, pl.ds(half * 18 + d, FREQ, stride=DIR), :] = sources[source][
+                        at + e, d * FREQ : (d + 1) * FREQ, side * 128 : (side + 1) * 128
+                    ].astype(jnp.float32)
+        spectrum = jnp.concatenate([held[piece].astype(jnp.bfloat16) for piece in range(4)], axis=1)
+        for m in range(3):
+            rows = slice(m * 384, (m + 1) * 384)
+            mixed = contract(jac_ref[:, rows], spectrum)
+            fd = fd_ref[rows, :]
             for piece in range(4):
                 e, side = divmod(piece, 2)
-                held[piece, pl.ds(half * 18 + d, FREQ, stride=DIR), :] = ref[
-                    at + e, d * FREQ : (d + 1) * FREQ, side * 128 : (side + 1) * 128
-                ].astype(jnp.float32)
-    spectrum = jnp.concatenate([held[piece].astype(jnp.bfloat16) for piece in range(4)], axis=1)
-    for m in range(3):
-        rows = slice(m * 384, (m + 1) * 384)
-        mixed = contract(jac_ref[:, rows], spectrum)
-        fd = fd_ref[rows, :]
-        for piece in range(4):
-            e, side = divmod(piece, 2)
-            lanes = slice(side * 128, (side + 1) * 128)
-            at = slice(piece * 128, (piece + 1) * 128)
-            v = held[piece, rows, :]
-            out_ref[e, rows, lanes] = (
-                v + rate[e : e + 1, lanes] * mixed[:, at] - (damp[e : e + 1, lanes] * fd) * v
-            ).astype(jnp.bfloat16)
-    wind = contract(wave_ref[...], spectrum)
-    wind = wind[0:8] + wind[8:16] + wind[16:24]
-    for e in range(2):
-        wind_ref[e] = (wind_in[e] + wind[:, e * LON : (e + 1) * LON])[:2]
-
-
-def second_source(pair, north, at_n, south, at_s, before, depth, damping, scale, fd, jac, wave, wind):
+                lanes = slice(side * 128, (side + 1) * 128)
+                at = slice(piece * 128, (piece + 1) * 128)
+                v = held[piece, rows, :]
+                out_ref[e, rows, lanes] = (
+                    v + rate[e : e + 1, lanes] * mixed[:, at] - (damp[e : e + 1, lanes] * fd) * v
+                ).astype(jnp.bfloat16)
+        wind = contract(wave_ref[...], spectrum)
+        wind = wind[0:8] + wind[8:16] + wind[16:24]
+        for e in range(2):
+            wind_ref[e] = (sources[wind_at][e] + wind[:, e * LON : (e + 1) * LON])[:2]
+
+    step = pl.program_id(0)
+    for i, job in enumerate(jobs):
+        pl.when(step == i)(lambda job=job: run(*job))
+
+
+def second_source(jobs, sources, before, depth, damping, scale, fd, jac, wave):
+    start = jobs[0][0]
+
     def body(*refs):
-        second_kernel(pair, at_n, at_s, *refs)
+        second_kernel(jobs, len(sources), *refs)
 
     return pl.pallas_call(
         body,
-        grid=(1,),
-        in_specs=[held_whole()] * 4
+        grid=(len(jobs),),
+        in_specs=[held_whole()] * (len(sources) + 2)
         + [smem()]
-        + [held_whole()] * 4
+        + [held_whole()] * 3
         + [pl.BlockSpec(memory_space=pl.ANY)] * len(before),
-        out_specs=[pl.BlockSpec((2, K, LON), lambda i: (pair, 0, 0)), pl.BlockSpec((2, 2, LON), lambda i: (pair, 0, 0))],
+        out_specs=[
+            pl.BlockSpec((2, K, LON), lambda i: (i + start, 0, 0)),
+            pl.BlockSpec((2, 2, LON), lambda i: (i + start, 0, 0)),
+        ],
         out_shape=[
             jax.ShapeDtypeStruct((ROWS, K, LON), jnp.bfloat16),
             jax.ShapeDtypeStruct((ROWS, 2, LON), jnp.float32),
         ],
-        input_output_aliases={9: 0, 10: 1} if before else {},
+        input_output_aliases={len(sources) + 6: 0, len(sources) + 7: 1} if before else {},
         scratch_shapes=[pltpu.VMEM((4, K, 128), jnp.float32)],
         compiler_params=params(),
-        cost_estimate=cost(2 * K * K * LON * 2, 4 * K * LON * 2),
-        name=f"second_source_{pair}",
-    )(north, south, depth, damping, scale, fd, jac, wave, wind, *before)
+        cost_estimate=cost(2 * K * K * LON * 2 * len(jobs), 4 * K * LON * 2 * len(jobs)),
+        name=f"second_source_{start}",
+    )(*sources, depth, damping, scale, fd, jac, wave, *before)
 
 
 def body(
@@ -418,37 +429,39 @@
         compass[:, 8 * at] = np.tile(np.cos(ANGLES), FREQ)
         compass[:, 8 * at + 1] = np.tile(np.sin(ANGLES), FREQ)
     comps = (flux_weight, freq_damp, wind_growth, jnp.asarray(compass))
-    common = (x, land_sea, depth_class, damping, transparency, outlets, source_scale)
+    common = (land_sea, depth_class, damping, transparency, outlets, source_scale)
     down = [(i + 1, i) for i in range(devices - 1)]
     up = [(i, i + 1) for i in range(devices - 1)]
     speed = jnp.broadcast_to(courant[:, None], (FREQ, 128))
     table = jnp.asarray(np.abs(np.stack([np.cos(ANGLES), np.sin(ANGLES)])), jnp.float32)
     local = (table, land_sea, transparency, speed)
-    n, s, winds, halo_n, halo_s = {}, {}, {}, {}, {}
-
-    fw, fd, wave, n[0], s[0], winds[0] = first_source(0, True, *common, comps, jacobian)
-    halo_n[0] = lax.ppermute(n[0], AXES, down)
+    n, s, winds, halo_s = {}, {}, {}, {}
+
+    fw, fd, wave, n[0], s[0], winds[0] = first_source((0,), x, jacobian, *common, comps)
+    halo_n = [lax.ppermute(n[0], AXES, down)]
     comps = (fw, fd, wave)
-    for pair in (1, 4, 3, 2):
-        n[pair], s[pair], winds[pair] = first_source(pair, False, *common, comps, jacobian)
-    halo_n[1] = lax.ppermute(n[1], AXES, down)
+    n[1], s[1], winds[1] = first_source((1,), x, jacobian, *common, comps)
+    halo_n.append(lax.ppermute(n[1], AXES, down))
+    rest = (4, 3, 2)
+    parts = first_source(rest, x, jacobian, *common, comps)
+    for i, pair in enumerate(rest):
+        n[pair], s[pair], winds[pair] = parts[3 * i : 3 * i + 3]
+    in_s, state_s = inner_sweep(False, *local, [s[pair] for pair in range(5)])
+    s[4], state_s, n[2] = lax.optimization_barrier((s[4], state_s, n[2]))
+    halo_s[0] = lax.ppermute(s[4], AXES, up)
     in_n, state_n = inner_sweep(True, *local, [n[pair] for pair in range(5)])
-    in_s, state_s = inner_sweep(False, *local, [s[pair] for pair in range(5)])
-    s[4], state_s = lax.optimization_barrier((s[4], state_s))
-    halo_s[0] = lax.ppermute(s[4], AXES, up)
+    s[3], state_n = lax.optimization_barrier((s[3], state_n))
+    halo_s[1] = lax.ppermute(s[3], AXES, up)
     last = (depth_class, damping, source_scale, fd, jacobian, wave)
-    part = second_source(2, in_n, 4, in_s, 0, (), *last, winds[2])
-    (edge,) = outer_sweep(True, 0, HALO, *local, n[4], state_n, (halo_n[0], halo_n[1]))
-    s[3], edge = lax.optimization_barrier((s[3], edge))
-    halo_s[1] = lax.ppermute(s[3], AXES, up)
-    part = second_source(3, edge, 0, in_s, 2, part, *last, winds[3])
-    part = second_source(4, edge, 2, in_s, 4, part, *last, winds[4])
+    (edge,) = outer_sweep(True, 0, HALO, *local, n[4], state_n, halo_n)
+    jobs = ((2, (2, 0), 3), (3, (2, 2), 4), (4, (2, 4), 5))
+    part = second_source(jobs, (in_n, edge, in_s, winds[2], winds[3], winds[4]), (), *last)
     state_s, *part = lax.optimization_barrier((state_s, *part))
     edge, state_s = outer_sweep(False, 0, 2, *local, s[0], state_s, (halo_s[0],))
-    part = second_source(1, in_n, 2, edge, 0, part, *last, winds[1])
+    part = second_source(((1, (1, 0), 2),), (in_n, edge, winds[1]), part, *last)
     state_s, *part = lax.optimization_barrier((state_s, *part))
     (edge,) = outer_sweep(False, 2, 2, *local, s[0], state_s, (halo_s[0], halo_s[1]))
-    out, wind_out = second_source(0, in_n, 0, edge, 0, part, *last, winds[0])
+    out, wind_out = second_source(((0, (1, 0), 2),), (in_n, edge, winds[0]), part, *last)
     return out.transpose(1, 0, 2), wind_out.transpose(1, 0, 2)
 
 

time: 81.7 us -> 78.2 us (0.957)
  Pallas kernels: 64.2 us -> 59.9 us
    pallas_call x10 -> x6, Pallas kernels: 39.6 us -> 35.3 us  [the longest x3 20.6 us: first_source(): pl.pallas_call(body, in_specs=[pl.BlockSpec(memory_space=pl.ANY)] * (2 +...]
  transfers between devices with their start and end apart: 4 -> 4, of which waited for: 1 -> 1; matrix products, arithmetic and copies ran while one was open for 0% -> 0% of each run, Pallas kernels for 63% -> 61%
where the time goes in v4:
time: 78.2 us; the launch traced here: 77.9 us
  Pallas kernels  59.9 us (77%)
  starting transfers between devices  14.7 us (19%)
  waiting for transfers between devices  2.15 us (3%)
  between operations  1.01 us (1%)
    pallas_call x3, Pallas kernels, first_source(): pl.pallas_call(body, in_specs=[pl.BlockSpec(memory_space=pl.ANY)] * (2 +...  20.6 us
    pallas_call x3, Pallas kernels, second_source(): pl.pallas_call(body, grid=(len(jobs),), in_specs=[held_whole()] * (len(so...  14.7 us
    pallas_call x2, Pallas kernels, inner_sweep(): pl.pallas_call(body, in_specs=[smem()] + [held_whole()] * (3 + len(source...  13.5 us
    pallas_call x3, Pallas kernels, outer_sweep(): pl.pallas_call(body, in_specs=[smem()] + [held_whole()] * (5 + len(halos)...  11.2 us
    ppermute x1, starting transfers between devices, body(): halo_n = [lax.ppermute(n[0], AXES, down)]  6.4 us
    ppermute x1, starting transfers between devices, body(): halo_s[0] = lax.ppermute(s[4], AXES, up)  3.47 us
    ppermute x1, starting transfers between devices, body(): halo_n.append(lax.ppermute(n[1], AXES, down))  2.68 us
    ppermute x1, waiting for transfers between devices, body(): halo_s[1] = lax.ppermute(s[3], AXES, up)  2.15 us
  transfers between devices with their start and end apart: 4, of which 1 were waited for; matrix products, arithmetic and copies ran while one was open for 0% of the time, Pallas kernels for 61%

profile of v4, /device:TPU:96, one launch (start us, length us, event | category | flops | bytes accessed | tf_op | source)
XLA Modules:
  0.0 77.9 jit_solution(5973127697398518299)
XLA Ops:
  0.6 5.8 %first_source_0.1 = (f32[1152,128]{1,0:T(8,128)}, f32[1152,128]{1,0:T(8,128)}, bf16[1152,128]{1,0:T(8,128)(2,1)}, bf16[2,592,256]{2,1,0:T(8,128)(2,1)}, bf16[2,5...) custom-call(bf16[10,1152,256]{2,1,0:T(8,128)(2,1)} %bitcast.3, bf16[1152,1152]{1,0:T(8,128)(2,1)} %refs_7_.11, ...), custom_call_target="tpu_custom_call" | custom-call | flops 1358954496 | bytes 2359296 | tf_op jit(solution)/shard_map/first_source_0/pallas_call | solution.py:180
  6.4 6.4 %collective-permute-start = (bf16[2,592,256]{2,1,0:T(8,128)(2,1)}, bf16[2,592,256]{2,1,0:T(8,128)(2,1)}, u32[]{:S(2)}, u32[]{:S(2)}) collective-permute-start(bf16[2,592,256]{2,1,0:T(8,128)(2,1)} %get-tuple-element.43.refs_4_), channel_id=1, source_target_pairs={{1,0},{2,1},{3,2},{4,3},{5,4},{6,5},{7,6},{8,7},{9,8},{10,9},{11,1... | collective-permute-start | bytes 1818632 | tf_op jit(solution)/shard_map/ppermute | solution.py:441
  12.8 0.0 copy-start
  12.8 0.0 copy-start.1
  12.8 0.0 copy-start.2
  12.9 0.0 copy-start.6
  12.9 0.0 copy-start.7
  12.9 0.0 copy-start.8
  12.9 0.0 copy-start.9
  12.9 0.0 copy-start.12
  12.9 0.0 copy-start.14
  12.9 6.1 %first_source_1.1 = (bf16[2,592,256]{2,1,0:T(8,128)(2,1)}, bf16[2,576,256]{2,1,0:T(8,128)(2,1)}, f32[2,8,256]{2,1,0:T(8,128)}) custom-call(bf16[10,1152,256]{2,1,0:T(8,128)(2,1)} %bitcast.4, bf16[1152,1152]{1,0:T(8,128)(2,1)} %refs_7_.11, s32[10,256]{1,0:T(8,128)} %refs_1_.15, s32[10,256]{1,0:T(8,128)} %refs_3_.9, f32[10,256]{1,0:T(8,128)} %refs_4_.9, ...), custom_call_target="tpu_custom_call" | custom-call | flops 1358954496 | bytes 2359296 | tf_op jit(solution)/shard_map/first_source_1/pallas_call | solution.py:180
  19.0 0.0 copy-start.18
  19.0 0.0 copy-start.13
  19.1 2.7 %collective-permute-start.1 = (bf16[2,592,256]{2,1,0:T(8,128)(2,1)}, bf16[2,592,256]{2,1,0:T(8,128)(2,1)S(1)}, u32[]{:S(2)}, u32[]{:S(2)}) collective-permute-start(bf16[2,592,256]{2,1,0:T(8,128)(2,1)} %get-tuple-element.47.refs_5_), channel_id=1, source_target_pairs={{1,0},{2,1},{3,2},{4,3},{5,4},{6,5},{7,6},{8,7},{9,8},{10,9},{11,1... | collective-permute-start | bytes 1818632 | tf_op jit(solution)/shard_map/ppermute | solution.py:444
  21.9 8.7 %first_source_4.1 = (bf16[2,576,256]{2,1,0:T(8,128)(2,1)S(1)}, bf16[2,592,256]{2,1,0:T(8,128)(2,1)S(1)}, f32[2,8,256]{2,1,0:T(8,128)S(1)}, bf16[2,576,256]{2,1,0...) custom-call(bf16[10,1152,256]{2,1,0:T(8,128)(2,1)S(1)} %bitcast.5, ...), custom_call_target="tpu_custom_call" | custom-call | flops 4076863488 | bytes 7077888 | tf_op jit(solution)/shard_map/first_source_4/pallas_call | solution.py:180
  30.6 0.1 broadcast_in_dim.2.refs_3_
  30.7 0.0 copy-start.15
  30.7 6.7 %inner_sweep_south.1 = (bf16[6,576,256]{2,1,0:T(8,128)(2,1)S(1)}, f32[3,576,256]{2,1,0:T(8,128)S(1)}) custom-call(f32[2,36]{1,0:T(2,128)S(1)} %copy-done.13, s32[10,256]{1,0:T(8,128)S(1)} %copy-done.6, f32[10,256]{1,0:T(8,128)S(1)} %copy-done.7, f32[32,128]{1,0:T(8,128)S(1)} %broadcast_in_dim.2.refs_3_, bf16[2,576,256]{2,1,0:T(8,128)(2,1)S(1)} %copy-done.4, ...), custom_call_target="tpu_custom_call" | custom-call | flops 2477260800 | bytes 17694720 | tf_op jit(solution)/shard_map/inner_sweep_south/pallas_call | solution.py:270
  37.5 3.5 %collective-permute-start.2 = (bf16[2,592,256]{2,1,0:T(8,128)(2,1)S(1)}, bf16[2,592,256]{2,1,0:T(8,128)(2,1)S(1)}, u32[]{:S(2)}, u32[]{:S(2)}) collective-permute-start(bf16[2,592,256]{2,1,0:T(8,128)(2,1)S(1)} %get-tuple-element.69.refs_8_), channel_id=1, source_target_pairs={{0,1},{1,2},{2,3},{3,4},{4,5},{5,6},{6,7},{7,8},{8,9},{9,10},{10,1... | collective-permute-start | bytes 1818632 | tf_op jit(solution)/shard_map/ppermute | solution.py:451
  41.0 6.8 %inner_sweep_north.1 = (bf16[6,576,256]{2,1,0:T(8,128)(2,1)S(1)}, f32[3,576,256]{2,1,0:T(8,128)S(1)}) custom-call(f32[2,36]{1,0:T(2,128)S(1)} %copy-done.13, s32[10,256]{1,0:T(8,128)S(1)} %copy-done.6, f32[10,256]{1,0:T(8,128)S(1)} %copy-done.7, f32[32,128]{1,0:T(8,128)S(1)} %broadcast_in_dim.2.refs_3_, bf16[2,592,256]{2,1,0:T(8,128)(2,1)S(1)} %copy-done.15, ...), custom_call_target="tpu_custom_call" | custom-call | flops 2477260800 | bytes 17694720 | tf_op jit(solution)/shard_map/inner_sweep_north/pallas_call | solution.py:270
  47.7 2.1 %collective-permute-start.3 = (bf16[2,592,256]{2,1,0:T(8,128)(2,1)S(1)}, bf16[2,592,256]{2,1,0:T(8,128)(2,1)S(1)}, u32[]{:S(2)}, u32[]{:S(2)}) collective-permute-start(bf16[2,592,256]{2,1,0:T(8,128)(2,1)S(1)} %get-tuple-element.78.refs_7_), channel_id=1, source_target_pairs={{0,1},{1,2},{2,3},{3,4},{4,5},{5,6},{6,7},{7,8},{8,9},{9,10},{10,1... | collective-permute-start | bytes 1818632 | tf_op jit(solution)/shard_map/ppermute | solution.py:454
  49.9 0.0 collective-permute-done.refs_6_
  49.9 0.0 collective-permute-done.1.refs_7_
  49.9 5.3 %outer_sweep_north_0.1.refs_1_ = bf16[4,576,256]{2,1,0:T(8,128)(2,1)S(1)} custom-call(f32[2,36]{1,0:T(2,128)S(1)} %copy-done.13, s32[10,256]{1,0:T(8,128)S(1)} %copy-done.6, f32[10,256]{1,0:T(8,128)S(1)} %copy-done.7, f32[32,128]{1,0:T(8,128)S(1)} %broadcast_in_dim.2.refs_3_, bf16[2,576,256]{2,1,0:T(8,128)(2,1)S(1)} %get-tuple-element.57.refs_8_.refs_4_, ...), custom_call_target="tpu_custom_call" | custom-call | flops 1321205760 | bytes 14745600 | tf_op jit(solution)/shard_map/outer_sweep_north_0/pallas_call | solution.py:327
  55.2 7.8 %second_source_2.1 = (bf16[10,1152,256]{2,1,0:T(8,128)(2,1)}, f32[10,2,256]{2,1,0:T(2,128)}) custom-call(bf16[6,576,256]{2,1,0:T(8,128)(2,1)S(1)} %get-tuple-element.58.refs_0_, bf16[4,576,256]{2,1,0:T(8,128)(2,1)S(1)} %outer_sweep_north_0.1.refs_1_, bf16[6,576,256]{2,1,0:T(8,128)(2,1)S(1)} %get-tuple-element.62.refs_2_, ...), custom_call_target="tpu_custom_call" | custom-call | flops 4076863488 | bytes 7077888 | tf_op jit(solution)/shard_map/second_source_2/pallas_call | solution.py:388
  63.0 0.0 collective-permute-done.2.refs_6_
  63.0 2.9 %outer_sweep_south_0.1 = (bf16[2,576,256]{2,1,0:T(8,128)(2,1)S(1)}, f32[3,576,256]{2,1,0:T(8,128)S(1)}) custom-call(f32[2,36]{1,0:T(2,128)S(1)} %copy-done.13, s32[10,256]{1,0:T(8,128)S(1)} %copy-done.6, f32[10,256]{1,0:T(8,128)S(1)} %copy-done.7, f32[32,128]{1,0:T(8,128)S(1)} %broadcast_in_dim.2.refs_3_, bf16[2,576,256]{2,1,0:T(8,128)(2,1)S(1)} %copy-done.4, ...), custom_call_target="tpu_custom_call" | custom-call | flops 660602880 | bytes 14745600 | tf_op jit(solution)/shard_map/outer_sweep_south_0/pallas_call | solution.py:327
  66.0 3.4 %second_source_1.1 = (bf16[10,1152,256]{2,1,0:T(8,128)(2,1)}, f32[10,2,256]{2,1,0:T(2,128)}) custom-call(bf16[6,576,256]{2,1,0:T(8,128)(2,1)S(1)} %get-tuple-element.58.refs_0_, bf16[2,576,256]{2,1,0:T(8,128)(2,1)S(1)} %get-tuple-element.71.refs_1_, f32[2,8,256]{2,1,0:T(8,128)S(1)} %copy-done.11, ...), custom_call_target="tpu_custom_call", output_to_operand_aliasing={{0}: (9, {}), {1}: (10, {})} | custom-call | flops 1358954496 | bytes 2359296 | tf_op jit(solution)/shard_map/second_source_1/pallas_call | solution.py:388
  69.4 2.1 %collective-permute-done.3.refs_7_ = bf16[2,592,256]{2,1,0:T(8,128)(2,1)S(1)} collective-permute-done((bf16[2,592,256]{2,1,0:T(8,128)(2,1)S(1)}, bf16[2,592,256]{2,1,0:T(8,128)(2,1)S(1)}, u32[]{:S(2)}, u32[]{:S(2)}) %collective-permute-start.3) | collective-permute-done | bytes 606240 | tf_op jit(solution)/shard_map/ppermute | solution.py:454
  71.6 2.9 %outer_sweep_south_2.1.refs_1_ = bf16[2,576,256]{2,1,0:T(8,128)(2,1)S(1)} custom-call(f32[2,36]{1,0:T(2,128)S(1)} %copy-done.13, s32[10,256]{1,0:T(8,128)S(1)} %copy-done.6, f32[10,256]{1,0:T(8,128)S(1)} %copy-done.7, f32[32,128]{1,0:T(8,128)S(1)} %broadcast_in_dim.2.refs_3_, bf16[2,576,256]{2,1,0:T(8,128)(2,1)S(1)} %copy-done.4, ...), custom_call_target="tpu_custom_call" | custom-call | flops 660602880 | bytes 14745600 | tf_op jit(solution)/shard_map/outer_sweep_south_2/pallas_call | solution.py:327
  74.5 3.4 %second_source_0.1 = (bf16[10,1152,256]{2,1,0:T(8,128)(2,1)}, f32[10,2,256]{2,1,0:T(2,128)}) custom-call(bf16[6,576,256]{2,1,0:T(8,128)(2,1)S(1)} %get-tuple-element.58.refs_0_, bf16[2,576,256]{2,1,0:T(8,128)(2,1)S(1)} %outer_sweep_south_2.1.refs_1_, f32[2,8,256]{2,1,0:T(8,128)S(1)} %copy-done.10, ...), custom_call_target="tpu_custom_call", output_to_operand_aliasing={{0}: (9, {}), {1}: (10, {})} | custom-call | flops 1358954496 | bytes 2359296 | tf_op jit(solution)/shard_map/second_source_0/pallas_call | solution.py:388
  (26 shorter events, 0.1 us)
Async XLA Ops:
  6.4 43.5 %collective-permute-start = (bf16[2,592,256]{2,1,0:T(8,128)(2,1)}, bf16[2,592,256]{2,1,0:T(8,128)(2,1)}, u32[]{:S(2)}, u32[]{:S(2)}) collective-permute-start(bf16[2,592,256]{2,1,0:T(8,128)(2,1)} %get-tuple-element.43.refs_4_), channel_id=1, source_target_pairs={{1,0},{2,1},{3,2},{4,3},{5,4},{6,5},{7,6},{8,7},{9,8},{10,9},{11,1... | collective-permute-start | bytes 1818632 | tf_op jit(solution)/shard_map/ppermute | solution.py:441
  12.8 9.0 %copy-start = (bf16[1152,1152]{1,0:T(8,128)(2,1)S(1)}, bf16[1152,1152]{1,0:T(8,128)(2,1)}, u32[]{:S(2)}) copy-start(bf16[1152,1152]{1,0:T(8,128)(2,1)} %refs_7_.11) | copy-start | bytes 7962628
  12.8 9.0 %copy-start.1 = (bf16[1152,10,256]{2,0,1:T(8,128)(2,1)S(1)}, bf16[1152,10,256]{2,0,1:T(8,128)(2,1)}, u32[]{:S(2)}) copy-start(bf16[1152,10,256]{2,0,1:T(8,128)(2,1)} %param.14) | copy-start | bytes 17694724
  12.8 9.0 %copy-start.2 = (f32[1152,128]{1,0:T(8,128)S(1)}, f32[1152,128]{1,0:T(8,128)}, u32[]{:S(2)}) copy-start(f32[1152,128]{1,0:T(8,128)} %get-tuple-element.45.refs_9_.refs_6_) | copy-start | bytes 1769476
  12.8 9.0 %copy-start.3 = (bf16[1152,128]{1,0:T(8,128)(2,1)S(1)}, bf16[1152,128]{1,0:T(8,128)(2,1)}, u32[]{:S(2)}) copy-start(bf16[1152,128]{1,0:T(8,128)(2,1)} %get-tuple-element.46.refs_10_.refs_11_.refs_8_) | copy-start | bytes 884740
  12.8 9.0 %copy-start.5 = (f32[1152,128]{1,0:T(8,128)S(1)}, f32[1152,128]{1,0:T(8,128)}, u32[]{:S(2)}) copy-start(f32[1152,128]{1,0:T(8,128)} %get-tuple-element.44.refs_8_) | copy-start | bytes 1769476
  12.9 9.0 %copy-start.6 = (s32[10,256]{1,0:T(8,128)S(1)}, s32[10,256]{1,0:T(8,128)}, u32[]{:S(2)}) copy-start(s32[10,256]{1,0:T(8,128)} %refs_1_.15) | copy-start | bytes 30724
  12.9 9.0 %copy-start.7 = (f32[10,256]{1,0:T(8,128)S(1)}, f32[10,256]{1,0:T(8,128)}, u32[]{:S(2)}) copy-start(f32[10,256]{1,0:T(8,128)} %refs_2_.15) | copy-start | bytes 30724
  12.9 9.0 %copy-start.8 = (s32[10,256]{1,0:T(8,128)S(1)}, s32[10,256]{1,0:T(8,128)}, u32[]{:S(2)}) copy-start(s32[10,256]{1,0:T(8,128)} %refs_3_.9) | copy-start | bytes 30724
  12.9 9.0 %copy-start.9 = (f32[10,256]{1,0:T(8,128)S(1)}, f32[10,256]{1,0:T(8,128)}, u32[]{:S(2)}) copy-start(f32[10,256]{1,0:T(8,128)} %refs_4_.9) | copy-start | bytes 30724
  12.9 8.9 %copy-start.12 = (f32[8]{0:T(128)S(1)}, f32[8]{0:T(128)}, u32[]{:S(2)}) copy-start(f32[8]{0:T(128)} %refs_5_.9) | copy-start | bytes 100
  12.9 8.9 %copy-start.14 = (s32[64]{0:T(128)S(1)}, s32[64]{0:T(128)}, u32[]{:S(2)}) copy-start(s32[64]{0:T(128)} %refs_6_.6) | copy-start | bytes 772
  19.0 11.6 %copy-start.18 = (f32[32]{0:T(128)S(1)}, f32[32]{0:T(128)}, u32[]{:S(2)}) copy-start(f32[32]{0:T(128)} %param.24) | copy-start | bytes 388
  19.0 11.6 %copy-start.4 = (bf16[2,576,256]{2,1,0:T(8,128)(2,1)S(1)}, bf16[2,576,256]{2,1,0:T(8,128)(2,1)}, u32[]{:S(2)}) copy-start(bf16[2,576,256]{2,1,0:T(8,128)(2,1)} %get-tuple-element.49.refs_4_) | copy-start | bytes 1769476
  19.0 11.6 %copy-start.13 = (f32[2,36]{1,0:T(2,128)S(1)}, f32[2,36]{1,0:T(2,128)}, u32[]{:S(2)}) copy-start(f32[2,36]{1,0:T(2,128)} %constant.5.clone.refs_0_) | copy-start | bytes 868
  19.1 11.6 %copy-start.17 = (bf16[2,576,256]{2,1,0:T(8,128)(2,1)S(1)}, bf16[2,576,256]{2,1,0:T(8,128)(2,1)}, u32[]{:S(2)}) copy-start(bf16[2,576,256]{2,1,0:T(8,128)(2,1)} %get-tuple-element.50.refs_5_) | copy-start | bytes 1769476
  19.1 30.8 %collective-permute-start.1 = (bf16[2,592,256]{2,1,0:T(8,128)(2,1)}, bf16[2,592,256]{2,1,0:T(8,128)(2,1)S(1)}, u32[]{:S(2)}, u32[]{:S(2)}) collective-permute-start(bf16[2,592,256]{2,1,0:T(8,128)(2,1)} %get-tuple-element.47.refs_5_), channel_id=1, source_target_pairs={{1,0},{2,1},{3,2},{4,3},{5,4},{6,5},{7,6},{8,7},{9,8},{10,9},{11,1... | collective-permute-start | bytes 1818632 | tf_op jit(solution)/shard_map/ppermute | solution.py:444
  30.7 10.3 %copy-start.15 = (bf16[2,592,256]{2,1,0:T(8,128)(2,1)S(1)}, bf16[2,592,256]{2,1,0:T(8,128)(2,1)}, u32[]{:S(2)}) copy-start(bf16[2,592,256]{2,1,0:T(8,128)(2,1)} %get-tuple-element.43.refs_4_) | copy-start | bytes 1818628
  30.7 10.3 %copy-start.16 = (bf16[2,592,256]{2,1,0:T(8,128)(2,1)S(1)}, bf16[2,592,256]{2,1,0:T(8,128)(2,1)}, u32[]{:S(2)}) copy-start(bf16[2,592,256]{2,1,0:T(8,128)(2,1)} %get-tuple-element.47.refs_5_) | copy-start | bytes 1818628
  37.5 25.6 %collective-permute-start.2 = (bf16[2,592,256]{2,1,0:T(8,128)(2,1)S(1)}, bf16[2,592,256]{2,1,0:T(8,128)(2,1)S(1)}, u32[]{:S(2)}, u32[]{:S(2)}) collective-permute-start(bf16[2,592,256]{2,1,0:T(8,128)(2,1)S(1)} %get-tuple-element.69.refs_8_), channel_id=1, source_target_pairs={{0,1},{1,2},{2,3},{3,4},{4,5},{5,6},{6,7},{7,8},{8,9},{9,10},{10,1... | collective-permute-start | bytes 1818632 | tf_op jit(solution)/shard_map/ppermute | solution.py:451
  47.7 23.8 %collective-permute-start.3 = (bf16[2,592,256]{2,1,0:T(8,128)(2,1)S(1)}, bf16[2,592,256]{2,1,0:T(8,128)(2,1)S(1)}, u32[]{:S(2)}, u32[]{:S(2)}) collective-permute-start(bf16[2,592,256]{2,1,0:T(8,128)(2,1)S(1)} %get-tuple-element.78.refs_7_), channel_id=1, source_target_pairs={{0,1},{1,2},{2,3},{3,4},{4,5},{5,6},{6,7},{7,8},{8,9},{9,10},{10,1... | collective-permute-start | bytes 1818632 | tf_op jit(solution)/shard_map/ppermute | solution.py:454
  63.0 3.0 %copy-start.11 = (f32[2,8,256]{2,1,0:T(8,128)S(1)}, f32[2,8,256]{2,1,0:T(8,128)}, u32[]{:S(2)}) copy-start(f32[2,8,256]{2,1,0:T(8,128)} %get-tuple-element.72.refs_2_) | copy-start | bytes 49156
  69.4 5.1 %copy-start.10 = (f32[2,8,256]{2,1,0:T(8,128)S(1)}, f32[2,8,256]{2,1,0:T(8,128)}, u32[]{:S(2)}) copy-start(f32[2,8,256]{2,1,0:T(8,128)} %get-tuple-element.79.refs_2_) | copy-start | bytes 49156

commit v5 on v4

--- a/solution.py
+++ b/solution.py
@@ -88,14 +88,18 @@
     sea, count, rate, held, x_near, jac_ref = refs[-7 - len(far) : -1 - len(far)]
     near, sems = refs[-1 - len(far) : -1], refs[-1]
     copies = [pltpu.make_async_copy(a, b, sems.at[i]) for i, (a, b) in enumerate(zip(far, near))]
-    waits = [pltpu.make_async_copy(jac_hbm, jac_ref, sems.at[len(far)])]
-    for i, pair in enumerate(pairs):
-        waits.append(
-            pltpu.make_async_copy(
-                x_ref.at[2 * pair : 2 * pair + 2], x_near.at[2 * i : 2 * i + 2], sems.at[len(far) + 1 + i]
-            )
+    chunks = [slice(m * 384, (m + 1) * 384) for m in range(3)]
+    jac_copies = [
+        pltpu.make_async_copy(jac_hbm.at[:, rows], jac_ref.at[:, rows], sems.at[len(far) + m])
+        for m, rows in enumerate(chunks)
+    ]
+    x_copies = [
+        pltpu.make_async_copy(
+            x_ref.at[2 * pair : 2 * pair + 2], x_near.at[2 * i : 2 * i + 2], sems.at[len(far) + 3 + i]
         )
-    for copy in copies + waits:
+        for i, pair in enumerate(pairs)
+    ]
+    for copy in copies + x_copies[:1] + jac_copies + x_copies[1:]:
         copy.start()
     for copy in copies:
         copy.wait()
@@ -112,10 +116,9 @@
     else:
         fw_ref, fd_ref, wave_ref = near[6:]
     point_fields(land_ref, depth_ref, outlets_ref, scale_ref, sea, count, rate)
-    waits[0].wait()
 
     for i, pair in enumerate(pairs):
-        waits[1 + i].wait()
+        x_copies[i].wait()
         to = 2 * i if opening else 0
         halves, wind_ref = (outs[:2], outs[2]) if opening else (outs[3 * i : 3 * i + 2], outs[3 * i + 2])
         fw = fw_ref[...]
@@ -128,8 +131,9 @@
             seeds.append(lone.astype(jnp.bfloat16))
             fields.append((rate[r, :], damp_ref[r, :]))
         spectrum = jnp.concatenate(seeds, axis=1)
-        for m in range(3):
-            rows = slice(m * 384, (m + 1) * 384)
+        for m, rows in enumerate(chunks):
+            if i == 0:
+                jac_copies[m].wait()
             mixed = contract(jac_ref[:, rows], spectrum)
             fd = fd_ref[rows, :]
             for piece in range(4):
@@ -172,7 +176,7 @@
     scratch += [pltpu.VMEM((2 * len(pairs), K, LON), jnp.bfloat16), pltpu.VMEM((K, K), jnp.bfloat16)]
     for at, a in enumerate(small):
         scratch.append((pltpu.SMEM if at in (4, 5) else pltpu.VMEM)(a.shape, a.dtype))
-    scratch.append(pltpu.SemaphoreType.DMA((len(small) + 1 + len(pairs),)))
+    scratch.append(pltpu.SemaphoreType.DMA((len(small) + 3 + len(pairs),)))
 
     def body(*refs):
         first_kernel(pairs, *refs)

time: 78.2 us -> 79.9 us (1.022)
  Pallas kernels: 59.9 us -> 61.6 us
    pallas_call x3, Pallas kernels: 20.6 us -> 22.3 us  [first_source(): pl.pallas_call(body, in_specs=[pl.BlockSpec(memory_space=pl.ANY)] * (2 +...]
  transfers between devices with their start and end apart: 4 -> 4, of which waited for: 1 -> 1; matrix products, arithmetic and copies ran while one was open for 0% -> 0% of each run, Pallas kernels for 61% -> 62%
where the time goes in v5:
time: 79.9 us; the launch traced here: 79.7 us
  Pallas kernels  61.6 us (77%)
  starting transfers between devices  14.7 us (18%)
  waiting for transfers between devices  2.15 us (3%)
  between operations  1.01 us (1%)
    pallas_call x3, Pallas kernels, first_source(): pl.pallas_call(body, in_specs=[pl.BlockSpec(memory_space=pl.ANY)] * (2 +...  22.3 us
    pallas_call x3, Pallas kernels, second_source(): pl.pallas_call(body, grid=(len(jobs),), in_specs=[held_whole()] * (len(so...  14.7 us
    pallas_call x2, Pallas kernels, inner_sweep(): pl.pallas_call(body, in_specs=[smem()] + [held_whole()] * (3 + len(source...  13.5 us
    pallas_call x3, Pallas kernels, outer_sweep(): pl.pallas_call(body, in_specs=[smem()] + [held_whole()] * (5 + len(halos)...  11.2 us
    ppermute x1, starting transfers between devices, body(): halo_n = [lax.ppermute(n[0], AXES, down)]  6.39 us
    ppermute x1, starting transfers between devices, body(): halo_s[0] = lax.ppermute(s[4], AXES, up)  3.47 us
    ppermute x1, starting transfers between devices, body(): halo_n.append(lax.ppermute(n[1], AXES, down))  2.69 us
    ppermute x1, waiting for transfers between devices, body(): halo_s[1] = lax.ppermute(s[3], AXES, up)  2.14 us
  transfers between devices with their start and end apart: 4, of which 1 were waited for; matrix products, arithmetic and copies ran while one was open for 0% of the time, Pallas kernels for 62%

profile of v5, /device:TPU:96, one launch (start us, length us, event | category | flops | bytes accessed | tf_op | source)
XLA Modules:
  0.0 79.7 jit_solution(10360311414332367316)
XLA Ops:
  0.6 6.2 %first_source_0.1 = (f32[1152,128]{1,0:T(8,128)}, f32[1152,128]{1,0:T(8,128)}, bf16[1152,128]{1,0:T(8,128)(2,1)}, bf16[2,592,256]{2,1,0:T(8,128)(2,1)}, bf16[2,5...) custom-call(bf16[10,1152,256]{2,1,0:T(8,128)(2,1)} %bitcast.3, bf16[1152,1152]{1,0:T(8,128)(2,1)} %refs_7_.11, ...), custom_call_target="tpu_custom_call" | custom-call | flops 1358954496 | bytes 2359296 | tf_op jit(solution)/shard_map/first_source_0/pallas_call | solution.py:184
  6.8 6.4 %collective-permute-start = (bf16[2,592,256]{2,1,0:T(8,128)(2,1)}, bf16[2,592,256]{2,1,0:T(8,128)(2,1)}, u32[]{:S(2)}, u32[]{:S(2)}) collective-permute-start(bf16[2,592,256]{2,1,0:T(8,128)(2,1)} %get-tuple-element.43.refs_4_), channel_id=1, source_target_pairs={{1,0},{2,1},{3,2},{4,3},{5,4},{6,5},{7,6},{8,7},{9,8},{10,9},{11,1... | collective-permute-start | bytes 1818632 | tf_op jit(solution)/shard_map/ppermute | solution.py:445
  13.2 0.0 copy-start
  13.2 0.0 copy-start.1
  13.3 0.0 copy-start.6
  13.3 0.0 copy-start.7
  13.3 0.0 copy-start.8
  13.3 0.0 copy-start.9
  13.3 0.0 copy-start.12
  13.3 0.0 copy-start.14
  13.3 6.3 %first_source_1.1 = (bf16[2,592,256]{2,1,0:T(8,128)(2,1)}, bf16[2,576,256]{2,1,0:T(8,128)(2,1)}, f32[2,8,256]{2,1,0:T(8,128)}) custom-call(bf16[10,1152,256]{2,1,0:T(8,128)(2,1)} %bitcast.4, bf16[1152,1152]{1,0:T(8,128)(2,1)} %refs_7_.11, s32[10,256]{1,0:T(8,128)} %refs_1_.15, s32[10,256]{1,0:T(8,128)} %refs_3_.9, f32[10,256]{1,0:T(8,128)} %refs_4_.9, ...), custom_call_target="tpu_custom_call" | custom-call | flops 1358954496 | bytes 2359296 | tf_op jit(solution)/shard_map/first_source_1/pallas_call | solution.py:184
  19.6 0.0 copy-start.18
  19.6 0.0 copy-start.13
  19.7 2.7 %collective-permute-start.1 = (bf16[2,592,256]{2,1,0:T(8,128)(2,1)}, bf16[2,592,256]{2,1,0:T(8,128)(2,1)S(1)}, u32[]{:S(2)}, u32[]{:S(2)}) collective-permute-start(bf16[2,592,256]{2,1,0:T(8,128)(2,1)} %get-tuple-element.47.refs_5_), channel_id=1, source_target_pairs={{1,0},{2,1},{3,2},{4,3},{5,4},{6,5},{7,6},{8,7},{9,8},{10,9},{11,1... | collective-permute-start | bytes 1818632 | tf_op jit(solution)/shard_map/ppermute | solution.py:448
  22.5 9.8 %first_source_4.1 = (bf16[2,576,256]{2,1,0:T(8,128)(2,1)S(1)}, bf16[2,592,256]{2,1,0:T(8,128)(2,1)S(1)}, f32[2,8,256]{2,1,0:T(8,128)S(1)}, bf16[2,576,256]{2,1,0...) custom-call(bf16[10,1152,256]{2,1,0:T(8,128)(2,1)S(1)} %bitcast.5, ...), custom_call_target="tpu_custom_call" | custom-call | flops 4076863488 | bytes 7077888 | tf_op jit(solution)/shard_map/first_source_4/pallas_call | solution.py:184
  32.3 0.1 broadcast_in_dim.2.refs_3_
  32.4 0.0 copy-done.13
  32.4 0.0 copy-start.15
  32.4 6.7 %inner_sweep_south.1 = (bf16[6,576,256]{2,1,0:T(8,128)(2,1)S(1)}, f32[3,576,256]{2,1,0:T(8,128)S(1)}) custom-call(f32[2,36]{1,0:T(2,128)S(1)} %copy-done.13, s32[10,256]{1,0:T(8,128)S(1)} %copy-done.6, f32[10,256]{1,0:T(8,128)S(1)} %copy-done.7, f32[32,128]{1,0:T(8,128)S(1)} %broadcast_in_dim.2.refs_3_, bf16[2,576,256]{2,1,0:T(8,128)(2,1)S(1)} %copy-done.4, ...), custom_call_target="tpu_custom_call" | custom-call | flops 2477260800 | bytes 17694720 | tf_op jit(solution)/shard_map/inner_sweep_south/pallas_call | solution.py:274
  39.2 3.5 %collective-permute-start.2 = (bf16[2,592,256]{2,1,0:T(8,128)(2,1)S(1)}, bf16[2,592,256]{2,1,0:T(8,128)(2,1)S(1)}, u32[]{:S(2)}, u32[]{:S(2)}) collective-permute-start(bf16[2,592,256]{2,1,0:T(8,128)(2,1)S(1)} %get-tuple-element.69.refs_8_), channel_id=1, source_target_pairs={{0,1},{1,2},{2,3},{3,4},{4,5},{5,6},{6,7},{7,8},{8,9},{9,10},{10,1... | collective-permute-start | bytes 1818632 | tf_op jit(solution)/shard_map/ppermute | solution.py:455
  42.7 6.8 %inner_sweep_north.1 = (bf16[6,576,256]{2,1,0:T(8,128)(2,1)S(1)}, f32[3,576,256]{2,1,0:T(8,128)S(1)}) custom-call(f32[2,36]{1,0:T(2,128)S(1)} %copy-done.13, s32[10,256]{1,0:T(8,128)S(1)} %copy-done.6, f32[10,256]{1,0:T(8,128)S(1)} %copy-done.7, f32[32,128]{1,0:T(8,128)S(1)} %broadcast_in_dim.2.refs_3_, bf16[2,592,256]{2,1,0:T(8,128)(2,1)S(1)} %copy-done.15, ...), custom_call_target="tpu_custom_call" | custom-call | flops 2477260800 | bytes 17694720 | tf_op jit(solution)/shard_map/inner_sweep_north/pallas_call | solution.py:274
  49.4 2.1 %collective-permute-start.3 = (bf16[2,592,256]{2,1,0:T(8,128)(2,1)S(1)}, bf16[2,592,256]{2,1,0:T(8,128)(2,1)S(1)}, u32[]{:S(2)}, u32[]{:S(2)}) collective-permute-start(bf16[2,592,256]{2,1,0:T(8,128)(2,1)S(1)} %get-tuple-element.78.refs_7_), channel_id=1, source_target_pairs={{0,1},{1,2},{2,3},{3,4},{4,5},{5,6},{6,7},{7,8},{8,9},{9,10},{10,1... | collective-permute-start | bytes 1818632 | tf_op jit(solution)/shard_map/ppermute | solution.py:458
  51.6 0.0 collective-permute-done.refs_6_
  51.6 0.0 collective-permute-done.1.refs_7_
  51.6 5.3 %outer_sweep_north_0.1.refs_1_ = bf16[4,576,256]{2,1,0:T(8,128)(2,1)S(1)} custom-call(f32[2,36]{1,0:T(2,128)S(1)} %copy-done.13, s32[10,256]{1,0:T(8,128)S(1)} %copy-done.6, f32[10,256]{1,0:T(8,128)S(1)} %copy-done.7, f32[32,128]{1,0:T(8,128)S(1)} %broadcast_in_dim.2.refs_3_, bf16[2,576,256]{2,1,0:T(8,128)(2,1)S(1)} %get-tuple-element.57.refs_8_.refs_4_, ...), custom_call_target="tpu_custom_call" | custom-call | flops 1321205760 | bytes 14745600 | tf_op jit(solution)/shard_map/outer_sweep_north_0/pallas_call | solution.py:331
  56.9 7.8 %second_source_2.1 = (bf16[10,1152,256]{2,1,0:T(8,128)(2,1)}, f32[10,2,256]{2,1,0:T(2,128)}) custom-call(bf16[6,576,256]{2,1,0:T(8,128)(2,1)S(1)} %get-tuple-element.58.refs_0_, bf16[4,576,256]{2,1,0:T(8,128)(2,1)S(1)} %outer_sweep_north_0.1.refs_1_, bf16[6,576,256]{2,1,0:T(8,128)(2,1)S(1)} %get-tuple-element.62.refs_2_, ...), custom_call_target="tpu_custom_call" | custom-call | flops 4076863488 | bytes 7077888 | tf_op jit(solution)/shard_map/second_source_2/pallas_call | solution.py:392
  64.7 0.0 collective-permute-done.2.refs_6_
  64.7 2.9 %outer_sweep_south_0.1 = (bf16[2,576,256]{2,1,0:T(8,128)(2,1)S(1)}, f32[3,576,256]{2,1,0:T(8,128)S(1)}) custom-call(f32[2,36]{1,0:T(2,128)S(1)} %copy-done.13, s32[10,256]{1,0:T(8,128)S(1)} %copy-done.6, f32[10,256]{1,0:T(8,128)S(1)} %copy-done.7, f32[32,128]{1,0:T(8,128)S(1)} %broadcast_in_dim.2.refs_3_, bf16[2,576,256]{2,1,0:T(8,128)(2,1)S(1)} %copy-done.4, ...), custom_call_target="tpu_custom_call" | custom-call | flops 660602880 | bytes 14745600 | tf_op jit(solution)/shard_map/outer_sweep_south_0/pallas_call | solution.py:331
  67.7 3.4 %second_source_1.1 = (bf16[10,1152,256]{2,1,0:T(8,128)(2,1)}, f32[10,2,256]{2,1,0:T(2,128)}) custom-call(bf16[6,576,256]{2,1,0:T(8,128)(2,1)S(1)} %get-tuple-element.58.refs_0_, bf16[2,576,256]{2,1,0:T(8,128)(2,1)S(1)} %get-tuple-element.71.refs_1_, f32[2,8,256]{2,1,0:T(8,128)S(1)} %copy-done.11, ...), custom_call_target="tpu_custom_call", output_to_operand_aliasing={{0}: (9, {}), {1}: (10, {})} | custom-call | flops 1358954496 | bytes 2359296 | tf_op jit(solution)/shard_map/second_source_1/pallas_call | solution.py:392
  71.1 2.1 %collective-permute-done.3.refs_7_ = bf16[2,592,256]{2,1,0:T(8,128)(2,1)S(1)} collective-permute-done((bf16[2,592,256]{2,1,0:T(8,128)(2,1)S(1)}, bf16[2,592,256]{2,1,0:T(8,128)(2,1)S(1)}, u32[]{:S(2)}, u32[]{:S(2)}) %collective-permute-start.3) | collective-permute-done | bytes 606240 | tf_op jit(solution)/shard_map/ppermute | solution.py:458
  73.3 2.9 %outer_sweep_south_2.1.refs_1_ = bf16[2,576,256]{2,1,0:T(8,128)(2,1)S(1)} custom-call(f32[2,36]{1,0:T(2,128)S(1)} %copy-done.13, s32[10,256]{1,0:T(8,128)S(1)} %copy-done.6, f32[10,256]{1,0:T(8,128)S(1)} %copy-done.7, f32[32,128]{1,0:T(8,128)S(1)} %broadcast_in_dim.2.refs_3_, bf16[2,576,256]{2,1,0:T(8,128)(2,1)S(1)} %copy-done.4, ...), custom_call_target="tpu_custom_call" | custom-call | flops 660602880 | bytes 14745600 | tf_op jit(solution)/shard_map/outer_sweep_south_2/pallas_call | solution.py:331
  76.2 3.4 %second_source_0.1 = (bf16[10,1152,256]{2,1,0:T(8,128)(2,1)}, f32[10,2,256]{2,1,0:T(2,128)}) custom-call(bf16[6,576,256]{2,1,0:T(8,128)(2,1)S(1)} %get-tuple-element.58.refs_0_, bf16[2,576,256]{2,1,0:T(8,128)(2,1)S(1)} %outer_sweep_south_2.1.refs_1_, f32[2,8,256]{2,1,0:T(8,128)S(1)} %copy-done.10, ...), custom_call_target="tpu_custom_call", output_to_operand_aliasing={{0}: (9, {}), {1}: (10, {})} | custom-call | flops 1358954496 | bytes 2359296 | tf_op jit(solution)/shard_map/second_source_0/pallas_call | solution.py:392
  (26 shorter events, 0.1 us)
Async XLA Ops:
  6.8 44.8 %collective-permute-start = (bf16[2,592,256]{2,1,0:T(8,128)(2,1)}, bf16[2,592,256]{2,1,0:T(8,128)(2,1)}, u32[]{:S(2)}, u32[]{:S(2)}) collective-permute-start(bf16[2,592,256]{2,1,0:T(8,128)(2,1)} %get-tuple-element.43.refs_4_), channel_id=1, source_target_pairs={{1,0},{2,1},{3,2},{4,3},{5,4},{6,5},{7,6},{8,7},{9,8},{10,9},{11,1... | collective-permute-start | bytes 1818632 | tf_op jit(solution)/shard_map/ppermute | solution.py:445
  13.2 9.1 %copy-start = (bf16[1152,1152]{1,0:T(8,128)(2,1)S(1)}, bf16[1152,1152]{1,0:T(8,128)(2,1)}, u32[]{:S(2)}) copy-start(bf16[1152,1152]{1,0:T(8,128)(2,1)} %refs_7_.11) | copy-start | bytes 7962628
  13.2 9.1 %copy-start.1 = (bf16[1152,10,256]{2,0,1:T(8,128)(2,1)S(1)}, bf16[1152,10,256]{2,0,1:T(8,128)(2,1)}, u32[]{:S(2)}) copy-start(bf16[1152,10,256]{2,0,1:T(8,128)(2,1)} %param.14) | copy-start | bytes 17694724
  13.2 9.1 %copy-start.2 = (f32[1152,128]{1,0:T(8,128)S(1)}, f32[1152,128]{1,0:T(8,128)}, u32[]{:S(2)}) copy-start(f32[1152,128]{1,0:T(8,128)} %get-tuple-element.45.refs_9_.refs_6_) | copy-start | bytes 1769476
  13.3 9.1 %copy-start.3 = (bf16[1152,128]{1,0:T(8,128)(2,1)S(1)}, bf16[1152,128]{1,0:T(8,128)(2,1)}, u32[]{:S(2)}) copy-start(bf16[1152,128]{1,0:T(8,128)(2,1)} %get-tuple-element.46.refs_10_.refs_11_.refs_8_) | copy-start | bytes 884740
  13.3 9.1 %copy-start.5 = (f32[1152,128]{1,0:T(8,128)S(1)}, f32[1152,128]{1,0:T(8,128)}, u32[]{:S(2)}) copy-start(f32[1152,128]{1,0:T(8,128)} %get-tuple-element.44.refs_8_) | copy-start | bytes 1769476
  13.3 9.1 %copy-start.6 = (s32[10,256]{1,0:T(8,128)S(1)}, s32[10,256]{1,0:T(8,128)}, u32[]{:S(2)}) copy-start(s32[10,256]{1,0:T(8,128)} %refs_1_.15) | copy-start | bytes 30724
  13.3 9.1 %copy-start.7 = (f32[10,256]{1,0:T(8,128)S(1)}, f32[10,256]{1,0:T(8,128)}, u32[]{:S(2)}) copy-start(f32[10,256]{1,0:T(8,128)} %refs_2_.15) | copy-start | bytes 30724
  13.3 9.1 %copy-start.8 = (s32[10,256]{1,0:T(8,128)S(1)}, s32[10,256]{1,0:T(8,128)}, u32[]{:S(2)}) copy-start(s32[10,256]{1,0:T(8,128)} %refs_3_.9) | copy-start | bytes 30724
  13.3 9.1 %copy-start.9 = (f32[10,256]{1,0:T(8,128)S(1)}, f32[10,256]{1,0:T(8,128)}, u32[]{:S(2)}) copy-start(f32[10,256]{1,0:T(8,128)} %refs_4_.9) | copy-start | bytes 30724
  13.3 9.1 %copy-start.12 = (f32[8]{0:T(128)S(1)}, f32[8]{0:T(128)}, u32[]{:S(2)}) copy-start(f32[8]{0:T(128)} %refs_5_.9) | copy-start | bytes 100
  13.3 9.1 %copy-start.14 = (s32[64]{0:T(128)S(1)}, s32[64]{0:T(128)}, u32[]{:S(2)}) copy-start(s32[64]{0:T(128)} %refs_6_.6) | copy-start | bytes 772
  19.6 12.7 %copy-start.18 = (f32[32]{0:T(128)S(1)}, f32[32]{0:T(128)}, u32[]{:S(2)}) copy-start(f32[32]{0:T(128)} %param.24) | copy-start | bytes 388
  19.6 12.8 %copy-start.4 = (bf16[2,576,256]{2,1,0:T(8,128)(2,1)S(1)}, bf16[2,576,256]{2,1,0:T(8,128)(2,1)}, u32[]{:S(2)}) copy-start(bf16[2,576,256]{2,1,0:T(8,128)(2,1)} %get-tuple-element.49.refs_4_) | copy-start | bytes 1769476
  19.6 12.8 %copy-start.13 = (f32[2,36]{1,0:T(2,128)S(1)}, f32[2,36]{1,0:T(2,128)}, u32[]{:S(2)}) copy-start(f32[2,36]{1,0:T(2,128)} %constant.5.clone.refs_0_) | copy-start | bytes 868
  19.7 12.7 %copy-start.17 = (bf16[2,576,256]{2,1,0:T(8,128)(2,1)S(1)}, bf16[2,576,256]{2,1,0:T(8,128)(2,1)}, u32[]{:S(2)}) copy-start(bf16[2,576,256]{2,1,0:T(8,128)(2,1)} %get-tuple-element.50.refs_5_) | copy-start | bytes 1769476
  19.7 31.9 %collective-permute-start.1 = (bf16[2,592,256]{2,1,0:T(8,128)(2,1)}, bf16[2,592,256]{2,1,0:T(8,128)(2,1)S(1)}, u32[]{:S(2)}, u32[]{:S(2)}) collective-permute-start(bf16[2,592,256]{2,1,0:T(8,128)(2,1)} %get-tuple-element.47.refs_5_), channel_id=1, source_target_pairs={{1,0},{2,1},{3,2},{4,3},{5,4},{6,5},{7,6},{8,7},{9,8},{10,9},{11,1... | collective-permute-start | bytes 1818632 | tf_op jit(solution)/shard_map/ppermute | solution.py:448
  32.4 10.3 %copy-start.15 = (bf16[2,592,256]{2,1,0:T(8,128)(2,1)S(1)}, bf16[2,592,256]{2,1,0:T(8,128)(2,1)}, u32[]{:S(2)}) copy-start(bf16[2,592,256]{2,1,0:T(8,128)(2,1)} %get-tuple-element.43.refs_4_) | copy-start | bytes 1818628
  32.4 10.2 %copy-start.16 = (bf16[2,592,256]{2,1,0:T(8,128)(2,1)S(1)}, bf16[2,592,256]{2,1,0:T(8,128)(2,1)}, u32[]{:S(2)}) copy-start(bf16[2,592,256]{2,1,0:T(8,128)(2,1)} %get-tuple-element.47.refs_5_) | copy-start | bytes 1818628
  39.2 25.6 %collective-permute-start.2 = (bf16[2,592,256]{2,1,0:T(8,128)(2,1)S(1)}, bf16[2,592,256]{2,1,0:T(8,128)(2,1)S(1)}, u32[]{:S(2)}, u32[]{:S(2)}) collective-permute-start(bf16[2,592,256]{2,1,0:T(8,128)(2,1)S(1)} %get-tuple-element.69.refs_8_), channel_id=1, source_target_pairs={{0,1},{1,2},{2,3},{3,4},{4,5},{5,6},{6,7},{7,8},{8,9},{9,10},{10,1... | collective-permute-start | bytes 1818632 | tf_op jit(solution)/shard_map/ppermute | solution.py:455
  49.4 23.8 %collective-permute-start.3 = (bf16[2,592,256]{2,1,0:T(8,128)(2,1)S(1)}, bf16[2,592,256]{2,1,0:T(8,128)(2,1)S(1)}, u32[]{:S(2)}, u32[]{:S(2)}) collective-permute-start(bf16[2,592,256]{2,1,0:T(8,128)(2,1)S(1)} %get-tuple-element.78.refs_7_), channel_id=1, source_target_pairs={{0,1},{1,2},{2,3},{3,4},{4,5},{5,6},{6,7},{7,8},{8,9},{9,10},{10,1... | collective-permute-start | bytes 1818632 | tf_op jit(solution)/shard_map/ppermute | solution.py:458
  64.7 3.0 %copy-start.11 = (f32[2,8,256]{2,1,0:T(8,128)S(1)}, f32[2,8,256]{2,1,0:T(8,128)}, u32[]{:S(2)}) copy-start(f32[2,8,256]{2,1,0:T(8,128)} %get-tuple-element.72.refs_2_) | copy-start | bytes 49156
  71.1 5.1 %copy-start.10 = (f32[2,8,256]{2,1,0:T(8,128)S(1)}, f32[2,8,256]{2,1,0:T(8,128)}, u32[]{:S(2)}) copy-start(f32[2,8,256]{2,1,0:T(8,128)} %get-tuple-element.79.refs_2_) | copy-start | bytes 49156

commit v6 on v4

--- a/solution.py
+++ b/solution.py
@@ -112,7 +112,6 @@
     else:
         fw_ref, fd_ref, wave_ref = near[6:]
     point_fields(land_ref, depth_ref, outlets_ref, scale_ref, sea, count, rate)
-    waits[0].wait()
 
     for i, pair in enumerate(pairs):
         waits[1 + i].wait()
@@ -128,6 +127,8 @@
             seeds.append(lone.astype(jnp.bfloat16))
             fields.append((rate[r, :], damp_ref[r, :]))
         spectrum = jnp.concatenate(seeds, axis=1)
+        if i == 0:
+            waits[0].wait()
         for m in range(3):
             rows = slice(m * 384, (m + 1) * 384)
             mixed = contract(jac_ref[:, rows], spectrum)

time: 78.2 us -> 80.1 us (1.024)
  Pallas kernels: 59.9 us -> 61.8 us
    pallas_call x3, Pallas kernels: 20.6 us -> 22.4 us  [first_source(): pl.pallas_call(body, in_specs=[pl.BlockSpec(memory_space=pl.ANY)] * (2 +...]
where the time goes in v6:
time: 80.1 us; the launch traced here: 79.8 us
  Pallas kernels  61.8 us (77%)
  starting transfers between devices  14.7 us (18%)
  waiting for transfers between devices  2.18 us (3%)
  between operations  1.01 us (1%)
    pallas_call x3, Pallas kernels, first_source(): pl.pallas_call(body, in_specs=[pl.BlockSpec(memory_space=pl.ANY)] * (2 +...  22.4 us
    pallas_call x3, Pallas kernels, second_source(): pl.pallas_call(body, grid=(len(jobs),), in_specs=[held_whole()] * (len(so...  14.7 us
    pallas_call x2, Pallas kernels, inner_sweep(): pl.pallas_call(body, in_specs=[smem()] + [held_whole()] * (3 + len(source...  13.5 us
    pallas_call x3, Pallas kernels, outer_sweep(): pl.pallas_call(body, in_specs=[smem()] + [held_whole()] * (5 + len(halos)...  11.2 us
    ppermute x1, starting transfers between devices, body(): halo_n = [lax.ppermute(n[0], AXES, down)]  6.4 us
    ppermute x1, starting transfers between devices, body(): halo_s[0] = lax.ppermute(s[4], AXES, up)  3.46 us
    ppermute x1, starting transfers between devices, body(): halo_n.append(lax.ppermute(n[1], AXES, down))  2.68 us
    ppermute x1, waiting for transfers between devices, body(): halo_s[1] = lax.ppermute(s[3], AXES, up)  2.17 us
  transfers between devices with their start and end apart: 4, of which 1 were waited for; matrix products, arithmetic and copies ran while one was open for 0% of the time, Pallas kernels for 61%

profile of v6, /device:TPU:96, one launch (start us, length us, event | category | flops | bytes accessed | tf_op | source)
XLA Modules:
  0.0 79.8 jit_solution(8356174163881035024)
XLA Ops:
  0.6 6.4 %first_source_0.1 = (f32[1152,128]{1,0:T(8,128)}, f32[1152,128]{1,0:T(8,128)}, bf16[1152,128]{1,0:T(8,128)(2,1)}, bf16[2,592,256]{2,1,0:T(8,128)(2,1)}, bf16[2,5...) custom-call(bf16[10,1152,256]{2,1,0:T(8,128)(2,1)} %bitcast.3, bf16[1152,1152]{1,0:T(8,128)(2,1)} %refs_7_.11, ...), custom_call_target="tpu_custom_call" | custom-call | flops 1358954496 | bytes 2359296 | tf_op jit(solution)/shard_map/first_source_0/pallas_call | solution.py:181
  7.0 6.4 %collective-permute-start = (bf16[2,592,256]{2,1,0:T(8,128)(2,1)}, bf16[2,592,256]{2,1,0:T(8,128)(2,1)}, u32[]{:S(2)}, u32[]{:S(2)}) collective-permute-start(bf16[2,592,256]{2,1,0:T(8,128)(2,1)} %get-tuple-element.43.refs_4_), channel_id=1, source_target_pairs={{1,0},{2,1},{3,2},{4,3},{5,4},{6,5},{7,6},{8,7},{9,8},{10,9},{11,1... | collective-permute-start | bytes 1818632 | tf_op jit(solution)/shard_map/ppermute | solution.py:442
  13.4 0.0 copy-start
  13.4 0.0 copy-start.1
  13.5 0.0 copy-start.6
  13.5 0.0 copy-start.7
  13.5 0.0 copy-start.8
  13.5 0.0 copy-start.9
  13.5 0.0 copy-start.12
  13.5 0.0 copy-start.14
  13.5 6.7 %first_source_1.1 = (bf16[2,592,256]{2,1,0:T(8,128)(2,1)}, bf16[2,576,256]{2,1,0:T(8,128)(2,1)}, f32[2,8,256]{2,1,0:T(8,128)}) custom-call(bf16[10,1152,256]{2,1,0:T(8,128)(2,1)} %bitcast.4, bf16[1152,1152]{1,0:T(8,128)(2,1)} %refs_7_.11, s32[10,256]{1,0:T(8,128)} %refs_1_.15, s32[10,256]{1,0:T(8,128)} %refs_3_.9, f32[10,256]{1,0:T(8,128)} %refs_4_.9, ...), custom_call_target="tpu_custom_call" | custom-call | flops 1358954496 | bytes 2359296 | tf_op jit(solution)/shard_map/first_source_1/pallas_call | solution.py:181
  20.2 0.0 copy-start.18
  20.2 0.0 copy-start.13
  20.3 0.0 copy-start.17
  20.3 2.7 %collective-permute-start.1 = (bf16[2,592,256]{2,1,0:T(8,128)(2,1)}, bf16[2,592,256]{2,1,0:T(8,128)(2,1)S(1)}, u32[]{:S(2)}, u32[]{:S(2)}) collective-permute-start(bf16[2,592,256]{2,1,0:T(8,128)(2,1)} %get-tuple-element.47.refs_5_), channel_id=1, source_target_pairs={{1,0},{2,1},{3,2},{4,3},{5,4},{6,5},{7,6},{8,7},{9,8},{10,9},{11,1... | collective-permute-start | bytes 1818632 | tf_op jit(solution)/shard_map/ppermute | solution.py:445
  23.1 9.4 %first_source_4.1 = (bf16[2,576,256]{2,1,0:T(8,128)(2,1)S(1)}, bf16[2,592,256]{2,1,0:T(8,128)(2,1)S(1)}, f32[2,8,256]{2,1,0:T(8,128)S(1)}, bf16[2,576,256]{2,1,0...) custom-call(bf16[10,1152,256]{2,1,0:T(8,128)(2,1)S(1)} %bitcast.5, ...), custom_call_target="tpu_custom_call" | custom-call | flops 4076863488 | bytes 7077888 | tf_op jit(solution)/shard_map/first_source_4/pallas_call | solution.py:181
  32.5 0.1 broadcast_in_dim.2.refs_3_
  32.5 0.0 copy-start.15
  32.6 6.7 %inner_sweep_south.1 = (bf16[6,576,256]{2,1,0:T(8,128)(2,1)S(1)}, f32[3,576,256]{2,1,0:T(8,128)S(1)}) custom-call(f32[2,36]{1,0:T(2,128)S(1)} %copy-done.13, s32[10,256]{1,0:T(8,128)S(1)} %copy-done.6, f32[10,256]{1,0:T(8,128)S(1)} %copy-done.7, f32[32,128]{1,0:T(8,128)S(1)} %broadcast_in_dim.2.refs_3_, bf16[2,576,256]{2,1,0:T(8,128)(2,1)S(1)} %copy-done.4, ...), custom_call_target="tpu_custom_call" | custom-call | flops 2477260800 | bytes 17694720 | tf_op jit(solution)/shard_map/inner_sweep_south/pallas_call | solution.py:271
  39.3 3.5 %collective-permute-start.2 = (bf16[2,592,256]{2,1,0:T(8,128)(2,1)S(1)}, bf16[2,592,256]{2,1,0:T(8,128)(2,1)S(1)}, u32[]{:S(2)}, u32[]{:S(2)}) collective-permute-start(bf16[2,592,256]{2,1,0:T(8,128)(2,1)S(1)} %get-tuple-element.69.refs_8_), channel_id=1, source_target_pairs={{0,1},{1,2},{2,3},{3,4},{4,5},{5,6},{6,7},{7,8},{8,9},{9,10},{10,1... | collective-permute-start | bytes 1818632 | tf_op jit(solution)/shard_map/ppermute | solution.py:452
  42.8 6.8 %inner_sweep_north.1 = (bf16[6,576,256]{2,1,0:T(8,128)(2,1)S(1)}, f32[3,576,256]{2,1,0:T(8,128)S(1)}) custom-call(f32[2,36]{1,0:T(2,128)S(1)} %copy-done.13, s32[10,256]{1,0:T(8,128)S(1)} %copy-done.6, f32[10,256]{1,0:T(8,128)S(1)} %copy-done.7, f32[32,128]{1,0:T(8,128)S(1)} %broadcast_in_dim.2.refs_3_, bf16[2,592,256]{2,1,0:T(8,128)(2,1)S(1)} %copy-done.15, ...), custom_call_target="tpu_custom_call" | custom-call | flops 2477260800 | bytes 17694720 | tf_op jit(solution)/shard_map/inner_sweep_north/pallas_call | solution.py:271
  49.6 2.1 %collective-permute-start.3 = (bf16[2,592,256]{2,1,0:T(8,128)(2,1)S(1)}, bf16[2,592,256]{2,1,0:T(8,128)(2,1)S(1)}, u32[]{:S(2)}, u32[]{:S(2)}) collective-permute-start(bf16[2,592,256]{2,1,0:T(8,128)(2,1)S(1)} %get-tuple-element.78.refs_7_), channel_id=1, source_target_pairs={{0,1},{1,2},{2,3},{3,4},{4,5},{5,6},{6,7},{7,8},{8,9},{9,10},{10,1... | collective-permute-start | bytes 1818632 | tf_op jit(solution)/shard_map/ppermute | solution.py:455
  51.7 0.0 collective-permute-done.refs_6_
  51.7 0.0 collective-permute-done.1.refs_7_
  51.7 5.3 %outer_sweep_north_0.1.refs_1_ = bf16[4,576,256]{2,1,0:T(8,128)(2,1)S(1)} custom-call(f32[2,36]{1,0:T(2,128)S(1)} %copy-done.13, s32[10,256]{1,0:T(8,128)S(1)} %copy-done.6, f32[10,256]{1,0:T(8,128)S(1)} %copy-done.7, f32[32,128]{1,0:T(8,128)S(1)} %broadcast_in_dim.2.refs_3_, bf16[2,576,256]{2,1,0:T(8,128)(2,1)S(1)} %get-tuple-element.57.refs_8_.refs_4_, ...), custom_call_target="tpu_custom_call" | custom-call | flops 1321205760 | bytes 14745600 | tf_op jit(solution)/shard_map/outer_sweep_north_0/pallas_call | solution.py:328
  57.1 7.8 %second_source_2.1 = (bf16[10,1152,256]{2,1,0:T(8,128)(2,1)}, f32[10,2,256]{2,1,0:T(2,128)}) custom-call(bf16[6,576,256]{2,1,0:T(8,128)(2,1)S(1)} %get-tuple-element.58.refs_0_, bf16[4,576,256]{2,1,0:T(8,128)(2,1)S(1)} %outer_sweep_north_0.1.refs_1_, bf16[6,576,256]{2,1,0:T(8,128)(2,1)S(1)} %get-tuple-element.62.refs_2_, ...), custom_call_target="tpu_custom_call" | custom-call | flops 4076863488 | bytes 7077888 | tf_op jit(solution)/shard_map/second_source_2/pallas_call | solution.py:389
  64.9 0.0 collective-permute-done.2.refs_6_
  64.9 2.9 %outer_sweep_south_0.1 = (bf16[2,576,256]{2,1,0:T(8,128)(2,1)S(1)}, f32[3,576,256]{2,1,0:T(8,128)S(1)}) custom-call(f32[2,36]{1,0:T(2,128)S(1)} %copy-done.13, s32[10,256]{1,0:T(8,128)S(1)} %copy-done.6, f32[10,256]{1,0:T(8,128)S(1)} %copy-done.7, f32[32,128]{1,0:T(8,128)S(1)} %broadcast_in_dim.2.refs_3_, bf16[2,576,256]{2,1,0:T(8,128)(2,1)S(1)} %copy-done.4, ...), custom_call_target="tpu_custom_call" | custom-call | flops 660602880 | bytes 14745600 | tf_op jit(solution)/shard_map/outer_sweep_south_0/pallas_call | solution.py:328
  67.8 3.4 %second_source_1.1 = (bf16[10,1152,256]{2,1,0:T(8,128)(2,1)}, f32[10,2,256]{2,1,0:T(2,128)}) custom-call(bf16[6,576,256]{2,1,0:T(8,128)(2,1)S(1)} %get-tuple-element.58.refs_0_, bf16[2,576,256]{2,1,0:T(8,128)(2,1)S(1)} %get-tuple-element.71.refs_1_, f32[2,8,256]{2,1,0:T(8,128)S(1)} %copy-done.11, ...), custom_call_target="tpu_custom_call", output_to_operand_aliasing={{0}: (9, {}), {1}: (10, {})} | custom-call | flops 1358954496 | bytes 2359296 | tf_op jit(solution)/shard_map/second_source_1/pallas_call | solution.py:389
  71.3 2.2 %collective-permute-done.3.refs_7_ = bf16[2,592,256]{2,1,0:T(8,128)(2,1)S(1)} collective-permute-done((bf16[2,592,256]{2,1,0:T(8,128)(2,1)S(1)}, bf16[2,592,256]{2,1,0:T(8,128)(2,1)S(1)}, u32[]{:S(2)}, u32[]{:S(2)}) %collective-permute-start.3) | collective-permute-done | bytes 606240 | tf_op jit(solution)/shard_map/ppermute | solution.py:455
  73.5 2.9 %outer_sweep_south_2.1.refs_1_ = bf16[2,576,256]{2,1,0:T(8,128)(2,1)S(1)} custom-call(f32[2,36]{1,0:T(2,128)S(1)} %copy-done.13, s32[10,256]{1,0:T(8,128)S(1)} %copy-done.6, f32[10,256]{1,0:T(8,128)S(1)} %copy-done.7, f32[32,128]{1,0:T(8,128)S(1)} %broadcast_in_dim.2.refs_3_, bf16[2,576,256]{2,1,0:T(8,128)(2,1)S(1)} %copy-done.4, ...), custom_call_target="tpu_custom_call" | custom-call | flops 660602880 | bytes 14745600 | tf_op jit(solution)/shard_map/outer_sweep_south_2/pallas_call | solution.py:328
  76.4 3.4 %second_source_0.1 = (bf16[10,1152,256]{2,1,0:T(8,128)(2,1)}, f32[10,2,256]{2,1,0:T(2,128)}) custom-call(bf16[6,576,256]{2,1,0:T(8,128)(2,1)S(1)} %get-tuple-element.58.refs_0_, bf16[2,576,256]{2,1,0:T(8,128)(2,1)S(1)} %outer_sweep_south_2.1.refs_1_, f32[2,8,256]{2,1,0:T(8,128)S(1)} %copy-done.10, ...), custom_call_target="tpu_custom_call", output_to_operand_aliasing={{0}: (9, {}), {1}: (10, {})} | custom-call | flops 1358954496 | bytes 2359296 | tf_op jit(solution)/shard_map/second_source_0/pallas_call | solution.py:389
  (26 shorter events, 0.1 us)
Async XLA Ops:
  7.0 44.7 %collective-permute-start = (bf16[2,592,256]{2,1,0:T(8,128)(2,1)}, bf16[2,592,256]{2,1,0:T(8,128)(2,1)}, u32[]{:S(2)}, u32[]{:S(2)}) collective-permute-start(bf16[2,592,256]{2,1,0:T(8,128)(2,1)} %get-tuple-element.43.refs_4_), channel_id=1, source_target_pairs={{1,0},{2,1},{3,2},{4,3},{5,4},{6,5},{7,6},{8,7},{9,8},{10,9},{11,1... | collective-permute-start | bytes 1818632 | tf_op jit(solution)/shard_map/ppermute | solution.py:442
  13.4 9.6 %copy-start = (bf16[1152,1152]{1,0:T(8,128)(2,1)S(1)}, bf16[1152,1152]{1,0:T(8,128)(2,1)}, u32[]{:S(2)}) copy-start(bf16[1152,1152]{1,0:T(8,128)(2,1)} %refs_7_.11) | copy-start | bytes 7962628
  13.4 9.5 %copy-start.1 = (bf16[1152,10,256]{2,0,1:T(8,128)(2,1)S(1)}, bf16[1152,10,256]{2,0,1:T(8,128)(2,1)}, u32[]{:S(2)}) copy-start(bf16[1152,10,256]{2,0,1:T(8,128)(2,1)} %param.14) | copy-start | bytes 17694724
  13.4 9.5 %copy-start.2 = (f32[1152,128]{1,0:T(8,128)S(1)}, f32[1152,128]{1,0:T(8,128)}, u32[]{:S(2)}) copy-start(f32[1152,128]{1,0:T(8,128)} %get-tuple-element.45.refs_9_.refs_6_) | copy-start | bytes 1769476
  13.4 9.5 %copy-start.3 = (bf16[1152,128]{1,0:T(8,128)(2,1)S(1)}, bf16[1152,128]{1,0:T(8,128)(2,1)}, u32[]{:S(2)}) copy-start(bf16[1152,128]{1,0:T(8,128)(2,1)} %get-tuple-element.46.refs_10_.refs_11_.refs_8_) | copy-start | bytes 884740
  13.5 9.5 %copy-start.5 = (f32[1152,128]{1,0:T(8,128)S(1)}, f32[1152,128]{1,0:T(8,128)}, u32[]{:S(2)}) copy-start(f32[1152,128]{1,0:T(8,128)} %get-tuple-element.44.refs_8_) | copy-start | bytes 1769476
  13.5 9.5 %copy-start.6 = (s32[10,256]{1,0:T(8,128)S(1)}, s32[10,256]{1,0:T(8,128)}, u32[]{:S(2)}) copy-start(s32[10,256]{1,0:T(8,128)} %refs_1_.15) | copy-start | bytes 30724
  13.5 9.5 %copy-start.7 = (f32[10,256]{1,0:T(8,128)S(1)}, f32[10,256]{1,0:T(8,128)}, u32[]{:S(2)}) copy-start(f32[10,256]{1,0:T(8,128)} %refs_2_.15) | copy-start | bytes 30724
  13.5 9.5 %copy-start.8 = (s32[10,256]{1,0:T(8,128)S(1)}, s32[10,256]{1,0:T(8,128)}, u32[]{:S(2)}) copy-start(s32[10,256]{1,0:T(8,128)} %refs_3_.9) | copy-start | bytes 30724
  13.5 9.5 %copy-start.9 = (f32[10,256]{1,0:T(8,128)S(1)}, f32[10,256]{1,0:T(8,128)}, u32[]{:S(2)}) copy-start(f32[10,256]{1,0:T(8,128)} %refs_4_.9) | copy-start | bytes 30724
  13.5 9.5 %copy-start.12 = (f32[8]{0:T(128)S(1)}, f32[8]{0:T(128)}, u32[]{:S(2)}) copy-start(f32[8]{0:T(128)} %refs_5_.9) | copy-start | bytes 100
  13.5 9.5 %copy-start.14 = (s32[64]{0:T(128)S(1)}, s32[64]{0:T(128)}, u32[]{:S(2)}) copy-start(s32[64]{0:T(128)} %refs_6_.6) | copy-start | bytes 772
  20.2 12.2 %copy-start.18 = (f32[32]{0:T(128)S(1)}, f32[32]{0:T(128)}, u32[]{:S(2)}) copy-start(f32[32]{0:T(128)} %param.24) | copy-start | bytes 388
  20.2 12.3 %copy-start.4 = (bf16[2,576,256]{2,1,0:T(8,128)(2,1)S(1)}, bf16[2,576,256]{2,1,0:T(8,128)(2,1)}, u32[]{:S(2)}) copy-start(bf16[2,576,256]{2,1,0:T(8,128)(2,1)} %get-tuple-element.49.refs_4_) | copy-start | bytes 1769476
  20.2 12.3 %copy-start.13 = (f32[2,36]{1,0:T(2,128)S(1)}, f32[2,36]{1,0:T(2,128)}, u32[]{:S(2)}) copy-start(f32[2,36]{1,0:T(2,128)} %constant.5.clone.refs_0_) | copy-start | bytes 868
  20.3 12.3 %copy-start.17 = (bf16[2,576,256]{2,1,0:T(8,128)(2,1)S(1)}, bf16[2,576,256]{2,1,0:T(8,128)(2,1)}, u32[]{:S(2)}) copy-start(bf16[2,576,256]{2,1,0:T(8,128)(2,1)} %get-tuple-element.50.refs_5_) | copy-start | bytes 1769476
  20.3 31.5 %collective-permute-start.1 = (bf16[2,592,256]{2,1,0:T(8,128)(2,1)}, bf16[2,592,256]{2,1,0:T(8,128)(2,1)S(1)}, u32[]{:S(2)}, u32[]{:S(2)}) collective-permute-start(bf16[2,592,256]{2,1,0:T(8,128)(2,1)} %get-tuple-element.47.refs_5_), channel_id=1, source_target_pairs={{1,0},{2,1},{3,2},{4,3},{5,4},{6,5},{7,6},{8,7},{9,8},{10,9},{11,1... | collective-permute-start | bytes 1818632 | tf_op jit(solution)/shard_map/ppermute | solution.py:445
  32.5 10.2 %copy-start.15 = (bf16[2,592,256]{2,1,0:T(8,128)(2,1)S(1)}, bf16[2,592,256]{2,1,0:T(8,128)(2,1)}, u32[]{:S(2)}) copy-start(bf16[2,592,256]{2,1,0:T(8,128)(2,1)} %get-tuple-element.43.refs_4_) | copy-start | bytes 1818628
  32.6 10.2 %copy-start.16 = (bf16[2,592,256]{2,1,0:T(8,128)(2,1)S(1)}, bf16[2,592,256]{2,1,0:T(8,128)(2,1)}, u32[]{:S(2)}) copy-start(bf16[2,592,256]{2,1,0:T(8,128)(2,1)} %get-tuple-element.47.refs_5_) | copy-start | bytes 1818628
  39.3 25.6 %collective-permute-start.2 = (bf16[2,592,256]{2,1,0:T(8,128)(2,1)S(1)}, bf16[2,592,256]{2,1,0:T(8,128)(2,1)S(1)}, u32[]{:S(2)}, u32[]{:S(2)}) collective-permute-start(bf16[2,592,256]{2,1,0:T(8,128)(2,1)S(1)} %get-tuple-element.69.refs_8_), channel_id=1, source_target_pairs={{0,1},{1,2},{2,3},{3,4},{4,5},{5,6},{6,7},{7,8},{8,9},{9,10},{10,1... | collective-permute-start | bytes 1818632 | tf_op jit(solution)/shard_map/ppermute | solution.py:452
  49.6 23.9 %collective-permute-start.3 = (bf16[2,592,256]{2,1,0:T(8,128)(2,1)S(1)}, bf16[2,592,256]{2,1,0:T(8,128)(2,1)S(1)}, u32[]{:S(2)}, u32[]{:S(2)}) collective-permute-start(bf16[2,592,256]{2,1,0:T(8,128)(2,1)S(1)} %get-tuple-element.78.refs_7_), channel_id=1, source_target_pairs={{0,1},{1,2},{2,3},{3,4},{4,5},{5,6},{6,7},{7,8},{8,9},{9,10},{10,1... | collective-permute-start | bytes 1818632 | tf_op jit(solution)/shard_map/ppermute | solution.py:455
  64.9 3.0 %copy-start.11 = (f32[2,8,256]{2,1,0:T(8,128)S(1)}, f32[2,8,256]{2,1,0:T(8,128)}, u32[]{:S(2)}) copy-start(f32[2,8,256]{2,1,0:T(8,128)} %get-tuple-element.72.refs_2_) | copy-start | bytes 49156
  71.3 5.1 %copy-start.10 = (f32[2,8,256]{2,1,0:T(8,128)S(1)}, f32[2,8,256]{2,1,0:T(8,128)}, u32[]{:S(2)}) copy-start(f32[2,8,256]{2,1,0:T(8,128)} %get-tuple-element.79.refs_2_) | copy-start | bytes 49156
